TPU v7x, 512 devices: a whole 4x4x16 slice. The times are simulated.
512 devices in a mesh: tok: 16 (over x, z_hi), feat: 32 (over y, z_lo, core).
Axes of the slice: x: 4, y: 4, z: 16 (z_hi: 4, z_lo: 4; z = z_hi * 4 + z_lo), core: 2. Of those that a mesh axis runs over, the one named last changes fastest.
Arguments:
- layer_inputs: bfloat16 [2048, 4096], P('tok', 'feat'), may hold values from -6 to 6
- output_grads: bfloat16 [2048, 8192], P('tok', 'feat'), may hold values from -6 to 6
- input_factor: float32 [4096, 4096], P('tok', 'feat'), may hold values from -1 to 4, as said below
- output_factor: float32 [8192, 8192], P('tok', 'feat'), may hold values from -1 to 4, as said below
- input_inverse: bfloat16 [4096, 4096], P('tok', 'feat'), may hold values from -2 to 16, as said below
- output_inverse: bfloat16 [8192, 8192], P('tok', 'feat'), may hold values from -2 to 16, as said below
Outputs:
- input_running: float32 [4096, 4096], P('tok', 'feat')
- output_running: float32 [8192, 8192], P('tok', 'feat')
- natural_gradient: float32 [4096, 8192], P('tok', 'feat')
Inputs may be any that keep to these rules, and one draw needn't show every extreme that they name: input_factor equals its transpose. output_factor equals its transpose. input_inverse equals its transpose. output_inverse equals its transpose.
All inputs are finite; a program needn't handle non-finite values.
Results may differ from a plain program's by a relative error of at most 0.0041.
Values may be sent and summed in bfloat16 or wider, within the bound.
No kernel may reach another device: no remote copies, remote signals or barrier semaphores. Data moves between devices by JAX's collectives and lax.ppermute only.
A program may use at most 64 MiB of HBM per device.

v0:
```python
import jax
import jax.numpy as jnp
from jax import lax
from jax.sharding import PartitionSpec as P

stat_decay = 0.9
by_rows = (((0,), (0,)), ((), ()))


def from_root(block, axis, source):
    block = jnp.where(lax.axis_index(axis) == source, block, jnp.zeros_like(block))
    return lax.psum(block, axis)


def per_device(
    layer_inputs, output_grads, input_factor, output_factor, input_inverse, output_inverse
):
    tokens = layer_inputs.shape[0] * lax.axis_size("tok")
    owner_count = lax.axis_size("feat") // lax.axis_size("tok")
    first_root = lax.axis_index("tok") * owner_count
    input_rows, output_rows = (
        lax.all_gather(layer_inputs, "feat", axis=1, tiled=True),
        lax.all_gather(output_grads, "feat", axis=1, tiled=True),
    )
    stretch = output_inverse.shape[0] // input_inverse.shape[0]
    output_width = output_inverse.shape[1]
    folded = output_inverse.reshape(input_inverse.shape[0], stretch, output_width)
    pieces = (
        lax.all_gather(input_inverse, "tok", axis=0, tiled=True),
        lax.all_gather(folded, "tok", axis=0, tiled=True),
    )
    row_count = pieces[0].shape[0]
    output_piece = pieces[1].reshape(row_count * stretch, output_width)
    input_mixed = jnp.dot(input_rows, pieces[0], preferred_element_type=jnp.float32)
    output_mixed = jnp.dot(output_rows, output_piece, preferred_element_type=jnp.float32)
    input_mixed = input_mixed.astype(jnp.bfloat16)
    output_mixed = output_mixed.astype(jnp.bfloat16)
    input_cols, output_cols, mixed_cols, grads_mixed = (
        lax.all_gather(layer_inputs, "tok", axis=0, tiled=True),
        lax.all_gather(output_grads, "tok", axis=0, tiled=True),
        lax.all_gather(input_mixed, "tok", axis=0, tiled=True),
        lax.all_gather(output_mixed, "tok", axis=0, tiled=True),
    )
    received = [
        (
            from_root(input_cols, "feat", first_root + offset),
            from_root(output_cols, "feat", first_root + offset),
            from_root(mixed_cols, "feat", first_root + offset),
        )
        for offset in range(owner_count)
    ]
    input_owned = jnp.concatenate([entry[0] for entry in received], axis=1)
    output_owned = jnp.concatenate([entry[1] for entry in received], axis=1)
    mixed_owned = jnp.concatenate([entry[2] for entry in received], axis=1)
    input_batch = (
        lax.dot_general(input_owned, input_cols, by_rows, preferred_element_type=jnp.float32)
        / tokens
    )
    output_batch = (
        lax.dot_general(output_owned, output_cols, by_rows, preferred_element_type=jnp.float32)
        / tokens
    )
    natural_gradient = (
        lax.dot_general(mixed_owned, grads_mixed, by_rows, preferred_element_type=jnp.float32)
        / tokens
    )
    input_running = stat_decay * input_factor + (1.0 - stat_decay) * input_batch
    output_running = stat_decay * output_factor + (1.0 - stat_decay) * output_batch
    return (input_running, output_running, natural_gradient)


def solution(mesh):
    in_specs = (
        P("tok", "feat"),
        P("tok", "feat"),
        P("tok", "feat"),
        P("tok", "feat"),
        P("tok", "feat"),
        P("tok", "feat"),
    )
    out_specs = (P("tok", "feat"), P("tok", "feat"), P("tok", "feat"))
    return jax.shard_map(
        per_device, mesh=mesh, in_specs=in_specs, out_specs=out_specs, check_vma=False
    )
```

profile of v0, /device:TPU:1, one launch (start us, length us, event | category | flops | bytes accessed | tf_op | source)
XLA Modules:
  0.0 840.9 jit_solution(11651380975492974479)
XLA Ops:
  7.2 0.7 all-gather.7.cloned.1.call-update
  7.9 0.7 all-gather.11.cloned.1.call-update
  8.7 0.7 all-gather.9.cloned.1.call-update
  9.4 1.8 reshape.12
  11.3 0.5 all-gather.13.cloned.1.call-update
  11.9 60.2 %all_gather.24 = bf16[2048,128]{1,0:T(8,128)(2,1)S(1)} all-gather(bf16[128,128]{1,0:T(8,128)(2,1)} %param.6), channel_id=1, replica_groups=mesh['tok'=16,'feat'=32] {'tok'}, dimensions={0}, use_global_device_ids=true | all-gather | bytes 557056 | tf_op jit(solution)/shard_map/all_gather | solution.py:39
  72.1 1.1 broadcast_select_fusion.5
  73.1 24.9 %all-gather.7.cloned.1.call-done = bf16[2048,256]{1,0:T(8,128)(2,1)} async-done(((bf16[128,256]{1,0:T(8,128)(2,1)}), bf16[2048,256]{1,0:T(8,128)(2,1)}) %all-gather.7.cloned.1.call-update) | async-done | bytes 1048592 | tf_op jit(solution)/shard_map/all_gather | solution.py:40
  98.0 2.8 broadcast_select_fusion.1
  100.8 71.7 %all-gather.11.cloned.1.call-done = bf16[4096,128]{1,0:T(8,128)(2,1)} async-done(((bf16[256,128]{1,0:T(8,128)(2,1)}), bf16[4096,128]{1,0:T(8,128)(2,1)}) %all-gather.11.cloned.1.call-update) | async-done | bytes 1048592 | tf_op jit(solution)/shard_map/all_gather | solution.py:29
  172.4 62.9 %all-gather.9.cloned.1.call-done = bf16[128,4096]{1,0:T(8,128)(2,1)} async-done(((bf16[128,128]{1,0:T(8,128)(2,1)}), bf16[128,4096]{1,0:T(8,128)(2,1)}) %all-gather.9.cloned.1.call-update) | async-done | bytes 1048592 | tf_op jit(solution)/shard_map/all_gather | solution.py:22
  235.3 2.0 convolution_convert_fusion.1
  237.3 63.5 %all_gather.28 = bf16[2048,128]{1,0:T(8,128)(2,1)S(1)} all-gather(bf16[128,128]{1,0:T(8,128)(2,1)S(1)} %convolution_convert_fusion.1), channel_id=1, replica_groups=mesh['tok'=16,'feat'=32] {'tok'}, dimensions={0}, use_global_device_ids=true | all-gather | bytes 557056 | tf_op jit(solution)/shard_map/all_gather | solution.py:41
  300.8 1.1 broadcast_select_fusion.4
  301.9 0.0 all-gather.17.cloned.1.call-start
  302.0 78.0 %all-gather.15.cloned.1.call-done = bf16[4096,2,256]{2,1,0:T(2,128)(2,1)} async-done(((bf16[256,2,256]{2,1,0:T(2,128)(2,1)}), bf16[4096,2,256]{2,1,0:T(2,128)(2,1)}) %all-gather.15.cloned.1.call-update) | async-done | bytes 4194320 | tf_op jit(solution)/shard_map/all_gather | solution.py:30
  380.0 7.3 reshape.13
  387.2 59.2 %all-gather.13.cloned.1.call-done = bf16[128,8192]{1,0:T(8,128)(2,1)} async-done(((bf16[128,256]{1,0:T(8,128)(2,1)}), bf16[128,8192]{1,0:T(8,128)(2,1)}) %all-gather.13.cloned.1.call-update) | async-done | bytes 2097168 | tf_op jit(solution)/shard_map/all_gather | solution.py:23
  446.4 4.2 convolution_convert_fusion
  450.6 301.9 %all-reduce.3.cloned.1.call-done = (bf16[2048,128]{1,0:T(8,128)(2,1)}, bf16[2048,128]{1,0:T(8,128)(2,1)}, bf16[2048,256]{1,0:T(8,128)(2,1)}, bf16[2048,256]{1,0:...) async-done(((bf16[2048,128]{1,0:T(8,128)(2,1)}, bf16[2048,128]{1,0:T(8,128)(2,1)}, bf16[2048,256]{1,0:T(8,128)(2,1)}, bf16[2048,256]{1,0:T(8,128)(2,1)}, ...) | async-done | bytes 4194320 | tf_op jit(solution)/shard_map/psum | solution.py:12
  752.5 2.4 fusion.10
  754.9 2.9 fusion.7
  757.8 73.9 %all-gather.17.cloned.1.call-done = bf16[2048,256]{1,0:T(8,128)(2,1)} async-done(((bf16[128,256]{1,0:T(8,128)(2,1)}), bf16[2048,256]{1,0:T(8,128)(2,1)}) %all-gather.17.cloned.1.call-update) | async-done | bytes 1048592 | tf_op jit(solution)/shard_map/all_gather | solution.py:42
  831.7 2.4 convolution_multiply_fusion
  (21 shorter events, 0.3 us)
Async XLA Ops:
  7.2 90.8 %all-gather.7.cloned.1.call-start = ((), (), s32[]{:S(2)}) async-start(), calls=%async_computation | async-start | bytes 1114112 | tf_op jit(solution)/shard_map/all_gather | solution.py:40
  7.9 164.5 %all-gather.11.cloned.1.call-start = ((), (), s32[]{:S(2)}) async-start(), calls=%async_computation.2 | async-start | bytes 1114112 | tf_op jit(solution)/shard_map/all_gather | solution.py:29
  8.6 226.7 %all-gather.9.cloned.1.call-start = ((), (), s32[]{:S(2)}) async-start(), calls=%async_computation.1 | async-start | bytes 1081344 | tf_op jit(solution)/shard_map/all_gather | solution.py:22
  9.4 370.6 %all-gather.15.cloned.1.call-start = ((), (), s32[]{:S(2)}) async-start(), calls=%async_computation.4 | async-start | bytes 4456448 | tf_op jit(solution)/shard_map/all_gather | solution.py:30
  11.2 435.2 %all-gather.13.cloned.1.call-start = ((), (), s32[]{:S(2)}) async-start(), calls=%async_computation.3 | async-start | bytes 2162688 | tf_op jit(solution)/shard_map/all_gather | solution.py:23
  11.8 740.7 %all-reduce.3.cloned.1.call-start = ((), (), s32[]{:S(2)}) async-start(), calls=%async_computation.6 | async-start | bytes 8388608 | tf_op jit(solution)/shard_map/psum | solution.py:12
  301.9 529.8 %all-gather.17.cloned.1.call-start = ((), (), s32[]{:S(2)}) async-start(), calls=%async_computation.5 | async-start | bytes 1114112 | tf_op jit(solution)/shard_map/all_gather | solution.py:42
  387.2 365.2 %copy-start.5 = (f32[256,128]{1,0:T(8,128)S(1)}, f32[256,128]{1,0:T(8,128)}, u32[]{:S(2)}) copy-start(f32[256,128]{1,0:T(8,128)} %param.8) | copy-start | bytes 393220
  450.6 304.3 %copy-start = (bf16[2048,256]{1,0:T(8,128)(2,1)S(1)}, bf16[2048,256]{1,0:T(8,128)(2,1)}, u32[]{:S(2)}) copy-start(bf16[2048,256]{1,0:T(8,128)(2,1)} %all-gather.7.cloned.1.call-done) | copy-start | bytes 3145732
  450.6 304.3 %copy-start.2 = (f32[512,256]{1,0:T(8,128)S(1)}, f32[512,256]{1,0:T(8,128)}, u32[]{:S(2)}) copy-start(f32[512,256]{1,0:T(8,128)} %param.9) | copy-start | bytes 1572868
  752.5 2.4 copy-start.1
  754.9 76.8 %copy-start.3 = (bf16[2048,128]{1,0:T(8,128)(2,1)S(1)}, bf16[2048,128]{1,0:T(8,128)(2,1)}, u32[]{:S(2)}) copy-start(bf16[2048,128]{1,0:T(8,128)(2,1)} %get-tuple-element.7) | copy-start | bytes 1572868
  754.9 76.8 %copy-start.4 = (bf16[2048,128]{1,0:T(8,128)(2,1)S(1)}, bf16[2048,128]{1,0:T(8,128)(2,1)}, u32[]{:S(2)}) copy-start(bf16[2048,128]{1,0:T(8,128)(2,1)} %get-tuple-element.8) | copy-start | bytes 1572868
Sparse Core Ops, SparseCore 0:
  11.0 86.9 all-gather.6
  101.0 71.4 all-gather.10
  174.5 60.7 all-gather.8
  238.8 141.1 all-gather.14
  381.9 64.4 all-gather.12
  450.2 302.2 all-reduce.2
  756.0 75.5 all-gather.16
where the time goes:
time: 841 us
  waiting for transfers between devices  675 us (80%)
  blocking collectives  124 us (15%)
  between operations  14.2 us (2%)
  matrix products  13.8 us (2%)
  local copies, waits for them, and re-layouts  9.03 us (1%)
    psum x1, waiting for transfers between devices, from_root(): return lax.psum(block, axis)  302 us
    all_gather x1, waiting for transfers between devices, per_device(): lax.all_gather(folded, 'tok', axis=0, tiled=True)  78 us
    all_gather x1, waiting for transfers between devices, per_device(): lax.all_gather(output_mixed, 'tok', axis=0, tiled=True)  73.9 us
    all_gather x1, waiting for transfers between devices, per_device(): lax.all_gather(input_inverse, 'tok', axis=0, tiled=True)  71.7 us
    all_gather x1, blocking collectives, per_device(): lax.all_gather(input_mixed, 'tok', axis=0, tiled=True)  63.5 us
    all_gather x1, waiting for transfers between devices, per_device(): lax.all_gather(layer_inputs, 'feat', axis=1, tiled=True)  62.9 us
    all_gather x1, blocking collectives, per_device(): lax.all_gather(layer_inputs, 'tok', axis=0, tiled=True)  60.2 us
    all_gather x1, waiting for transfers between devices, per_device(): lax.all_gather(output_grads, 'feat', axis=1, tiled=True)  59.2 us
  transfers between devices with their start and end apart: 7, of which 7 were waited for; matrix products, arithmetic and copies ran while one was open for 3% of the time, Pallas kernels for 0%

commit v1 on v0

v1 whole, which is shorter than its diff:
```python
import jax
import jax.numpy as jnp
from jax import lax
from jax.sharding import Mesh, PartitionSpec as P

stat_decay = 0.9
by_rows = (((0,), (0,)), ((), ()))
by_cols = (((1,), (1,)), ((), ()))
TOK = ("x", "zh")
FEAT = ("y", "zl", "core")
SIDE = 4
CORES = 2


def swap_pairs():
    blocks = SIDE * SIDE
    pairs = []
    for a in range(blocks):
        for b in range(blocks):
            for c in range(CORES):
                pairs.append(((a * blocks + b) * CORES + c, (b * blocks + a) * CORES + c))
    return pairs


def gather(block, axis):
    return lax.all_gather(block, axis, axis=0, tiled=True)


def scatter_sum(partial, axis, wire):
    parts = partial.reshape(SIDE, partial.shape[0] // SIDE, partial.shape[1]).astype(wire)
    parts = lax.all_to_all(parts, axis, 0, 0)
    return jnp.sum(parts.astype(jnp.float32), axis=0)


def dot(left, right, dims):
    return lax.dot_general(left, right, dims, preferred_element_type=jnp.float32)


def per_device(
    layer_inputs, output_grads, input_factor, output_factor, input_inverse, output_inverse
):
    tokens = layer_inputs.shape[0] * SIDE * SIDE
    width = layer_inputs.shape[1]
    both = jnp.concatenate([layer_inputs, output_grads], axis=1)

    swapped = lax.ppermute(both, TOK + FEAT, swap_pairs())
    cols = gather(gather(both, "zh"), "x")
    rows = gather(gather(swapped, "zl"), "y")
    rows = lax.all_gather(rows, "core", axis=0, tiled=False)

    input_cols, output_cols = cols[:, :width], cols[:, width:]
    input_rows = jnp.concatenate([rows[0, :, :width], rows[1, :, :width]], axis=1)
    output_rows = jnp.concatenate([rows[0, :, width:], rows[1, :, width:]], axis=1)

    grads_part = dot(output_rows, output_inverse, (((1,), (0,)), ((), ())))
    grads_mixed = scatter_sum(scatter_sum(grads_part, "x", jnp.bfloat16), "zh", jnp.bfloat16)
    grads_mixed = gather(gather(grads_mixed.astype(jnp.bfloat16), "zh"), "x")

    halves = input_cols.reshape(CORES, tokens // CORES, width)
    halves = lax.all_to_all(halves, "core", 0, 0)
    inverse = lax.all_gather(input_inverse, "core", axis=0, tiled=False)
    input_part = dot(halves[0], inverse[0], by_cols) + dot(halves[1], inverse[1], by_cols)
    input_mixed = scatter_sum(scatter_sum(input_part, "y", jnp.float32), "zl", jnp.float32)
    input_mixed = gather(gather(input_mixed.astype(jnp.bfloat16), "zl"), "y")
    input_mixed = gather(input_mixed, "core")

    input_batch = dot(input_rows, input_cols, by_rows) / tokens
    output_batch = dot(output_rows, output_cols, by_rows) / tokens
    natural_gradient = dot(input_mixed, grads_mixed, by_rows) / tokens
    input_running = stat_decay * input_factor + (1.0 - stat_decay) * input_batch
    output_running = stat_decay * output_factor + (1.0 - stat_decay) * output_batch
    return (input_running, output_running, natural_gradient)


def solution(mesh):
    grid = Mesh(mesh.devices.reshape(SIDE, SIDE, SIDE, SIDE, CORES), TOK + FEAT)
    spec = P(TOK, FEAT)
    return jax.shard_map(
        per_device, mesh=grid, in_specs=(spec,) * 6, out_specs=(spec,) * 3, check_vma=False
    )
```

time: 841 us -> 272 us (0.32)
  waiting for transfers between devices: 675 us -> 90.3 us
  blocking collectives: 124 us -> 143 us
  starting transfers between devices: 0.27 us -> 8.91 us
    psum x1 -> x0, waiting for transfers between devices: 302 us -> none  [from_root(): return lax.psum(block, axis)]
    all_gather x6 -> x5, waiting for transfers between devices: 370 us -> 88.9 us  [the longest x4 88.9 us: gather(): return lax.all_gather(block, axis, axis=0, tiled=True)]
    all_to_all x0 -> x3, blocking collectives: none -> 48.1 us  [the longest x2 43.6 us: scatter_sum(): parts = lax.all_to_all(parts, axis, 0, 0)]
    all_gather x2 -> x6, blocking collectives: 124 us -> 94.7 us  [the longest x5 92.5 us: gather(): return lax.all_gather(block, axis, axis=0, tiled=True)]
    reshape x2 -> x0, local copies, waits for them, and re-layouts: 9 us -> none  [the longest x1 7.25 us: per_device(): output_piece = pieces[1].reshape(row_count * stretch, output_width)]
  transfers between devices with their start and end apart: 7 -> 8, of which waited for: 7 -> 4; matrix products, arithmetic and copies ran while one was open for 3% -> 4% of each run, Pallas kernels for 0% -> 0%
where the time goes in v1:
time: 272 us
  blocking collectives  143 us (53%)
  waiting for transfers between devices  90.3 us (33%)
  between operations  13.9 us (5%)
  starting transfers between devices  8.91 us (3%)
  matrix products  7.68 us (3%)
  local copies, waits for them, and re-layouts  6.79 us (2%)
    all_gather x5, blocking collectives, gather(): return lax.all_gather(block, axis, axis=0, tiled=True)  92.5 us
    all_gather x4, waiting for transfers between devices, gather(): return lax.all_gather(block, axis, axis=0, tiled=True)  88.9 us
    all_to_all x2, blocking collectives, scatter_sum(): parts = lax.all_to_all(parts, axis, 0, 0)  43.6 us
    all_to_all x2, starting transfers between devices, scatter_sum(): parts = lax.all_to_all(parts, axis, 0, 0)  8.05 us
    dot_general x6, matrix products, dot(): lax.dot_general(left, right, dims, preferred_element_type=jnp.float32)  7.68 us
  transfers between devices with their start and end apart: 8, of which 4 were waited for; matrix products, arithmetic and copies ran while one was open for 4% of the time, Pallas kernels for 0%

profile of v1, /device:TPU:1, one launch (start us, length us, event | category | flops | bytes accessed | tf_op | source)
XLA Modules:
  0.0 271.5 jit_solution(7765106196672017941)
XLA Ops:
  8.0 0.8 constant_dynamic-update-slice_fusion
  9.6 30.9 %all_gather.39 = bf16[512,384]{1,0:T(8,128)(2,1)} all-gather(bf16[128,384]{1,0:T(8,128)(2,1)S(1)} %collective-permute-done), channel_id=1, replica_groups=mesh['x'=4,'zh'=4,'y'=4,'zl'=4,'core'=2] {'zl'}, dimensions={0}, use_global_device_ids=true | all-gather | bytes 491520 | tf_op jit(solution)/shard_map/all_gather | solution.py:26
  40.5 24.1 %all_gather.43 = bf16[512,384]{1,0:T(8,128)(2,1)} all-gather(bf16[128,384]{1,0:T(8,128)(2,1)S(1)} %constant_dynamic-update-slice_fusion), channel_id=1, replica_groups=mesh['x'=4,'zh'=4,'y'=4,'zl'=4,'core'=2] {'zh'}, dimensions={0}, use_global_device_ids=true | all-gather | bytes 491520 | tf_op jit(solution)/shard_map/all_gather | solution.py:26
  64.7 17.7 %all-gather.8.cloned.1.call-done = bf16[2048,384]{1,0:T(8,128)(2,1)} async-done(((bf16[512,384]{1,0:T(8,128)(2,1)}), bf16[2048,384]{1,0:T(8,128)(2,1)}) %all-gather.8.cloned.1.call-update) | async-done | bytes 1572880 | tf_op jit(solution)/shard_map/all_gather | solution.py:26
  82.4 2.2 all-gather.1
  84.6 34.2 %all-gather.10.cloned.1.call-done = bf16[2048,384]{1,0:T(8,128)(2,1)} async-done(((bf16[512,384]{1,0:T(8,128)(2,1)}), bf16[2048,384]{1,0:T(8,128)(2,1)}) %all-gather.10.cloned.1.call-update) | async-done | bytes 1572880 | tf_op jit(solution)/shard_map/all_gather | solution.py:26
  118.8 1.1 slice.44
  119.9 4.5 %all_to_all.25 = bf16[2,1024,128]{2,1,0:T(8,128)(2,1)S(1)} all-to-all(bf16[2,1024,128]{2,1,0:T(8,128)(2,1)S(1)} %bitcast.26), channel_id=1, replica_groups=mesh['x'=4,'zh'=4,'y'=4,'zl'=4,'core'=2] {'core'}, dimensions={0} | all-to-all | bytes 1048576 | tf_op jit(solution)/shard_map/all_to_all | solution.py:60
  124.9 18.0 %all_to_all.26 = f32[4,256,256]{2,1,0:T(8,128)S(1)} all-to-all(f32[4,256,256]{2,1,0:T(8,128)S(1)} %bitcast.23), channel_id=1, replica_groups=mesh['x'=4,'zh'=4,'y'=4,'zl'=4,'core'=2] {'y'}, dimensions={0} | all-to-all | bytes 2097152 | tf_op jit(solution)/shard_map/all_to_all | solution.py:31
  143.7 4.5 %all-to-all-start.2 = ((f32[4,64,256]{2,1,0:T(8,128)}), f32[4,64,256]{2,1,0:T(8,128)S(1)}, u32[]{:S(2)}, u32[]{:S(2)}) async-start(f32[4,64,256]{2,1,0:T(8,128)} %bitcast.9), calls=%async_computation.2 | async-start | bytes 524288 | tf_op jit(solution)/shard_map/all_to_all | solution.py:31
  148.3 1.7 slice_bitcast_fusion.1
  150.0 1.0 copy-done.1
  150.9 1.7 convolution_convert_fusion
  152.6 1.3 all-to-all-done.2
  153.9 3.5 %all-to-all-start.3 = ((bf16[4,512,256]{2,1,0:T(8,128)(2,1)}), bf16[4,512,256]{2,1,0:T(8,128)(2,1)S(1)}, u32[]{:S(2)}, u32[]{:S(2)}) async-start(bf16[4,512,256]{2,1,0:T(8,128)(2,1)} %bitcast.10), calls=%async_computation.3 | async-start | bytes 2097152 | tf_op jit(solution)/shard_map/all_to_all | solution.py:31
  157.5 10.6 %all_gather.47 = bf16[256,256]{1,0:T(8,128)(2,1)S(1)} all-gather(bf16[64,256]{1,0:T(8,128)(2,1)S(1)} %reduce_sum.43), channel_id=1, replica_groups=mesh['x'=4,'zh'=4,'y'=4,'zl'=4,'core'=2] {'zl'}, dimensions={0}, use_global_device_ids=true | all-gather | bytes 163840 | tf_op jit(solution)/shard_map/all_gather | solution.py:26
  168.2 10.8 %all_gather.48 = bf16[1024,256]{1,0:T(8,128)(2,1)} all-gather(bf16[256,256]{1,0:T(8,128)(2,1)S(1)} %all_gather.47), channel_id=1, replica_groups=mesh['x'=4,'zh'=4,'y'=4,'zl'=4,'core'=2] {'y'}, dimensions={0}, use_global_device_ids=true | all-gather | bytes 655360 | tf_op jit(solution)/shard_map/all_gather | solution.py:26
  179.4 25.6 %all_to_all.27 = bf16[4,128,256]{2,1,0:T(8,128)(2,1)S(1)} all-to-all(bf16[4,128,256]{2,1,0:T(8,128)(2,1)S(1)} %bitcast.27), channel_id=1, replica_groups=mesh['x'=4,'zh'=4,'y'=4,'zl'=4,'core'=2] {'zh'}, dimensions={0} | all-to-all | bytes 524288 | tf_op jit(solution)/shard_map/all_to_all | solution.py:31
  205.0 16.1 %all_gather.50 = bf16[512,256]{1,0:T(8,128)(2,1)} all-gather(bf16[128,256]{1,0:T(8,128)(2,1)S(1)} %reduce_sum.45), channel_id=1, replica_groups=mesh['x'=4,'zh'=4,'y'=4,'zl'=4,'core'=2] {'zh'}, dimensions={0}, use_global_device_ids=true | all-gather | bytes 327680 | tf_op jit(solution)/shard_map/all_gather | solution.py:26
  221.2 1.4 slice_bitcast_fusion.3
  222.6 1.1 fusion.3
  223.7 1.5 fusion.2
  225.3 37.0 %all-gather.14.cloned.1.call-done = bf16[2048,256]{1,0:T(8,128)(2,1)} async-done(((bf16[512,256]{1,0:T(8,128)(2,1)}), bf16[2048,256]{1,0:T(8,128)(2,1)}) %all-gather.14.cloned.1.call-update) | async-done | bytes 1048592 | tf_op jit(solution)/shard_map/all_gather | solution.py:26
  262.3 2.7 %convolution_multiply_fusion = f32[256,256]{1,0:T(8,128)} fusion(bf16[2048,256]{1,0:T(8,128)(2,1)} %all-gather.12.cloned.1.call-done, bf16[2048,256]{1,0:T(8,128)(2,1)} %all-gather.14.cloned.1.call-done), kind=kOutput, calls=%fused_computation.6 | convolution fusion | flops 268500992 | bytes 2359296 | tf_op jit(solution)/shard_map/dot_general | solution.py:36
  (35 shorter events, 3.5 us)
Async XLA Ops:
  7.2 143.8 %copy-start = (bf16[512,256]{1,0:T(8,128)(2,1)S(1)}, bf16[512,256]{1,0:T(8,128)(2,1)}, u32[]{:S(2)}) copy-start(bf16[512,256]{1,0:T(8,128)(2,1)} %param.11) | copy-start | bytes 786436
  7.2 75.2 %copy-start.4 = (bf16[256,128]{1,0:T(8,128)(2,1)S(1)}, bf16[256,128]{1,0:T(8,128)(2,1)}, u32[]{:S(2)}) copy-start(bf16[256,128]{1,0:T(8,128)(2,1)} %param.10) | copy-start | bytes 196612
  7.2 75.2 %all-gather.8.cloned.1.call-start = ((), (), s32[]{:S(2)}) async-start(), calls=%async_computation.5 | async-start | bytes 1966080 | tf_op jit(solution)/shard_map/all_gather | solution.py:26
  8.9 0.7 collective-permute-start
  40.5 78.3 %all-gather.10.cloned.1.call-start = ((), (), s32[]{:S(2)}) async-start(), calls=%async_computation.6 | async-start | bytes 1966080 | tf_op jit(solution)/shard_map/all_gather | solution.py:26
  64.6 83.7 %all-gather.16.cloned.1.call-start = ((), (), s32[]{:S(2)}) async-start(), calls=%async_computation.9 | async-start | bytes 4718592 | tf_op jit(solution)/shard_map/all_gather | solution.py:49
  143.7 10.2 %all-to-all-start.2 = ((f32[4,64,256]{2,1,0:T(8,128)}), f32[4,64,256]{2,1,0:T(8,128)S(1)}, u32[]{:S(2)}, u32[]{:S(2)}) async-start(f32[4,64,256]{2,1,0:T(8,128)} %bitcast.9), calls=%async_computation.2 | async-start | bytes 524288 | tf_op jit(solution)/shard_map/all_to_all | solution.py:31
  150.0 1.0 copy-start.1
  153.9 25.1 %all-to-all-start.3 = ((bf16[4,512,256]{2,1,0:T(8,128)(2,1)}), bf16[4,512,256]{2,1,0:T(8,128)(2,1)S(1)}, u32[]{:S(2)}, u32[]{:S(2)}) async-start(bf16[4,512,256]{2,1,0:T(8,128)(2,1)} %bitcast.10), calls=%async_computation.3 | async-start | bytes 2097152 | tf_op jit(solution)/shard_map/all_to_all | solution.py:31
  157.5 67.8 %all-gather.12.cloned.1.call-start = ((), (), s32[]{:S(2)}) async-start(), calls=%async_computation.7 | async-start | bytes 1572864 | tf_op jit(solution)/shard_map/all_gather | solution.py:26
  179.0 83.2 %all-gather.14.cloned.1.call-start = ((), (), s32[]{:S(2)}) async-start(), calls=%async_computation.8 | async-start | bytes 1310720 | tf_op jit(solution)/shard_map/all_gather | solution.py:26
  179.4 43.2 %copy-start.6 = (f32[256,128]{1,0:T(8,128)S(1)}, f32[256,128]{1,0:T(8,128)}, u32[]{:S(2)}) copy-start(f32[256,128]{1,0:T(8,128)} %param.8) | copy-start | bytes 393220
  205.0 17.6 %copy-start.3 = (bf16[2048,384]{1,0:T(8,128)(2,1)S(1)}, bf16[2048,384]{1,0:T(8,128)(2,1)}, u32[]{:S(2)}) copy-start(bf16[2048,384]{1,0:T(8,128)(2,1)} %all-gather.10.cloned.1.call-done) | copy-start | bytes 4718596
  221.1 2.6 copy-start.2
  221.2 2.6 copy-start.5
Sparse Core Ops, SparseCore 0:
  40.6 41.6 all-gather.7
  84.4 34.2 all-gather.9
  120.9 24.1 all-gather.15
  179.2 29.1 all-gather.11
  221.3 40.9 all-gather.13

commit v2 on v1

--- a/solution.py
+++ b/solution.py
@@ -36,25 +36,39 @@
     return lax.dot_general(left, right, dims, preferred_element_type=jnp.float32)
 
 
+def gather_direct(block, axis):
+    count = lax.axis_size(axis)
+    copies = jnp.broadcast_to(block[None], (count,) + block.shape)
+    return lax.all_to_all(copies, axis, 0, 0).reshape(count * block.shape[0], block.shape[1])
+
+
 def per_device(
     layer_inputs, output_grads, input_factor, output_factor, input_inverse, output_inverse
 ):
     tokens = layer_inputs.shape[0] * SIDE * SIDE
     width = layer_inputs.shape[1]
+    grads_width = output_grads.shape[1]
+    core = lax.axis_index("core")
     both = jnp.concatenate([layer_inputs, output_grads], axis=1)
 
     swapped = lax.ppermute(both, TOK + FEAT, swap_pairs())
-    cols = gather(gather(both, "zh"), "x")
-    rows = gather(gather(swapped, "zl"), "y")
-    rows = lax.all_gather(rows, "core", axis=0, tiled=False)
+    cols = gather(both, "zh")
+    swapped, cols = lax.optimization_barrier((swapped, cols))
+    cols = gather(cols, "x")
+    rows = gather_direct(gather(swapped, "zl"), "y")
+    other = lax.ppermute(rows, "core", [(0, 1), (1, 0)])
 
     input_cols, output_cols = cols[:, :width], cols[:, width:]
-    input_rows = jnp.concatenate([rows[0, :, :width], rows[1, :, :width]], axis=1)
-    output_rows = jnp.concatenate([rows[0, :, width:], rows[1, :, width:]], axis=1)
-
-    grads_part = dot(output_rows, output_inverse, (((1,), (0,)), ((), ())))
+    own_inverse = lax.dynamic_slice_in_dim(output_inverse, core * grads_width, grads_width)
+    other_inverse = lax.dynamic_slice_in_dim(
+        output_inverse, (1 - core) * grads_width, grads_width
+    )
+    plain = (((1,), (0,)), ((), ()))
+    grads_part = dot(rows[:, width:], own_inverse, plain) + dot(
+        other[:, width:], other_inverse, plain
+    )
     grads_mixed = scatter_sum(scatter_sum(grads_part, "x", jnp.bfloat16), "zh", jnp.bfloat16)
-    grads_mixed = gather(gather(grads_mixed.astype(jnp.bfloat16), "zh"), "x")
+    grads_mixed = gather_direct(gather(grads_mixed.astype(jnp.bfloat16), "zh"), "x")
 
     halves = input_cols.reshape(CORES, tokens // CORES, width)
     halves = lax.all_to_all(halves, "core", 0, 0)
@@ -62,10 +76,17 @@
     input_part = dot(halves[0], inverse[0], by_cols) + dot(halves[1], inverse[1], by_cols)
     input_mixed = scatter_sum(scatter_sum(input_part, "y", jnp.float32), "zl", jnp.float32)
     input_mixed = gather(gather(input_mixed.astype(jnp.bfloat16), "zl"), "y")
-    input_mixed = gather(input_mixed, "core")
+    input_mixed = gather_direct(input_mixed, "core")
 
-    input_batch = dot(input_rows, input_cols, by_rows) / tokens
-    output_batch = dot(output_rows, output_cols, by_rows) / tokens
+    def batch(own, far, columns):
+        own = dot(own, columns, by_rows) / tokens
+        far = dot(far, columns, by_rows) / tokens
+        return jnp.where(
+            core == 0, jnp.concatenate([own, far]), jnp.concatenate([far, own])
+        )
+
+    input_batch = batch(rows[:, :width], other[:, :width], input_cols)
+    output_batch = batch(rows[:, width:], other[:, width:], output_cols)
     natural_gradient = dot(input_mixed, grads_mixed, by_rows) / tokens
     input_running = stat_decay * input_factor + (1.0 - stat_decay) * input_batch
     output_running = stat_decay * output_factor + (1.0 - stat_decay) * output_batch

time: 272 us -> 247 us (0.908)
  waiting for transfers between devices: 90.3 us -> 37.8 us
  starting transfers between devices: 8.91 us -> 39.2 us
  blocking collectives: 143 us -> 133 us
  matrix products: 7.68 us -> 12.2 us
  other arithmetic: 1.1 us -> 4.56 us
    all_gather x4 -> x1, waiting for transfers between devices: 88.9 us -> 0.01 us  [gather(): return lax.all_gather(block, axis, axis=0, tiled=True)]
    all_to_all x2 -> x4, waiting for transfers between devices: 1.33 us -> 28.4 us  [scatter_sum(): parts = lax.all_to_all(parts, axis, 0, 0)]
    all_to_all x0 -> x2, starting transfers between devices: none -> 16.2 us  [gather_direct(): lax.all_to_all(copies, axis, 0, 0)]
    all_to_all x2 -> x1, blocking collectives: 43.6 us -> 27.6 us  [gather_direct(): lax.all_to_all(copies, axis, 0, 0)]
    all_to_all x0 -> x2, waiting for transfers between devices: none -> 9.36 us  [gather_direct(): lax.all_to_all(copies, axis, 0, 0)]
    all_to_all x2 -> x4, starting transfers between devices: 8.05 us -> 16.5 us  [scatter_sum(): parts = lax.all_to_all(parts, axis, 0, 0)]
    ppermute x0 -> x1, starting transfers between devices: none -> 5.83 us  [per_device(): other = lax.ppermute(rows, 'core', [(0, 1), (1, 0)])]
    all_gather x5, blocking collectives: 92.5 us -> 98.2 us  [gather(): return lax.all_gather(block, axis, axis=0, tiled=True)]
  transfers between devices with their start and end apart: 8 -> 9, of which waited for: 4 -> 4; matrix products, arithmetic and copies ran while one was open for 4% -> 7% of each run, Pallas kernels for 0% -> 0%
where the time goes in v2:
time: 247 us; the launch traced here: 246 us
  blocking collectives  133 us (54%)
  starting transfers between devices  39.2 us (16%)
  waiting for transfers between devices  37.8 us (15%)
  between operations  14.2 us (6%)
  matrix products  12.2 us (5%)
  local copies, waits for them, and re-layouts  5 us (2%)
  other arithmetic  4.56 us (2%)
    all_gather x5, blocking collectives, gather(): return lax.all_gather(block, axis, axis=0, tiled=True)  98.2 us
    all_to_all x4, waiting for transfers between devices, scatter_sum(): parts = lax.all_to_all(parts, axis, 0, 0)  28.4 us
    all_to_all x1, blocking collectives, gather_direct(): lax.all_to_all(copies, axis, 0, 0)  27.6 us
    all_to_all x4, starting transfers between devices, scatter_sum(): parts = lax.all_to_all(parts, axis, 0, 0)  16.5 us
    all_to_all x2, starting transfers between devices, gather_direct(): lax.all_to_all(copies, axis, 0, 0)  16.2 us
    dot_general x9, matrix products, dot(): lax.dot_general(left, right, dims, preferred_element_type=jnp.float32)  12.2 us
    all_to_all x2, waiting for transfers between devices, gather_direct(): lax.all_to_all(copies, axis, 0, 0)  9.36 us
    ppermute x1, starting transfers between devices, per_device(): other = lax.ppermute(rows, 'core', [(0, 1), (1, 0)])  5.83 us
  transfers between devices with their start and end apart: 9, of which 4 were waited for; matrix products, arithmetic and copies ran while one was open for 7% of the time, Pallas kernels for 0%

profile of v2, /device:TPU:1, one launch (start us, length us, event | category | flops | bytes accessed | tf_op | source)
XLA Modules:
  0.0 246.1 jit_solution(5367173830395066779)
XLA Ops:
  9.5 34.5 %all_gather.24 = bf16[512,384]{1,0:T(8,128)(2,1)} all-gather(bf16[128,384]{1,0:T(8,128)(2,1)S(1)} %constant_dynamic-update-slice_fusion), channel_id=1, replica_groups=mesh['x'=4,'zh'=4,'y'=4,'zl'=4,'core'=2] {'zh'}, dimensions={0}, use_global_device_ids=true | all-gather | bytes 491520 | tf_op jit(solution)/shard_map/all_gather | solution.py:26
  44.1 16.6 %all_gather.25 = bf16[512,384]{1,0:T(8,128)(2,1)S(1)} all-gather(bf16[128,384]{1,0:T(8,128)(2,1)S(1)} %collective-permute-done), channel_id=1, replica_groups=mesh['x'=4,'zh'=4,'y'=4,'zl'=4,'core'=2] {'zl'}, dimensions={0}, use_global_device_ids=true | all-gather | bytes 491520 | tf_op jit(solution)/shard_map/all_gather | solution.py:26
  60.8 27.6 %all_to_all.40 = bf16[4,512,384]{2,1,0:T(8,128)(2,1)S(1)} all-to-all(bf16[4,512,384]{2,1,0:T(8,128)(2,1)S(1)} %broadcast_in_dim.6), channel_id=1, replica_groups=mesh['x'=4,'zh'=4,'y'=4,'zl'=4,'core'=2] {'y'}, dimensions={0} | all-to-all | bytes 3145728 | tf_op jit(solution)/shard_map/all_to_all | solution.py:42
  88.4 5.8 %collective-permute-start.1 = (bf16[2048,384]{1,0:T(8,128)(2,1)S(1)}, bf16[2048,384]{1,0:T(8,128)(2,1)}, u32[]{:S(2)}, u32[]{:S(2)}) collective-permute-start(bf16[2048,384]{1,0:T(8,128)(2,1)S(1)} %bitcast.16), channel_id=1, source_target_pairs={{0,1},{1,0},{2,3},{3,2},{4,5},{5,4},{6,7},{7,6},{8,9},{9,8},{10,11... | collective-permute-start | bytes 4718600 | tf_op jit(solution)/shard_map/ppermute | solution.py:59
  94.2 3.1 %all-gather = bf16[512,128]{1,0:T(8,128)(2,1)S(1)} all-gather(bf16[256,128]{1,0:T(8,128)(2,1)S(1)} %copy-done.4), channel_id=2, replica_groups=mesh['x'=4,'zh'=4,'y'=4,'zl'=4,'core'=2] {'core'}, dimensions={0}, use_global_device_ids=true | all-gather | bytes 196608 | tf_op jit(solution)/shard_map/all_gather | solution.py:75
  98.4 4.2 %all_to_all.41 = bf16[2,1024,128]{2,1,0:T(8,128)(2,1)S(1)} all-to-all(bf16[2,1024,128]{2,1,0:T(8,128)(2,1)S(1)} %bitcast.22), channel_id=1, replica_groups=mesh['x'=4,'zh'=4,'y'=4,'zl'=4,'core'=2] {'core'}, dimensions={0} | all-to-all | bytes 1048576 | tf_op jit(solution)/shard_map/all_to_all | solution.py:74
  104.1 3.5 %all-to-all-start.2 = ((f32[4,256,256]{2,1,0:T(8,128)}), f32[4,256,256]{2,1,0:T(8,128)S(1)}, u32[]{:S(2)}, u32[]{:S(2)}) async-start(f32[4,256,256]{2,1,0:T(8,128)} %bitcast.4), calls=%async_computation.2 | async-start | bytes 2097152 | tf_op jit(solution)/shard_map/all_to_all | solution.py:31
  108.1 2.7 %fusion = bf16[2048,256]{1,0:T(8,128)(2,1)} fusion(f32[2048,256]{1,0:T(8,128)S(1)} %fusion.5, bf16[2048,384]{1,0:T(8,128)(2,1)} %collective-permute-done.1, bf16[512,256]{1,0:T(8,128)(2,1)S(1)} %copy-done, s32[]{:T(128)S(6)} %select_n.27), kind=kOutput, calls=%fused_computation.1 | convolution fusion | flops 269484032 | bytes 4325380 | tf_op jit(solution)/shard_map/dot_general | solution.py:36
  110.8 11.7 %all-to-all-done.2 = f32[4,256,256]{2,1,0:T(8,128)S(1)} async-done(((f32[4,256,256]{2,1,0:T(8,128)}), f32[4,256,256]{2,1,0:T(8,128)S(1)}, u32[]{:S(2)}, u32[]{:S(2)}) %all-to-all-start.2) | async-done | bytes 1048608 | tf_op jit(solution)/shard_map/all_to_all | solution.py:31
  122.5 4.2 %all-to-all-start.5 = ((bf16[4,512,256]{2,1,0:T(8,128)(2,1)}), bf16[4,512,256]{2,1,0:T(8,128)(2,1)}, u32[]{:S(2)}, u32[]{:S(2)}) async-start(bf16[4,512,256]{2,1,0:T(8,128)(2,1)} %bitcast.7), calls=%async_computation.5 | async-start | bytes 2097152 | tf_op jit(solution)/shard_map/all_to_all | solution.py:31
  127.5 13.2 %all-to-all-done.5 = bf16[4,512,256]{2,1,0:T(8,128)(2,1)} async-done(((bf16[4,512,256]{2,1,0:T(8,128)(2,1)}), bf16[4,512,256]{2,1,0:T(8,128)(2,1)}, u32[]{:S(2)}, u32[]{:S(2)}) %all-to-all-start.5) | async-done | bytes 1048608 | tf_op jit(solution)/shard_map/all_to_all | solution.py:31
  140.7 3.4 %all-to-all-start.3 = ((f32[4,64,256]{2,1,0:T(8,128)}), f32[4,64,256]{2,1,0:T(8,128)S(1)}, u32[]{:S(2)}, u32[]{:S(2)}) async-start(f32[4,64,256]{2,1,0:T(8,128)} %bitcast.5), calls=%async_computation.3 | async-start | bytes 524288 | tf_op jit(solution)/shard_map/all_to_all | solution.py:31
  144.1 2.2 reduce_sum.44
  146.3 3.5 %all-to-all-done.3 = f32[4,64,256]{2,1,0:T(8,128)S(1)} async-done(((f32[4,64,256]{2,1,0:T(8,128)}), f32[4,64,256]{2,1,0:T(8,128)S(1)}, u32[]{:S(2)}, u32[]{:S(2)}) %all-to-all-start.3) | async-done | bytes 262176 | tf_op jit(solution)/shard_map/all_to_all | solution.py:31
  149.7 5.3 %all-to-all-start.6 = ((bf16[4,128,256]{2,1,0:T(8,128)(2,1)}), bf16[4,128,256]{2,1,0:T(8,128)(2,1)S(1)}, u32[]{:S(2)}, u32[]{:S(2)}) async-start(bf16[4,128,256]{2,1,0:T(8,128)(2,1)} %bitcast.8), calls=%async_computation.6 | async-start | bytes 524288 | tf_op jit(solution)/shard_map/all_to_all | solution.py:31
  156.5 1.7 convolution_multiply_fusion.2
  158.2 14.1 %all_gather.29 = bf16[256,256]{1,0:T(8,128)(2,1)S(1)} all-gather(bf16[64,256]{1,0:T(8,128)(2,1)S(1)} %reduce_sum.43), channel_id=1, replica_groups=mesh['x'=4,'zh'=4,'y'=4,'zl'=4,'core'=2] {'zl'}, dimensions={0}, use_global_device_ids=true | all-gather | bytes 163840 | tf_op jit(solution)/shard_map/all_gather | solution.py:26
  172.3 10.2 %all_gather.30 = bf16[1024,256]{1,0:T(8,128)(2,1)S(1)} all-gather(bf16[256,256]{1,0:T(8,128)(2,1)S(1)} %all_gather.29), channel_id=1, replica_groups=mesh['x'=4,'zh'=4,'y'=4,'zl'=4,'core'=2] {'y'}, dimensions={0}, use_global_device_ids=true | all-gather | bytes 655360 | tf_op jit(solution)/shard_map/all_gather | solution.py:26
  183.6 12.6 %all-to-all-start.4 = ((bf16[2,1024,256]{2,1,0:T(8,128)(2,1)}), bf16[2,1024,256]{2,1,0:T(8,128)(2,1)S(1)}, u32[]{:S(2)}, u32[]{:S(2)}) async-start(bf16[2,1024,256]{2,1,0:T(8,128)(2,1)} %broadcast_in_dim.7), calls=%async_computation.4 | async-start | bytes 2097152 | tf_op jit(solution)/shard_map/all_to_all | solution.py:42
  196.2 22.8 %all_gather.31 = bf16[512,256]{1,0:T(8,128)(2,1)S(1)} all-gather(bf16[128,256]{1,0:T(8,128)(2,1)S(1)} %reduce_sum.45), channel_id=1, replica_groups=mesh['x'=4,'zh'=4,'y'=4,'zl'=4,'core'=2] {'zh'}, dimensions={0}, use_global_device_ids=true | all-gather | bytes 327680 | tf_op jit(solution)/shard_map/all_gather | solution.py:26
  220.1 3.6 %all-to-all-start.7 = ((bf16[4,512,256]{2,1,0:T(8,128)(2,1)}), bf16[4,512,256]{2,1,0:T(8,128)(2,1)S(1)}, u32[]{:S(2)}, u32[]{:S(2)}) async-start(bf16[4,512,256]{2,1,0:T(8,128)(2,1)} %broadcast_in_dim.8), calls=%async_computation.7 | async-start | bytes 2097152 | tf_op jit(solution)/shard_map/all_to_all | solution.py:42
  223.7 1.7 convolution_multiply_fusion.3
  226.1 1.7 convolution_multiply_fusion.1
  228.7 9.4 %all-to-all-done.7 = bf16[4,512,256]{2,1,0:T(8,128)(2,1)S(1)} async-done(((bf16[4,512,256]{2,1,0:T(8,128)(2,1)}), bf16[4,512,256]{2,1,0:T(8,128)(2,1)S(1)}, u32[]{:S(2)}, u32[]{:S(2)}) %all-to-all-start.7) | async-done | bytes 1048608 | tf_op jit(solution)/shard_map/all_to_all | solution.py:42
  (34 shorter events, 12.7 us)
Async XLA Ops:
  7.2 100.5 %copy-start = (bf16[512,256]{1,0:T(8,128)(2,1)S(1)}, bf16[512,256]{1,0:T(8,128)(2,1)}, u32[]{:S(2)}) copy-start(bf16[512,256]{1,0:T(8,128)(2,1)} %param.11) | copy-start | bytes 786436
  7.2 90.1 %all-gather.3.cloned.1.call-start = ((), (), s32[]{:S(2)}) async-start(), calls=%async_computation.8 | async-start | bytes 1966080 | tf_op jit(solution)/shard_map/all_gather | solution.py:26
  8.9 35.2 %collective-permute-start = (bf16[128,384]{1,0:T(8,128)(2,1)S(1)}, bf16[128,384]{1,0:T(8,128)(2,1)S(1)}, u32[]{:S(2)}, u32[]{:S(2)}) collective-permute-start(bf16[128,384]{1,0:T(8,128)(2,1)S(1)} %constant_dynamic-update-slice_fusion), channel_id=1, source_target_pairs={{0,0},{1,1},{2,32},{3,33},{4,64},{5,65},{6,96},{7,97},{8,128},{9,1... | collective-permute-start | bytes 294920 | tf_op jit(solution)/shard_map/ppermute | solution.py:54
  60.8 33.4 %copy-start.4 = (bf16[256,128]{1,0:T(8,128)(2,1)S(1)}, bf16[256,128]{1,0:T(8,128)(2,1)}, u32[]{:S(2)}) copy-start(bf16[256,128]{1,0:T(8,128)(2,1)} %param.10) | copy-start | bytes 196612
  88.4 19.7 %collective-permute-start.1 = (bf16[2048,384]{1,0:T(8,128)(2,1)S(1)}, bf16[2048,384]{1,0:T(8,128)(2,1)}, u32[]{:S(2)}, u32[]{:S(2)}) collective-permute-start(bf16[2048,384]{1,0:T(8,128)(2,1)S(1)} %bitcast.16), channel_id=1, source_target_pairs={{0,1},{1,0},{2,3},{3,2},{4,5},{5,4},{6,7},{7,6},{8,9},{9,8},{10,11... | collective-permute-start | bytes 4718600 | tf_op jit(solution)/shard_map/ppermute | solution.py:59
  104.1 18.3 %all-to-all-start.2 = ((f32[4,256,256]{2,1,0:T(8,128)}), f32[4,256,256]{2,1,0:T(8,128)S(1)}, u32[]{:S(2)}, u32[]{:S(2)}) async-start(f32[4,256,256]{2,1,0:T(8,128)} %bitcast.4), calls=%async_computation.2 | async-start | bytes 2097152 | tf_op jit(solution)/shard_map/all_to_all | solution.py:31
  122.5 18.2 %all-to-all-start.5 = ((bf16[4,512,256]{2,1,0:T(8,128)(2,1)}), bf16[4,512,256]{2,1,0:T(8,128)(2,1)}, u32[]{:S(2)}, u32[]{:S(2)}) async-start(bf16[4,512,256]{2,1,0:T(8,128)(2,1)} %bitcast.7), calls=%async_computation.5 | async-start | bytes 2097152 | tf_op jit(solution)/shard_map/all_to_all | solution.py:31
  140.7 9.0 %all-to-all-start.3 = ((f32[4,64,256]{2,1,0:T(8,128)}), f32[4,64,256]{2,1,0:T(8,128)S(1)}, u32[]{:S(2)}, u32[]{:S(2)}) async-start(f32[4,64,256]{2,1,0:T(8,128)} %bitcast.5), calls=%async_computation.3 | async-start | bytes 524288 | tf_op jit(solution)/shard_map/all_to_all | solution.py:31
  149.7 32.8 %all-to-all-start.6 = ((bf16[4,128,256]{2,1,0:T(8,128)(2,1)}), bf16[4,128,256]{2,1,0:T(8,128)(2,1)S(1)}, u32[]{:S(2)}, u32[]{:S(2)}) async-start(bf16[4,128,256]{2,1,0:T(8,128)(2,1)} %bitcast.8), calls=%async_computation.6 | async-start | bytes 524288 | tf_op jit(solution)/shard_map/all_to_all | solution.py:31
  183.6 35.4 %all-to-all-start.4 = ((bf16[2,1024,256]{2,1,0:T(8,128)(2,1)}), bf16[2,1024,256]{2,1,0:T(8,128)(2,1)S(1)}, u32[]{:S(2)}, u32[]{:S(2)}) async-start(bf16[2,1024,256]{2,1,0:T(8,128)(2,1)} %broadcast_in_dim.7), calls=%async_computation.4 | async-start | bytes 2097152 | tf_op jit(solution)/shard_map/all_to_all | solution.py:42
  220.1 5.3 %copy-start.3 = (f32[256,128]{1,0:T(8,128)S(1)}, f32[256,128]{1,0:T(8,128)}, u32[]{:S(2)}) copy-start(f32[256,128]{1,0:T(8,128)} %param.8) | copy-start | bytes 393220
  220.1 18.0 %all-to-all-start.7 = ((bf16[4,512,256]{2,1,0:T(8,128)(2,1)}), bf16[4,512,256]{2,1,0:T(8,128)(2,1)S(1)}, u32[]{:S(2)}, u32[]{:S(2)}) async-start(bf16[4,512,256]{2,1,0:T(8,128)(2,1)} %broadcast_in_dim.8), calls=%async_computation.7 | async-start | bytes 2097152 | tf_op jit(solution)/shard_map/all_to_all | solution.py:42
  223.7 2.4 copy-start.2
  225.4 2.4 copy-start.1
Sparse Core Ops, SparseCore 0:
  44.2 38.0 all-gather.2

commit v3 on v1

v3 whole, which is shorter than its diff:
```python
import functools

import jax
import jax.numpy as jnp
from jax import lax
from jax.experimental import pallas as pl
from jax.experimental.pallas import tpu as pltpu
from jax.sharding import Mesh, PartitionSpec as P

stat_decay = 0.9
by_rows = (((0,), (0,)), ((), ()))
by_cols = (((1,), (1,)), ((), ()))
plain = (((1,), (0,)), ((), ()))
TOK = ("x", "zh")
FEAT = ("y", "zl", "core")
ALL = TOK + FEAT
SIDE = 4
CORES = 2
f32, bf16 = jnp.float32, jnp.bfloat16


def device(x, zh, y, zl, core):
    return (((x * SIDE + zh) * SIDE + y) * SIDE + zl) * CORES + core


def role_groups(first, second):
    groups = []
    for core, axis in ((0, first), (1, second)):
        others = [name for name in ALL[:4] if name != axis]
        for i in range(SIDE):
            for j in range(SIDE):
                for k in range(SIDE):
                    fixed = dict(zip(others, (i, j, k)))
                    groups.append(
                        [device(core=core, **fixed, **{axis: n}) for n in range(SIDE)]
                    )
    return groups


def swap_pairs():
    pairs = []
    for x in range(SIDE):
        for zh in range(SIDE):
            for y in range(SIDE):
                for zl in range(SIDE):
                    pairs.append((device(x, zh, y, zl, 0), device(x, zh, y, zl, 0)))
                    pairs.append((device(x, zh, y, zl, 1), device(y, zl, x, zh, 1)))
    return pairs


def ring_pairs(turn):
    pairs = []
    for group in role_groups("x", "y"):
        pairs += [(group[n], group[(n + turn) % SIDE]) for n in range(SIDE)]
    return pairs


def gather(block, groups):
    return lax.all_gather(block, ALL, axis_index_groups=groups, axis=0, tiled=False)


def exchange(parts, groups):
    return lax.all_to_all(parts, ALL, 0, 0, axis_index_groups=groups)


def gather_direct(block, groups):
    return exchange(jnp.broadcast_to(block[None], (SIDE,) + block.shape), groups)


def core_swap(block):
    return lax.ppermute(block, "core", [(0, 1), (1, 0)])


def dot(left, right, dims):
    return lax.dot_general(left, right, dims, preferred_element_type=f32)


def flat(block):
    return block.reshape(-1, block.shape[-1])


def local_call(body, out_shape, role, *operands, flops=0, steps=None, blocks=None):
    moved = sum(o.size * o.dtype.itemsize for o in operands)
    moved += sum(o.size * o.dtype.itemsize for o in jax.tree.leaves(out_shape))
    whole = pl.BlockSpec(memory_space=pltpu.VMEM)
    if steps is None:
        grid, in_blocks = (), [whole] * len(operands)
        out_blocks = jax.tree.map(lambda _: whole, out_shape)
    else:
        grid, in_blocks, out_blocks = (steps,), blocks[0], blocks[1]
    return pl.pallas_call(
        body,
        grid=grid,
        out_shape=out_shape,
        in_specs=[pl.BlockSpec(memory_space=pltpu.SMEM)] + in_blocks,
        out_specs=out_blocks,
        compiler_params=pltpu.CompilerParams(vmem_limit_bytes=24 * 1024 * 1024),
        cost_estimate=pl.CostEstimate(flops=flops, bytes_accessed=moved, transcendentals=0),
    )(role, *operands)


def block_at(shape, place):
    def index(step):
        return tuple(step if axis == place else 0 for axis in range(len(shape)))

    return pl.BlockSpec(shape, index)


def high_low(value):
    high = value.astype(bf16)
    return high, (value - high.astype(f32)).astype(bf16)


def partial_body(role, mine, in_inverse, out_inverse, out):
    deep = out_inverse.shape[1] // CORES

    @pl.when(role[0] == 0)
    def _():
        inverse = jnp.concatenate([in_inverse[0], in_inverse[1]], axis=1)
        high, low = high_low(dot(flat(mine[0, :, 0]), inverse, by_cols))
        out[0, 0] = high
        out[0, 1] = low

    @pl.when(role[0] == 1)
    def _():
        near, far = flat(mine[0, :, 0]), flat(mine[0, :, 1])
        for half in range(CORES):
            part = dot(near, out_inverse[half, :deep], plain)
            part = part + dot(far, out_inverse[half, deep:], plain)
            out[0, half] = part.astype(bf16)


def resum_body(role, parts, out):
    rows = out.shape[2]

    @pl.loop(0, SIDE)
    def _(i):
        at = pl.ds(pl.multiple_of(i * rows, rows), rows)
        totals = [
            sum(parts[k, half, at, :].astype(f32) for k in range(SIDE)) for half in range(CORES)
        ]

        @pl.when(role[0] == 0)
        def _():
            high, low = high_low(totals[0] + totals[1])
            out[i, 0] = high
            out[i, 1] = low

        @pl.when(role[0] == 1)
        def _():
            out[i, 0] = totals[0].astype(bf16)
            out[i, 1] = totals[1].astype(bf16)


def finish_body(role, parts, out):
    totals = [sum(parts[k, half].astype(f32) for k in range(SIDE)) for half in range(CORES)]

    @pl.when(role[0] == 0)
    def _():
        out[0] = (totals[0] + totals[1]).astype(bf16)
        out[1] = jnp.zeros_like(out[1])

    @pl.when(role[0] == 1)
    def _():
        out[0] = totals[0].astype(bf16)
        out[1] = totals[1].astype(bf16)


def natural_body(tokens, role, mixed, crossed, out):
    @pl.when(pl.program_id(0) == 0)
    def _():
        out[...] = jnp.zeros_like(out)

    @pl.when(role[0] == 0)
    def _():
        out[...] += dot(flat(mixed[0, :, 0]), flat(crossed[0]), by_rows) / tokens

    @pl.when(role[0] == 1)
    def _():
        out[...] += dot(flat(crossed[0]), flat(mixed[0, :, 1]), by_rows) / tokens


def running_body(role, mine, their, late, their_late, in_old, out_old, in_new, out_new):
    tokens = late.shape[0] * late.shape[1] * late.shape[2]
    width, wide = in_old.shape[1], out_old.shape[1]
    new_part = 1.0 - stat_decay

    def finish(in_rows, near_rows, far_rows, in_cols, out_cols):
        batch = sum(dot(in_rows(i), in_cols(i), by_rows) for i in range(SIDE)) / tokens
        in_new[...] = stat_decay * in_old[...] + new_part * batch
        for half, rows in ((0, near_rows), (1, far_rows)):
            at = pl.ds(half * wide, wide)
            batch = sum(dot(rows(i), out_cols(i), by_rows) for i in range(SIDE)) / tokens
            out_new[at, :] = stat_decay * out_old[at, :] + new_part * batch

    def part(ref, half, start=0, stop=None):
        return lambda i: flat(ref[i, :, half, :, start:stop])

    def turned(ref, spot):
        return lambda i: flat(ref[lax.rem(spot + (SIDE - i), SIDE)])

    @pl.when(role[0] == 0)
    def _():
        rows, cols = turned(their_late, role[2]), part(mine, 0, 0, width)
        finish(rows, part(their, 0), part(their, 1), cols, part(mine, 1))

    @pl.when(role[0] == 1)
    def _():
        rows, cols = turned(late, role[1]), part(their, 0, width)
        finish(rows, part(mine, 0), part(mine, 1), cols, turned(their_late, role[2]))


def per_device(
    layer_inputs, output_grads, input_factor, output_factor, input_inverse, output_inverse
):
    rows = layer_inputs.shape[0]
    wide = output_grads.shape[1]
    tokens = rows * SIDE * SIDE
    core = lax.axis_index("core")
    first = core == 0
    role = core.astype(jnp.int32).reshape(1)
    spot = (lax.axis_index("x"), lax.axis_index("y"))
    tied = lax.optimization_barrier

    out_z = role_groups("zh", "zl")
    out_xy = role_groups("x", "y")
    back_z = role_groups("zl", "zh")
    back_xy = role_groups("y", "x")

    grads_pair = lax.all_gather(output_grads, "core", axis=0, tiled=False)
    grads_moved = lax.ppermute(grads_pair, ALL, swap_pairs())
    grads_pair, layer_inputs = tied((grads_pair, layer_inputs))
    input_pair = lax.all_gather(layer_inputs, "core", axis=1, tiled=True)
    inputs_moved = lax.ppermute(input_pair, ALL, swap_pairs())

    block = jnp.where(first, jnp.stack([input_pair, grads_pair[0]]), grads_moved)
    block = gather(block, out_z)
    block, late, inputs_moved, input_inverse, output_inverse = tied(
        (block, grads_pair[1], inputs_moved, input_inverse, output_inverse)
    )
    mine = gather_direct(block, out_xy)
    in_inverse = lax.all_gather(input_inverse, "core", axis=0, tiled=False)
    out_inverse = lax.all_gather(output_inverse, "core", axis=0, tiled=False)

    part = local_call(
        partial_body,
        jax.ShapeDtypeStruct((SIDE, CORES, SIDE * rows, wide), bf16),
        role,
        mine,
        in_inverse,
        out_inverse,
        flops=2 * tokens * 4 * wide * wide,
        steps=SIDE,
        blocks=(
            [
                block_at((1, SIDE, CORES, rows, wide), 0),
                block_at(in_inverse.shape, None),
                block_at(out_inverse.shape, None),
            ],
            block_at((1, CORES, SIDE * rows, wide), 0),
        ),
    )
    part, late, inputs_moved = tied((part, late, inputs_moved))
    late = gather(jnp.where(first, late, inputs_moved), out_z)
    part = exchange(part, back_xy)
    part, late = tied((part, late))
    part = local_call(
        resum_body,
        jax.ShapeDtypeStruct((SIDE, CORES, rows, wide), bf16),
        role,
        part,
    )
    part, late = tied((part, late))
    part = exchange(part, back_z)
    left = lax.ppermute(late, ALL, ring_pairs(1))
    right = lax.ppermute(late, ALL, ring_pairs(-1))
    span = SIDE // CORES
    ahead = lax.ppermute(left[:span], ALL, ring_pairs(1))
    behind = lax.ppermute(right[span:], ALL, ring_pairs(-1))
    late = jnp.stack([late, left, jnp.concatenate([ahead, behind]), right])
    part, late = tied((part, late))
    mixed = local_call(
        finish_body, jax.ShapeDtypeStruct((CORES, rows, wide), bf16), role, part
    )
    mixed = gather(mixed, back_z)
    mixed, mine, late = tied((mixed, mine, late))
    mixed = gather_direct(mixed, back_xy)
    their, their_late = core_swap(mine), core_swap(late)
    input_running, output_running = local_call(
        running_body,
        (
            jax.ShapeDtypeStruct(input_factor.shape, f32),
            jax.ShapeDtypeStruct(output_factor.shape, f32),
        ),
        jnp.stack([core, jnp.where(first, spot[0], spot[1]), jnp.where(first, spot[1], spot[0])]),
        mine,
        their,
        late,
        their_late,
        input_factor,
        output_factor,
        flops=2 * tokens * (2 * wide * wide + wide * wide // 2),
    )
    mixed, input_running, output_running = tied((mixed, input_running, output_running))
    crossed = core_swap(mixed[:, :, 0])
    natural_gradient = local_call(
        functools.partial(natural_body, tokens),
        jax.ShapeDtypeStruct((wide, wide), f32),
        role,
        mixed,
        crossed,
        flops=2 * tokens * wide * wide,
        steps=SIDE,
        blocks=(
            [
                block_at((1, SIDE, CORES, rows, wide), 0),
                block_at((1, SIDE, rows, wide), 0),
            ],
            block_at((wide, wide), None),
        ),
    )
    return (input_running, output_running, natural_gradient)


def solution(mesh):
    grid = Mesh(mesh.devices.reshape(SIDE, SIDE, SIDE, SIDE, CORES), ALL)
    spec = P(TOK, FEAT)
    return jax.shard_map(
        per_device, mesh=grid, in_specs=(spec,) * 6, out_specs=(spec,) * 3, check_vma=False
    )
```

time: 272 us -> 175 us (0.64)
  blocking collectives: 143 us -> 74.8 us
  waiting for transfers between devices: 90.3 us -> 28.5 us
  starting transfers between devices: 8.91 us -> 49.7 us
  between operations: 13.9 us -> 0.86 us
  Pallas kernels: 0 us -> 11.4 us
  matrix products: 7.68 us -> 0 us
    all_gather x5 -> x0, waiting for transfers between devices: 88.9 us -> none  [the longest x4 88.9 us: gather(): return lax.all_gather(block, axis, axis=0, tiled=True)]
    all_to_all x3 -> x0, blocking collectives: 48.1 us -> none  [the longest x2 43.6 us: scatter_sum(): parts = lax.all_to_all(parts, axis, 0, 0)]
    ppermute x1 -> x9, starting transfers between devices: 0.65 us -> 22.2 us  [the longest x3 7.91 us: core_swap(): return lax.ppermute(block, 'core', [(0, 1), (1, 0)])]
    all_to_all x2 -> x4, waiting for transfers between devices: 1.33 us -> 21.6 us  [exchange(): return lax.all_to_all(parts, ALL, 0, 0, axis_index_groups=groups)]
    all_gather x6 -> x7, blocking collectives: 94.7 us -> 74.8 us  [the longest x3 59.9 us: gather(): lax.all_gather(block, ALL, axis_index_groups=groups, axis=0, tiled=False)]
    all_to_all x2 -> x4, starting transfers between devices: 8.05 us -> 27.5 us  [exchange(): return lax.all_to_all(parts, ALL, 0, 0, axis_index_groups=groups)]
    pallas_call x0 -> x5, Pallas kernels: none -> 11.4 us  [local_call(): pl.pallas_call(body, grid=grid, out_shape=out_shape, in_specs=[pl.BlockSp...]
    dot_general x6 -> x0, matrix products: 7.68 us -> none  [dot(): lax.dot_general(left, right, dims, preferred_element_type=jnp.float32)]
  transfers between devices with their start and end apart: 8 -> 13, of which waited for: 4 -> 9; matrix products, arithmetic and copies ran while one was open for 4% -> 2% of each run, Pallas kernels for 0% -> 2%
where the time goes in v3:
time: 175 us; the launch traced here: 174 us
  blocking collectives  74.8 us (43%)
  starting transfers between devices  49.7 us (28%)
  waiting for transfers between devices  28.5 us (16%)
  Pallas kernels  11.4 us (7%)
  local copies, waits for them, and re-layouts  8.64 us (5%)
    all_gather x3, blocking collectives, gather(): lax.all_gather(block, ALL, axis_index_groups=groups, axis=0, tiled=False)  59.9 us
    all_to_all x4, starting transfers between devices, exchange(): return lax.all_to_all(parts, ALL, 0, 0, axis_index_groups=groups)  27.5 us
    all_to_all x4, waiting for transfers between devices, exchange(): return lax.all_to_all(parts, ALL, 0, 0, axis_index_groups=groups)  21.6 us
    pallas_call x5, Pallas kernels, local_call(): pl.pallas_call(body, grid=grid, out_shape=out_shape, in_specs=[pl.BlockSp...  11.4 us
    all_gather x1, blocking collectives, per_device(): grads_pair = lax.all_gather(output_grads, 'core', axis=0, tiled=False)  8.64 us
    ppermute x3, starting transfers between devices, core_swap(): return lax.ppermute(block, 'core', [(0, 1), (1, 0)])  7.91 us
    ppermute x1, starting transfers between devices, per_device(): behind = lax.ppermute(right[span:], ALL, ring_pairs(-1))  4.57 us
    ppermute x1, starting transfers between devices, per_device(): right = lax.ppermute(late, ALL, ring_pairs(-1))  4.3 us
  transfers between devices with their start and end apart: 13, of which 9 were waited for; matrix products, arithmetic and copies ran while one was open for 2% of the time, Pallas kernels for 2%

profile of v3, /device:TPU:1, one launch (start us, length us, event | category | flops | bytes accessed | tf_op | source)
XLA Modules:
  0.0 174.1 jit_solution(16092819980684859954)
XLA Ops:
  0.6 8.6 %all-gather = bf16[256,256]{1,0:T(8,128)(2,1)S(1)} all-gather(bf16[128,256]{1,0:T(8,128)(2,1)} %param.7), channel_id=2, replica_groups=mesh['x'=4,'zh'=4,'y'=4,'zl'=4,'core'=2] {'core'}, dimensions={0}, use_global_device_ids=true | all-gather | bytes 196608 | tf_op jit(solution)/shard_map/all_gather | solution.py:230
  9.9 2.1 %all_gather.41 = bf16[128,256]{1,0:T(8,128)(2,1)S(1)} all-gather(bf16[128,128]{1,0:T(8,128)(2,1)} %param.6), channel_id=1, replica_groups=mesh['x'=4,'zh'=4,'y'=4,'zl'=4,'core'=2] {'core'}, dimensions={1}, use_global_device_ids=true | all-gather | bytes 98304 | tf_op jit(solution)/shard_map/all_gather | solution.py:233
  12.8 25.8 %all-gather.1 = bf16[8,128,256]{2,1,0:T(8,128)(2,1)S(1)} all-gather(bf16[2,128,256]{2,1,0:T(8,128)(2,1)S(1)} %maximum_select_fusion), channel_id=3, replica_groups={{0,32,64,96},{2,34,66,98},{4,36,68,100},{6,38,70,102},{8,40,72,104},{10..., dimensions={0}, use_global_device_ids=true | all-gather | bytes 655360 | tf_op jit(solution)/shard_map/all_gather | solution.py:59
  40.2 7.7 %all-to-all-start = ((bf16[4,4,2,128,256]{4,3,2,1,0:T(8,128)(2,1)}), bf16[4,4,2,128,256]{4,3,2,1,0:T(8,128)(2,1)S(1)}, u32[]{:S(2)}, u32[]{:S(2)}) async-start(bf16[4,4,2,128,256]{4,3,2,1,0:T(8,128)(2,1)} %broadcast_in_dim.4), calls=%async_computation | async-start | bytes 4194304 | tf_op jit(solution)/shard_map/all_to_all | solution.py:63
  49.7 2.2 %all-gather.3 = bf16[1024,256]{1,0:T(8,128)(2,1)S(1)} all-gather(bf16[512,256]{1,0:T(8,128)(2,1)S(1)} %copy-done.3), channel_id=5, replica_groups=mesh['x'=4,'zh'=4,'y'=4,'zl'=4,'core'=2] {'core'}, dimensions={0}, use_global_device_ids=true | all-gather | bytes 786432 | tf_op jit(solution)/shard_map/all_gather | solution.py:243
  51.9 11.3 %all-to-all-done.mine = bf16[4,4,2,128,256]{4,3,2,1,0:T(8,128)(2,1)S(1)} async-done(((bf16[4,4,2,128,256]{4,3,2,1,0:T(8,128)(2,1)}), bf16[4,4,2,128,256]{4,3,2,1,0:T(8,128)(2,1)S(1)}, u32[]{:S(2)}, u32[]{:S(2)}) %all-to-all-start) | async-done | bytes 2097184 | tf_op jit(solution)/shard_map/all_to_all | solution.py:63
  66.3 4.5 %all-to-all-start.1 = ((bf16[4,2,512,256]{3,2,1,0:T(8,128)(2,1)}), bf16[4,2,512,256]{3,2,1,0:T(8,128)(2,1)}, u32[]{:S(2)}, u32[]{:S(2)}) async-start(bf16[4,2,512,256]{3,2,1,0:T(8,128)(2,1)} %copy-done), calls=%async_computation.1 | async-start | bytes 4194304 | tf_op jit(solution)/shard_map/all_to_all | solution.py:63
  70.8 11.4 %all-gather.4 = bf16[512,256]{1,0:T(8,128)(2,1)S(1)} all-gather(bf16[128,256]{1,0:T(8,128)(2,1)S(1)} %broadcast_select_fusion), channel_id=6, replica_groups={{0,32,64,96},{2,34,66,98},{4,36,68,100},{6,38,70,102},{8,40,72,104},{10..., dimensions={0}, use_global_device_ids=true | all-gather | bytes 327680 | tf_op jit(solution)/shard_map/all_gather | solution.py:59
  82.2 4.0 %all-to-all-done.1.parts = bf16[4,2,512,256]{3,2,1,0:T(8,128)(2,1)} async-done(((bf16[4,2,512,256]{3,2,1,0:T(8,128)(2,1)}), bf16[4,2,512,256]{3,2,1,0:T(8,128)(2,1)}, u32[]{:S(2)}, u32[]{:S(2)}) %all-to-all-start.1) | async-done | bytes 2097184 | tf_op jit(solution)/shard_map/all_to_all | solution.py:63
  86.2 2.7 %shard_map.86 = bf16[4,2,128,256]{3,2,1,0:T(8,128)(2,1)} custom-call(s32[1]{0:T(128)} %bitcast.role, bf16[4,2,512,256]{3,2,1,0:T(8,128)(2,1)} %all-to-all-done.1.parts), custom_call_target="tpu_custom_call" | custom-call | bytes 2621440 | tf_op jit(solution)/shard_map/pallas_call | solution.py:91
  89.0 10.8 %all-to-all-start.2 = ((bf16[4,2,128,256]{3,2,1,0:T(8,128)(2,1)}), bf16[4,2,128,256]{3,2,1,0:T(8,128)(2,1)}, u32[]{:S(2)}, u32[]{:S(2)}) async-start(bf16[4,2,128,256]{3,2,1,0:T(8,128)(2,1)} %shard_map.86), calls=%async_computation.2 | async-start | bytes 1048576 | tf_op jit(solution)/shard_map/all_to_all | solution.py:63
  99.7 2.2 %collective-permute-start.2 = (bf16[4,128,256]{2,1,0:T(8,128)(2,1)S(1)}, bf16[4,128,256]{2,1,0:T(8,128)(2,1)S(1)}, u32[]{:S(2)}, u32[]{:S(2)}) collective-permute-start(bf16[4,128,256]{2,1,0:T(8,128)(2,1)S(1)} %bitcast.23), channel_id=1, source_target_pairs={{0,128},{128,256},{256,384},{384,0},{2,130},{130,258},{258,386},{3... | collective-permute-start | bytes 786440 | tf_op jit(solution)/shard_map/ppermute | solution.py:275
  101.9 4.3 %collective-permute-start.4 = (bf16[4,128,256]{2,1,0:T(8,128)(2,1)S(1)}, bf16[4,128,256]{2,1,0:T(8,128)(2,1)S(1)}, u32[]{:S(2)}, u32[]{:S(2)}) collective-permute-start(bf16[4,128,256]{2,1,0:T(8,128)(2,1)S(1)} %bitcast.24), channel_id=1, source_target_pairs={{0,384},{128,0},{256,128},{384,256},{2,386},{130,2},{258,130},{386... | collective-permute-start | bytes 786440 | tf_op jit(solution)/shard_map/ppermute | solution.py:276
  106.2 2.2 %collective-permute-done.2 = bf16[4,128,256]{2,1,0:T(8,128)(2,1)S(1)} collective-permute-done((bf16[4,128,256]{2,1,0:T(8,128)(2,1)S(1)}, bf16[4,128,256]{2,1,0:T(8,128)(2,1)S(1)}, u32[]{:S(2)}, u32[]{:S(2)}) %collective-permute-start.2) | collective-permute-done | bytes 262176 | tf_op jit(solution)/shard_map/ppermute | solution.py:275
  108.5 1.9 %collective-permute-start.3 = (bf16[2,128,256]{2,1,0:T(8,128)(2,1)S(1)}, bf16[2,128,256]{2,1,0:T(8,128)(2,1)S(1)}, u32[]{:S(2)}, u32[]{:S(2)}) collective-permute-start(bf16[2,128,256]{2,1,0:T(8,128)(2,1)S(1)} %slice.20), channel_id=1, source_target_pairs={{0,128},{128,256},{256,384},{384,0},{2,130},{130,258},{258,386},{3... | collective-permute-start | bytes 393224 | tf_op jit(solution)/shard_map/ppermute | solution.py:278
  110.4 4.6 %collective-permute-start.5 = (bf16[2,128,256]{2,1,0:T(8,128)(2,1)S(1)}, bf16[2,128,256]{2,1,0:T(8,128)(2,1)S(1)}, u32[]{:S(2)}, u32[]{:S(2)}) collective-permute-start(bf16[2,128,256]{2,1,0:T(8,128)(2,1)S(1)} %slice.21), channel_id=1, source_target_pairs={{0,384},{128,0},{256,128},{384,256},{2,386},{130,2},{258,130},{386... | collective-permute-start | bytes 393224 | tf_op jit(solution)/shard_map/ppermute | solution.py:279
  118.6 22.7 %all-gather.5 = bf16[8,128,256]{2,1,0:T(8,128)(2,1)S(1)} all-gather(bf16[2,128,256]{2,1,0:T(8,128)(2,1)S(1)} %shard_map.87), channel_id=7, replica_groups={{0,2,4,6},{8,10,12,14},{16,18,20,22},{24,26,28,30},{32,34,36,38},{40,42..., dimensions={0}, use_global_device_ids=true | all-gather | bytes 655360 | tf_op jit(solution)/shard_map/all_gather | solution.py:59
  141.3 1.9 %collective-permute-start.6 = (bf16[4,4,2,128,256]{4,3,2,1,0:T(8,128)(2,1)S(1)}, bf16[4,4,2,128,256]{4,3,2,1,0:T(8,128)(2,1)}, u32[]{:S(2)}, u32[]{:S(2)}) collective-permute-start(bf16[4,4,2,128,256]{4,3,2,1,0:T(8,128)(2,1)S(1)} %all-to-all-done.mine), channel_id=1, source_target_pairs={{0,1},{1,0},{2,3},{3,2},{4,5},{5,4},{6,7},{7,6},{8,9},{9,8},{10,11... | collective-permute-start | bytes 6291464 | tf_op jit(solution)/shard_map/ppermute | solution.py:71
  144.8 4.6 %all-to-all-start.3 = ((bf16[4,4,2,128,256]{4,3,1,2,0:T(8,128)(2,1)}), bf16[4,4,2,128,256]{4,3,1,2,0:T(8,128)(2,1)}, u32[]{:S(2)}, u32[]{:S(2)}) async-start(bf16[4,4,2,128,256]{4,3,1,2,0:T(8,128)(2,1)} %broadcast_in_dim.5), calls=%async_computation.3 | async-start | bytes 4194304 | tf_op jit(solution)/shard_map/all_to_all | solution.py:63
  149.4 2.5 %collective-permute-start.7 = (bf16[4,4,128,256]{3,2,1,0:T(8,128)(2,1)S(1)}, bf16[4,4,128,256]{3,2,1,0:T(8,128)(2,1)}, u32[]{:S(2)}, u32[]{:S(2)}) collective-permute-start(bf16[4,4,128,256]{3,2,1,0:T(8,128)(2,1)S(1)} %pad_maximum_fusion.late), channel_id=1, source_target_pairs={{0,1},{1,0},{2,3},{3,2},{4,5},{5,4},{6,7},{7,6},{8,9},{9,8},{10,11... | collective-permute-start | bytes 3145736 | tf_op jit(solution)/shard_map/ppermute | solution.py:71
  152.1 2.3 %collective-permute-done.7.their_late = bf16[4,4,128,256]{3,2,1,0:T(8,128)(2,1)} collective-permute-done((bf16[4,4,128,256]{3,2,1,0:T(8,128)(2,1)S(1)}, bf16[4,4,128,256]{3,2,1,0:T(8,128)(2,1)}, u32[]{:S(2)}, u32[]{:S(2)}) %collective-permute-start.7) | collective-permute-done | bytes 1048608 | tf_op jit(solution)/shard_map/ppermute | solution.py:71
  155.4 3.8 %shard_map.88 = (f32[256,128]{1,0:T(8,128)}, f32[512,256]{1,0:T(8,128)}) custom-call(s32[3]{0:T(128)S(1)} %pad_add_fusion.role, bf16[4,4,2,128,256]{4,3,2,1,0:T(8,128)(2,1)S(1)} %all-to-all-done.mine, bf16[4,4,2,128,256]{4,3,2,1,0:T(8,128)(2,1)} %collective-permute-done.6.their, bf16[4,4,128,256]{3,2,1,0:T(8,128)(2,1)S(1)} %pad_maximum_fusion.late, ...), custom_call_target="tpu_custom_call" | custom-call | flops 671088640 | bytes 7602176 | tf_op jit(solution)/shard_map/pallas_call | solution.py:91
  159.2 5.9 %all-to-all-done.3 = bf16[4,4,2,128,256]{4,3,1,2,0:T(8,128)(2,1)} async-done(((bf16[4,4,2,128,256]{4,3,1,2,0:T(8,128)(2,1)}), bf16[4,4,2,128,256]{4,3,1,2,0:T(8,128)(2,1)}, u32[]{:S(2)}, u32[]{:S(2)}) %all-to-all-start.3) | async-done | bytes 2097184 | tf_op jit(solution)/shard_map/all_to_all | solution.py:63
  166.5 3.5 %collective-permute-start.8 = (bf16[4,4,128,256]{3,2,1,0:T(8,128)(2,1)S(1)}, bf16[4,4,128,256]{3,2,1,0:T(8,128)(2,1)S(1)}, u32[]{:S(2)}, u32[]{:S(2)}) collective-permute-start(bf16[4,4,128,256]{3,2,1,0:T(8,128)(2,1)S(1)} %slice_bitcast_fusion), channel_id=1, source_target_pairs={{0,1},{1,0},{2,3},{3,2},{4,5},{5,4},{6,7},{7,6},{8,9},{9,8},{10,11... | collective-permute-start | bytes 3145736 | tf_op jit(solution)/shard_map/ppermute | solution.py:71
  (37 shorter events, 19.7 us)
Async XLA Ops:
  9.3 3.5 %collective-permute-start = (bf16[2,128,256]{2,1,0:T(8,128)(2,1)S(1)}, bf16[2,128,256]{2,1,0:T(8,128)(2,1)S(1)}, u32[]{:S(2)}, u32[]{:S(2)}) collective-permute-start(bf16[2,128,256]{2,1,0:T(8,128)(2,1)S(1)} %bitcast.28), channel_id=1, source_target_pairs={{0,0},{1,1},{2,2},{3,33},{4,4},{5,65},{6,6},{7,97},{8,8},{9,129},{... | collective-permute-start | bytes 393224 | tf_op jit(solution)/shard_map/ppermute | solution.py:231
  12.1 26.5 %collective-permute-start.1 = (bf16[128,256]{1,0:T(8,128)(2,1)S(1)}, bf16[128,256]{1,0:T(8,128)(2,1)S(1)}, u32[]{:S(2)}, u32[]{:S(2)}) collective-permute-start(bf16[128,256]{1,0:T(8,128)(2,1)S(1)} %all_gather.41), channel_id=1, source_target_pairs={{0,0},{1,1},{2,2},{3,33},{4,4},{5,65},{6,6},{7,97},{8,8},{9,129},{... | collective-permute-start | bytes 196616 | tf_op jit(solution)/shard_map/ppermute | solution.py:234
  40.2 7.7 %copy-start.4 = (bf16[256,128]{1,0:T(8,128)(2,1)S(1)}, bf16[256,128]{1,0:T(8,128)(2,1)}, u32[]{:S(2)}) copy-start(bf16[256,128]{1,0:T(8,128)(2,1)} %param.10) | copy-start | bytes 196612
  40.2 9.6 %copy-start.3 = (bf16[512,256]{1,0:T(8,128)(2,1)S(1)}, bf16[512,256]{1,0:T(8,128)(2,1)}, u32[]{:S(2)}) copy-start(bf16[512,256]{1,0:T(8,128)(2,1)} %param.11) | copy-start | bytes 786436
  40.2 23.0 %all-to-all-start = ((bf16[4,4,2,128,256]{4,3,2,1,0:T(8,128)(2,1)}), bf16[4,4,2,128,256]{4,3,2,1,0:T(8,128)(2,1)S(1)}, u32[]{:S(2)}, u32[]{:S(2)}) async-start(bf16[4,4,2,128,256]{4,3,2,1,0:T(8,128)(2,1)} %broadcast_in_dim.4), calls=%async_computation | async-start | bytes 4194304 | tf_op jit(solution)/shard_map/all_to_all | solution.py:63
  65.0 1.3 copy-start
  66.3 19.9 %all-to-all-start.1 = ((bf16[4,2,512,256]{3,2,1,0:T(8,128)(2,1)}), bf16[4,2,512,256]{3,2,1,0:T(8,128)(2,1)}, u32[]{:S(2)}, u32[]{:S(2)}) async-start(bf16[4,2,512,256]{3,2,1,0:T(8,128)(2,1)} %copy-done), calls=%async_computation.1 | async-start | bytes 4194304 | tf_op jit(solution)/shard_map/all_to_all | solution.py:63
  89.0 28.5 %all-to-all-start.2 = ((bf16[4,2,128,256]{3,2,1,0:T(8,128)(2,1)}), bf16[4,2,128,256]{3,2,1,0:T(8,128)(2,1)}, u32[]{:S(2)}, u32[]{:S(2)}) async-start(bf16[4,2,128,256]{3,2,1,0:T(8,128)(2,1)} %shard_map.86), calls=%async_computation.2 | async-start | bytes 1048576 | tf_op jit(solution)/shard_map/all_to_all | solution.py:63
  99.7 8.7 %collective-permute-start.2 = (bf16[4,128,256]{2,1,0:T(8,128)(2,1)S(1)}, bf16[4,128,256]{2,1,0:T(8,128)(2,1)S(1)}, u32[]{:S(2)}, u32[]{:S(2)}) collective-permute-start(bf16[4,128,256]{2,1,0:T(8,128)(2,1)S(1)} %bitcast.23), channel_id=1, source_target_pairs={{0,128},{128,256},{256,384},{384,0},{2,130},{130,258},{258,386},{3... | collective-permute-start | bytes 786440 | tf_op jit(solution)/shard_map/ppermute | solution.py:275
  101.9 8.5 %collective-permute-start.4 = (bf16[4,128,256]{2,1,0:T(8,128)(2,1)S(1)}, bf16[4,128,256]{2,1,0:T(8,128)(2,1)S(1)}, u32[]{:S(2)}, u32[]{:S(2)}) collective-permute-start(bf16[4,128,256]{2,1,0:T(8,128)(2,1)S(1)} %bitcast.24), channel_id=1, source_target_pairs={{0,384},{128,0},{256,128},{384,256},{2,386},{130,2},{258,130},{386... | collective-permute-start | bytes 786440 | tf_op jit(solution)/shard_map/ppermute | solution.py:276
  108.5 7.2 %collective-permute-start.3 = (bf16[2,128,256]{2,1,0:T(8,128)(2,1)S(1)}, bf16[2,128,256]{2,1,0:T(8,128)(2,1)S(1)}, u32[]{:S(2)}, u32[]{:S(2)}) collective-permute-start(bf16[2,128,256]{2,1,0:T(8,128)(2,1)S(1)} %slice.20), channel_id=1, source_target_pairs={{0,128},{128,256},{256,384},{384,0},{2,130},{130,258},{258,386},{3... | collective-permute-start | bytes 393224 | tf_op jit(solution)/shard_map/ppermute | solution.py:278
  110.4 6.5 %collective-permute-start.5 = (bf16[2,128,256]{2,1,0:T(8,128)(2,1)S(1)}, bf16[2,128,256]{2,1,0:T(8,128)(2,1)S(1)}, u32[]{:S(2)}, u32[]{:S(2)}) collective-permute-start(bf16[2,128,256]{2,1,0:T(8,128)(2,1)S(1)} %slice.21), channel_id=1, source_target_pairs={{0,384},{128,0},{256,128},{384,256},{2,386},{130,2},{258,130},{386... | collective-permute-start | bytes 393224 | tf_op jit(solution)/shard_map/ppermute | solution.py:279
  141.3 13.0 %collective-permute-start.6 = (bf16[4,4,2,128,256]{4,3,2,1,0:T(8,128)(2,1)S(1)}, bf16[4,4,2,128,256]{4,3,2,1,0:T(8,128)(2,1)}, u32[]{:S(2)}, u32[]{:S(2)}) collective-permute-start(bf16[4,4,2,128,256]{4,3,2,1,0:T(8,128)(2,1)S(1)} %all-to-all-done.mine), channel_id=1, source_target_pairs={{0,1},{1,0},{2,3},{3,2},{4,5},{5,4},{6,7},{7,6},{8,9},{9,8},{10,11... | collective-permute-start | bytes 6291464 | tf_op jit(solution)/shard_map/ppermute | solution.py:71
  144.8 9.6 %copy-start.2 = (f32[256,128]{1,0:T(8,128)S(1)}, f32[256,128]{1,0:T(8,128)}, u32[]{:S(2)}) copy-start(f32[256,128]{1,0:T(8,128)} %in_old.1) | copy-start | bytes 393220
  144.8 20.3 %all-to-all-start.3 = ((bf16[4,4,2,128,256]{4,3,1,2,0:T(8,128)(2,1)}), bf16[4,4,2,128,256]{4,3,1,2,0:T(8,128)(2,1)}, u32[]{:S(2)}, u32[]{:S(2)}) async-start(bf16[4,4,2,128,256]{4,3,1,2,0:T(8,128)(2,1)} %broadcast_in_dim.5), calls=%async_computation.3 | async-start | bytes 4194304 | tf_op jit(solution)/shard_map/all_to_all | solution.py:63
  149.4 5.0 %collective-permute-start.7 = (bf16[4,4,128,256]{3,2,1,0:T(8,128)(2,1)S(1)}, bf16[4,4,128,256]{3,2,1,0:T(8,128)(2,1)}, u32[]{:S(2)}, u32[]{:S(2)}) collective-permute-start(bf16[4,4,128,256]{3,2,1,0:T(8,128)(2,1)S(1)} %pad_maximum_fusion.late), channel_id=1, source_target_pairs={{0,1},{1,0},{2,3},{3,2},{4,5},{5,4},{6,7},{7,6},{8,9},{9,8},{10,11... | collective-permute-start | bytes 3145736 | tf_op jit(solution)/shard_map/ppermute | solution.py:71
  154.4 1.0 copy-start.1
  166.5 5.7 %collective-permute-start.8 = (bf16[4,4,128,256]{3,2,1,0:T(8,128)(2,1)S(1)}, bf16[4,4,128,256]{3,2,1,0:T(8,128)(2,1)S(1)}, u32[]{:S(2)}, u32[]{:S(2)}) collective-permute-start(bf16[4,4,128,256]{3,2,1,0:T(8,128)(2,1)S(1)} %slice_bitcast_fusion), channel_id=1, source_target_pairs={{0,1},{1,0},{2,3},{3,2},{4,5},{5,4},{6,7},{7,6},{8,9},{9,8},{10,11... | collective-permute-start | bytes 3145736 | tf_op jit(solution)/shard_map/ppermute | solution.py:71

commit v4 on v3

--- a/solution.py
+++ b/solution.py
@@ -1,4 +1,5 @@
 import functools
+import math
 
 import jax
 import jax.numpy as jnp
@@ -79,13 +80,13 @@
     return block.reshape(-1, block.shape[-1])
 
 
-def local_call(body, out_shape, role, *operands, flops=0, steps=None, blocks=None):
+def local_call(body, out_shape, role, *operands, flops=0, steps=None, blocks=None, out_blocks=None, scratch=()):
     moved = sum(o.size * o.dtype.itemsize for o in operands)
-    moved += sum(o.size * o.dtype.itemsize for o in jax.tree.leaves(out_shape))
+    moved += sum(math.prod(o.shape) * o.dtype.itemsize for o in jax.tree.leaves(out_shape))
     whole = pl.BlockSpec(memory_space=pltpu.VMEM)
     if steps is None:
         grid, in_blocks = (), [whole] * len(operands)
-        out_blocks = jax.tree.map(lambda _: whole, out_shape)
+        out_blocks = out_blocks or jax.tree.map(lambda _: whole, out_shape)
     else:
         grid, in_blocks, out_blocks = (steps,), blocks[0], blocks[1]
     return pl.pallas_call(
@@ -94,7 +95,8 @@
         out_shape=out_shape,
         in_specs=[pl.BlockSpec(memory_space=pltpu.SMEM)] + in_blocks,
         out_specs=out_blocks,
-        compiler_params=pltpu.CompilerParams(vmem_limit_bytes=24 * 1024 * 1024),
+        scratch_shapes=list(scratch),
+        compiler_params=pltpu.CompilerParams(vmem_limit_bytes=14 * 1024 * 1024),
         cost_estimate=pl.CostEstimate(flops=flops, bytes_accessed=moved, transcendentals=0),
     )(role, *operands)
 
@@ -111,45 +113,48 @@
     return high, (value - high.astype(f32)).astype(bf16)
 
 
-def partial_body(role, mine, in_inverse, out_inverse, out):
+def partial_body(role, mine, in_inverse, out_inverse, out, ready, sems):
     deep = out_inverse.shape[1] // CORES
 
+    def send(i):
+        return pltpu.make_async_copy(ready.at[i], out.at[i], sems.at[i])
+
     @pl.when(role[0] == 0)
     def _():
         inverse = jnp.concatenate([in_inverse[0], in_inverse[1]], axis=1)
-        high, low = high_low(dot(flat(mine[0, :, 0]), inverse, by_cols))
-        out[0, 0] = high
-        out[0, 1] = low
+
+        @pl.loop(0, SIDE)
+        def _(i):
+            high, low = high_low(dot(flat(mine[i, :, 0]), inverse, by_cols))
+            ready[i, 0] = high
+            ready[i, 1] = low
+            send(i).start()
 
     @pl.when(role[0] == 1)
     def _():
-        near, far = flat(mine[0, :, 0]), flat(mine[0, :, 1])
-        for half in range(CORES):
-            part = dot(near, out_inverse[half, :deep], plain)
-            part = part + dot(far, out_inverse[half, deep:], plain)
-            out[0, half] = part.astype(bf16)
-
-
-def resum_body(role, parts, out):
-    rows = out.shape[2]
+        @pl.loop(0, SIDE)
+        def _(i):
+            near, far = flat(mine[i, :, 0]), flat(mine[i, :, 1])
+            for half in range(CORES):
+                part = dot(near, out_inverse[half, :deep], plain)
+                part = part + dot(far, out_inverse[half, deep:], plain)
+                ready[i, half] = part.astype(bf16)
+            send(i).start()
 
     @pl.loop(0, SIDE)
     def _(i):
-        at = pl.ds(pl.multiple_of(i * rows, rows), rows)
-        totals = [
-            sum(parts[k, half, at, :].astype(f32) for k in range(SIDE)) for half in range(CORES)
-        ]
-
-        @pl.when(role[0] == 0)
-        def _():
-            high, low = high_low(totals[0] + totals[1])
-            out[i, 0] = high
-            out[i, 1] = low
-
-        @pl.when(role[0] == 1)
-        def _():
-            out[i, 0] = totals[0].astype(bf16)
-            out[i, 1] = totals[1].astype(bf16)
+        send(i).wait()
+
+
+def resum(first, parts):
+    total = jnp.sum(parts.astype(f32), axis=0)
+    whole = total[0] + total[1]
+    high = lax.reduce_precision(whole, exponent_bits=8, mantissa_bits=7)
+    parts = [
+        jnp.where(first, high, total[0]).astype(bf16),
+        jnp.where(first, whole - high, total[1]).astype(bf16),
+    ]
+    return jnp.stack([part.reshape(SIDE, -1, part.shape[1]) for part in parts], axis=1)
 
 
 def finish_body(role, parts, out):
@@ -232,7 +237,6 @@
     grads_pair, layer_inputs = tied((grads_pair, layer_inputs))
     input_pair = lax.all_gather(layer_inputs, "core", axis=1, tiled=True)
     inputs_moved = lax.ppermute(input_pair, ALL, swap_pairs())
-
     block = jnp.where(first, jnp.stack([input_pair, grads_pair[0]]), grads_moved)
     block = gather(block, out_z)
     block, late, inputs_moved, input_inverse, output_inverse = tied(
@@ -244,32 +248,23 @@
 
     part = local_call(
         partial_body,
-        jax.ShapeDtypeStruct((SIDE, CORES, SIDE * rows, wide), bf16),
+        pltpu.HBM((SIDE, CORES, SIDE * rows, wide), bf16),
         role,
         mine,
         in_inverse,
         out_inverse,
         flops=2 * tokens * 4 * wide * wide,
-        steps=SIDE,
-        blocks=(
-            [
-                block_at((1, SIDE, CORES, rows, wide), 0),
-                block_at(in_inverse.shape, None),
-                block_at(out_inverse.shape, None),
-            ],
-            block_at((1, CORES, SIDE * rows, wide), 0),
-        ),
-    )
-    part, late, inputs_moved = tied((part, late, inputs_moved))
+        out_blocks=pl.BlockSpec(memory_space=pltpu.HBM),
+        scratch=[
+            pltpu.VMEM((SIDE, CORES, SIDE * rows, wide), bf16),
+            pltpu.SemaphoreType.DMA((SIDE,)),
+        ],
+    )
+    part, late = tied((part, late))
     late = gather(jnp.where(first, late, inputs_moved), out_z)
     part = exchange(part, back_xy)
     part, late = tied((part, late))
-    part = local_call(
-        resum_body,
-        jax.ShapeDtypeStruct((SIDE, CORES, rows, wide), bf16),
-        role,
-        part,
-    )
+    part = resum(first, part)
     part, late = tied((part, late))
     part = exchange(part, back_z)
     left = lax.ppermute(late, ALL, ring_pairs(1))
@@ -278,14 +273,14 @@
     ahead = lax.ppermute(left[:span], ALL, ring_pairs(1))
     behind = lax.ppermute(right[span:], ALL, ring_pairs(-1))
     late = jnp.stack([late, left, jnp.concatenate([ahead, behind]), right])
+    late, mine = tied((late, mine))
+    their, their_late = core_swap(mine), core_swap(late)
     part, late = tied((part, late))
     mixed = local_call(
         finish_body, jax.ShapeDtypeStruct((CORES, rows, wide), bf16), role, part
     )
     mixed = gather(mixed, back_z)
-    mixed, mine, late = tied((mixed, mine, late))
     mixed = gather_direct(mixed, back_xy)
-    their, their_late = core_swap(mine), core_swap(late)
     input_running, output_running = local_call(
         running_body,
         (

time: 175 us -> 174 us (level)
  blocking collectives: 74.8 us -> 71 us
  other arithmetic: 0.27 us -> 3.25 us
  Pallas kernels: 11.4 us -> 9.41 us
    all_gather x3, blocking collectives: 59.9 us -> 56.2 us  [gather(): lax.all_gather(block, ALL, axis_index_groups=groups, axis=0, tiled=False)]
    reduce_sum x0 -> x1, other arithmetic: none -> 2.02 us  [resum(): total = jnp.sum(parts.astype(f32), axis=0)]
    pallas_call x5 -> x4, Pallas kernels: 11.4 us -> 9.41 us  [local_call(): pl.pallas_call(body, grid=grid, out_shape=out_shape, in_specs=[pl.BlockSp...]
  transfers between devices with their start and end apart: 13 -> 13, of which waited for: 9 -> 8; matrix products, arithmetic and copies ran while one was open for 2% -> 2% of each run, Pallas kernels for 2% -> 3%
where the time goes in v4:
time: 174 us; the launch traced here: 172 us
  blocking collectives  71 us (41%)
  starting transfers between devices  51.3 us (29%)
  waiting for transfers between devices  28.8 us (17%)
  Pallas kernels  9.41 us (5%)
  local copies, waits for them, and re-layouts  7.4 us (4%)
  other arithmetic  3.25 us (2%)
    all_gather x3, blocking collectives, gather(): lax.all_gather(block, ALL, axis_index_groups=groups, axis=0, tiled=False)  56.2 us
    all_to_all x4, starting transfers between devices, exchange(): return lax.all_to_all(parts, ALL, 0, 0, axis_index_groups=groups)  27.5 us
    all_to_all x4, waiting for transfers between devices, exchange(): return lax.all_to_all(parts, ALL, 0, 0, axis_index_groups=groups)  21.5 us
    ppermute x3, starting transfers between devices, core_swap(): return lax.ppermute(block, 'core', [(0, 1), (1, 0)])  9.56 us
    pallas_call x4, Pallas kernels, local_call(): pl.pallas_call(body, grid=grid, out_shape=out_shape, in_specs=[pl.BlockSp...  9.41 us
    all_gather x1, blocking collectives, per_device(): grads_pair = lax.all_gather(output_grads, 'core', axis=0, tiled=False)  8.64 us
    ppermute x1, starting transfers between devices, per_device(): behind = lax.ppermute(right[span:], ALL, ring_pairs(-1))  4.57 us
    ppermute x1, starting transfers between devices, per_device(): right = lax.ppermute(late, ALL, ring_pairs(-1))  4.3 us
  transfers between devices with their start and end apart: 13, of which 8 were waited for; matrix products, arithmetic and copies ran while one was open for 2% of the time, Pallas kernels for 3%

profile of v4, /device:TPU:1, one launch (start us, length us, event | category | flops | bytes accessed | tf_op | source)
XLA Modules:
  0.0 172.1 jit_solution(16099694987289274266)
XLA Ops:
  0.6 8.6 %all-gather = bf16[256,256]{1,0:T(8,128)(2,1)S(1)} all-gather(bf16[128,256]{1,0:T(8,128)(2,1)} %param.7), channel_id=2, replica_groups=mesh['x'=4,'zh'=4,'y'=4,'zl'=4,'core'=2] {'core'}, dimensions={0}, use_global_device_ids=true | all-gather | bytes 196608 | tf_op jit(solution)/shard_map/all_gather | solution.py:235
  9.9 2.1 %all_gather.41 = bf16[128,256]{1,0:T(8,128)(2,1)S(1)} all-gather(bf16[128,128]{1,0:T(8,128)(2,1)} %param.6), channel_id=1, replica_groups=mesh['x'=4,'zh'=4,'y'=4,'zl'=4,'core'=2] {'core'}, dimensions={1}, use_global_device_ids=true | all-gather | bytes 98304 | tf_op jit(solution)/shard_map/all_gather | solution.py:238
  12.8 25.8 %all-gather.1 = bf16[8,128,256]{2,1,0:T(8,128)(2,1)S(1)} all-gather(bf16[2,128,256]{2,1,0:T(8,128)(2,1)S(1)} %maximum_select_fusion), channel_id=3, replica_groups={{0,32,64,96},{2,34,66,98},{4,36,68,100},{6,38,70,102},{8,40,72,104},{10..., dimensions={0}, use_global_device_ids=true | all-gather | bytes 655360 | tf_op jit(solution)/shard_map/all_gather | solution.py:60
  40.2 7.7 %all-to-all-start = ((bf16[4,4,2,128,256]{4,3,2,1,0:T(8,128)(2,1)}), bf16[4,4,2,128,256]{4,3,2,1,0:T(8,128)(2,1)S(1)}, u32[]{:S(2)}, u32[]{:S(2)}) async-start(bf16[4,4,2,128,256]{4,3,2,1,0:T(8,128)(2,1)} %broadcast_in_dim.4), calls=%async_computation | async-start | bytes 4194304 | tf_op jit(solution)/shard_map/all_to_all | solution.py:64
  49.7 2.2 %all-gather.3 = bf16[1024,256]{1,0:T(8,128)(2,1)S(1)} all-gather(bf16[512,256]{1,0:T(8,128)(2,1)S(1)} %copy-done.2), channel_id=5, replica_groups=mesh['x'=4,'zh'=4,'y'=4,'zl'=4,'core'=2] {'core'}, dimensions={0}, use_global_device_ids=true | all-gather | bytes 786432 | tf_op jit(solution)/shard_map/all_gather | solution.py:247
  51.9 11.3 %all-to-all-done.mine = bf16[4,4,2,128,256]{4,3,2,1,0:T(8,128)(2,1)S(1)} async-done(((bf16[4,4,2,128,256]{4,3,2,1,0:T(8,128)(2,1)}), bf16[4,4,2,128,256]{4,3,2,1,0:T(8,128)(2,1)S(1)}, u32[]{:S(2)}, u32[]{:S(2)}) %all-to-all-start) | async-done | bytes 2097184 | tf_op jit(solution)/shard_map/all_to_all | solution.py:64
  63.2 2.6 %shard_map.85 = bf16[4,2,512,256]{3,2,1,0:T(8,128)(2,1)} custom-call(s32[1]{0:T(128)} %bitcast.role, bf16[4,4,2,128,256]{4,3,2,1,0:T(8,128)(2,1)S(1)} %all-to-all-done.mine, bf16[2,256,128]{2,1,0:T(8,128)(2,1)S(1)} %bitcast.22, bf16[2,512,256]{2,1,0:T(8,128)(2,1)S(1)} %bitcast.21), custom_call_target="tpu_custom_call" | custom-call | flops 1073741824 | bytes 4849664 | tf_op jit(solution)/shard_map/pallas_call | solution.py:92
  65.8 4.5 %all-to-all-start.1 = ((bf16[4,2,512,256]{3,2,1,0:T(8,128)(2,1)}), bf16[4,2,512,256]{3,2,1,0:T(8,128)(2,1)}, u32[]{:S(2)}, u32[]{:S(2)}) async-start(bf16[4,2,512,256]{3,2,1,0:T(8,128)(2,1)} %shard_map.85), calls=%async_computation.1 | async-start | bytes 4194304 | tf_op jit(solution)/shard_map/all_to_all | solution.py:64
  70.3 11.4 %all-gather.4 = bf16[512,256]{1,0:T(8,128)(2,1)S(1)} all-gather(bf16[128,256]{1,0:T(8,128)(2,1)S(1)} %broadcast_select_fusion), channel_id=6, replica_groups={{0,32,64,96},{2,34,66,98},{4,36,68,100},{6,38,70,102},{8,40,72,104},{10..., dimensions={0}, use_global_device_ids=true | all-gather | bytes 327680 | tf_op jit(solution)/shard_map/all_gather | solution.py:60
  81.7 4.0 %all-to-all-done.1 = bf16[4,2,512,256]{3,2,1,0:T(8,128)(2,1)} async-done(((bf16[4,2,512,256]{3,2,1,0:T(8,128)(2,1)}), bf16[4,2,512,256]{3,2,1,0:T(8,128)(2,1)}, u32[]{:S(2)}, u32[]{:S(2)}) %all-to-all-start.1) | async-done | bytes 2097184 | tf_op jit(solution)/shard_map/all_to_all | solution.py:64
  85.7 2.0 %convert_reduce_fusion = f32[2,512,256]{2,1,0:T(8,128)S(1)} fusion(bf16[4,2,512,256]{3,2,1,0:T(8,128)(2,1)} %all-to-all-done.1), kind=kLoop, calls=%fused_computation | loop fusion | flops 1835008 | bytes 3145728 | tf_op jit(solution)/shard_map/reduce_sum | solution.py:150
  88.8 10.8 %all-to-all-start.2 = ((bf16[4,2,128,256]{3,2,1,0:T(8,128)(2,1)}), bf16[4,2,128,256]{3,2,1,0:T(8,128)(2,1)}, u32[]{:S(2)}, u32[]{:S(2)}) async-start(bf16[4,2,128,256]{3,2,1,0:T(8,128)(2,1)} %pad_maximum_fusion.1), calls=%async_computation.2 | async-start | bytes 1048576 | tf_op jit(solution)/shard_map/all_to_all | solution.py:64
  99.6 2.2 %collective-permute-start.2 = (bf16[4,128,256]{2,1,0:T(8,128)(2,1)S(1)}, bf16[4,128,256]{2,1,0:T(8,128)(2,1)S(1)}, u32[]{:S(2)}, u32[]{:S(2)}) collective-permute-start(bf16[4,128,256]{2,1,0:T(8,128)(2,1)S(1)} %bitcast.27), channel_id=1, source_target_pairs={{0,128},{128,256},{256,384},{384,0},{2,130},{130,258},{258,386},{3... | collective-permute-start | bytes 786440 | tf_op jit(solution)/shard_map/ppermute | solution.py:270
  101.7 4.3 %collective-permute-start.4 = (bf16[4,128,256]{2,1,0:T(8,128)(2,1)S(1)}, bf16[4,128,256]{2,1,0:T(8,128)(2,1)S(1)}, u32[]{:S(2)}, u32[]{:S(2)}) collective-permute-start(bf16[4,128,256]{2,1,0:T(8,128)(2,1)S(1)} %bitcast.28), channel_id=1, source_target_pairs={{0,384},{128,0},{256,128},{384,256},{2,386},{130,2},{258,130},{386... | collective-permute-start | bytes 786440 | tf_op jit(solution)/shard_map/ppermute | solution.py:271
  106.0 2.2 %collective-permute-done.2 = bf16[4,128,256]{2,1,0:T(8,128)(2,1)S(1)} collective-permute-done((bf16[4,128,256]{2,1,0:T(8,128)(2,1)S(1)}, bf16[4,128,256]{2,1,0:T(8,128)(2,1)S(1)}, u32[]{:S(2)}, u32[]{:S(2)}) %collective-permute-start.2) | collective-permute-done | bytes 262176 | tf_op jit(solution)/shard_map/ppermute | solution.py:270
  110.2 4.6 %collective-permute-start.5 = (bf16[2,128,256]{2,1,0:T(8,128)(2,1)S(1)}, bf16[2,128,256]{2,1,0:T(8,128)(2,1)S(1)}, u32[]{:S(2)}, u32[]{:S(2)}) collective-permute-start(bf16[2,128,256]{2,1,0:T(8,128)(2,1)S(1)} %slice.33), channel_id=1, source_target_pairs={{0,384},{128,0},{256,128},{384,256},{2,386},{130,2},{258,130},{386... | collective-permute-start | bytes 393224 | tf_op jit(solution)/shard_map/ppermute | solution.py:274
  116.9 4.6 %collective-permute-start.6 = (bf16[4,4,2,128,256]{4,3,2,1,0:T(8,128)(2,1)S(1)}, bf16[4,4,2,128,256]{4,3,2,1,0:T(8,128)(2,1)}, u32[]{:S(2)}, u32[]{:S(2)}) collective-permute-start(bf16[4,4,2,128,256]{4,3,2,1,0:T(8,128)(2,1)S(1)} %all-to-all-done.mine), channel_id=1, source_target_pairs={{0,1},{1,0},{2,3},{3,2},{4,5},{5,4},{6,7},{7,6},{8,9},{9,8},{10,11... | collective-permute-start | bytes 6291464 | tf_op jit(solution)/shard_map/ppermute | solution.py:72
  122.7 19.0 %all-gather.5 = bf16[8,128,256]{2,1,0:T(8,128)(2,1)S(1)} all-gather(bf16[2,128,256]{2,1,0:T(8,128)(2,1)S(1)} %shard_map.86), channel_id=7, replica_groups={{0,2,4,6},{8,10,12,14},{16,18,20,22},{24,26,28,30},{32,34,36,38},{40,42..., dimensions={0}, use_global_device_ids=true | all-gather | bytes 655360 | tf_op jit(solution)/shard_map/all_gather | solution.py:60
  143.3 4.6 %all-to-all-start.3 = ((bf16[4,4,2,128,256]{4,3,1,2,0:T(8,128)(2,1)}), bf16[4,4,2,128,256]{4,3,1,2,0:T(8,128)(2,1)}, u32[]{:S(2)}, u32[]{:S(2)}) async-start(bf16[4,4,2,128,256]{4,3,1,2,0:T(8,128)(2,1)} %broadcast_in_dim.5), calls=%async_computation.3 | async-start | bytes 4194304 | tf_op jit(solution)/shard_map/all_to_all | solution.py:64
  147.9 2.0 %collective-permute-start.7 = (bf16[4,4,128,256]{3,2,1,0:T(8,128)(2,1)S(1)}, bf16[4,4,128,256]{3,2,1,0:T(8,128)(2,1)}, u32[]{:S(2)}, u32[]{:S(2)}) collective-permute-start(bf16[4,4,128,256]{3,2,1,0:T(8,128)(2,1)S(1)} %pad_maximum_fusion.late), channel_id=1, source_target_pairs={{0,1},{1,0},{2,3},{3,2},{4,5},{5,4},{6,7},{7,6},{8,9},{9,8},{10,11... | collective-permute-start | bytes 3145736 | tf_op jit(solution)/shard_map/ppermute | solution.py:72
  150.0 2.6 %collective-permute-done.7.their_late = bf16[4,4,128,256]{3,2,1,0:T(8,128)(2,1)} collective-permute-done((bf16[4,4,128,256]{3,2,1,0:T(8,128)(2,1)S(1)}, bf16[4,4,128,256]{3,2,1,0:T(8,128)(2,1)}, u32[]{:S(2)}, u32[]{:S(2)}) %collective-permute-start.7) | collective-permute-done | bytes 1048608 | tf_op jit(solution)/shard_map/ppermute | solution.py:72
  153.7 3.8 %shard_map.87 = (f32[256,128]{1,0:T(8,128)}, f32[512,256]{1,0:T(8,128)}) custom-call(s32[3]{0:T(128)S(1)} %pad_add_fusion.role, bf16[4,4,2,128,256]{4,3,2,1,0:T(8,128)(2,1)S(1)} %all-to-all-done.mine, bf16[4,4,2,128,256]{4,3,2,1,0:T(8,128)(2,1)} %collective-permute-done.6.their, bf16[4,4,128,256]{3,2,1,0:T(8,128)(2,1)S(1)} %pad_maximum_fusion.late, ...), custom_call_target="tpu_custom_call" | custom-call | flops 671088640 | bytes 7602176 | tf_op jit(solution)/shard_map/pallas_call | solution.py:92
  157.4 6.2 %all-to-all-done.3 = bf16[4,4,2,128,256]{4,3,1,2,0:T(8,128)(2,1)} async-done(((bf16[4,4,2,128,256]{4,3,1,2,0:T(8,128)(2,1)}), bf16[4,4,2,128,256]{4,3,1,2,0:T(8,128)(2,1)}, u32[]{:S(2)}, u32[]{:S(2)}) %all-to-all-start.3) | async-done | bytes 2097184 | tf_op jit(solution)/shard_map/all_to_all | solution.py:64
  165.0 2.9 %collective-permute-start.8 = (bf16[4,4,128,256]{3,2,1,0:T(8,128)(2,1)S(1)}, bf16[4,4,128,256]{3,2,1,0:T(8,128)(2,1)S(1)}, u32[]{:S(2)}, u32[]{:S(2)}) collective-permute-start(bf16[4,4,128,256]{3,2,1,0:T(8,128)(2,1)S(1)} %slice_bitcast_fusion), channel_id=1, source_target_pairs={{0,1},{1,0},{2,3},{3,2},{4,5},{5,4},{6,7},{7,6},{8,9},{9,8},{10,11... | collective-permute-start | bytes 3145736 | tf_op jit(solution)/shard_map/ppermute | solution.py:72
  (38 shorter events, 19.3 us)
Async XLA Ops:
  9.3 3.5 %collective-permute-start = (bf16[2,128,256]{2,1,0:T(8,128)(2,1)S(1)}, bf16[2,128,256]{2,1,0:T(8,128)(2,1)S(1)}, u32[]{:S(2)}, u32[]{:S(2)}) collective-permute-start(bf16[2,128,256]{2,1,0:T(8,128)(2,1)S(1)} %bitcast.32), channel_id=1, source_target_pairs={{0,0},{1,1},{2,2},{3,33},{4,4},{5,65},{6,6},{7,97},{8,8},{9,129},{... | collective-permute-start | bytes 393224 | tf_op jit(solution)/shard_map/ppermute | solution.py:236
  12.1 26.5 %collective-permute-start.1 = (bf16[128,256]{1,0:T(8,128)(2,1)S(1)}, bf16[128,256]{1,0:T(8,128)(2,1)S(1)}, u32[]{:S(2)}, u32[]{:S(2)}) collective-permute-start(bf16[128,256]{1,0:T(8,128)(2,1)S(1)} %all_gather.41), channel_id=1, source_target_pairs={{0,0},{1,1},{2,2},{3,33},{4,4},{5,65},{6,6},{7,97},{8,8},{9,129},{... | collective-permute-start | bytes 196616 | tf_op jit(solution)/shard_map/ppermute | solution.py:239
  40.2 7.7 %copy-start.3 = (bf16[256,128]{1,0:T(8,128)(2,1)S(1)}, bf16[256,128]{1,0:T(8,128)(2,1)}, u32[]{:S(2)}) copy-start(bf16[256,128]{1,0:T(8,128)(2,1)} %param.10) | copy-start | bytes 196612
  40.2 9.6 %copy-start.2 = (bf16[512,256]{1,0:T(8,128)(2,1)S(1)}, bf16[512,256]{1,0:T(8,128)(2,1)}, u32[]{:S(2)}) copy-start(bf16[512,256]{1,0:T(8,128)(2,1)} %param.11) | copy-start | bytes 786436
  40.2 23.0 %all-to-all-start = ((bf16[4,4,2,128,256]{4,3,2,1,0:T(8,128)(2,1)}), bf16[4,4,2,128,256]{4,3,2,1,0:T(8,128)(2,1)S(1)}, u32[]{:S(2)}, u32[]{:S(2)}) async-start(bf16[4,4,2,128,256]{4,3,2,1,0:T(8,128)(2,1)} %broadcast_in_dim.4), calls=%async_computation | async-start | bytes 4194304 | tf_op jit(solution)/shard_map/all_to_all | solution.py:64
  65.8 19.9 %all-to-all-start.1 = ((bf16[4,2,512,256]{3,2,1,0:T(8,128)(2,1)}), bf16[4,2,512,256]{3,2,1,0:T(8,128)(2,1)}, u32[]{:S(2)}, u32[]{:S(2)}) async-start(bf16[4,2,512,256]{3,2,1,0:T(8,128)(2,1)} %shard_map.85), calls=%async_computation.1 | async-start | bytes 4194304 | tf_op jit(solution)/shard_map/all_to_all | solution.py:64
  88.8 32.8 %all-to-all-start.2 = ((bf16[4,2,128,256]{3,2,1,0:T(8,128)(2,1)}), bf16[4,2,128,256]{3,2,1,0:T(8,128)(2,1)}, u32[]{:S(2)}, u32[]{:S(2)}) async-start(bf16[4,2,128,256]{3,2,1,0:T(8,128)(2,1)} %pad_maximum_fusion.1), calls=%async_computation.2 | async-start | bytes 1048576 | tf_op jit(solution)/shard_map/all_to_all | solution.py:64
  99.6 8.7 %collective-permute-start.2 = (bf16[4,128,256]{2,1,0:T(8,128)(2,1)S(1)}, bf16[4,128,256]{2,1,0:T(8,128)(2,1)S(1)}, u32[]{:S(2)}, u32[]{:S(2)}) collective-permute-start(bf16[4,128,256]{2,1,0:T(8,128)(2,1)S(1)} %bitcast.27), channel_id=1, source_target_pairs={{0,128},{128,256},{256,384},{384,0},{2,130},{130,258},{258,386},{3... | collective-permute-start | bytes 786440 | tf_op jit(solution)/shard_map/ppermute | solution.py:270
  101.7 8.5 %collective-permute-start.4 = (bf16[4,128,256]{2,1,0:T(8,128)(2,1)S(1)}, bf16[4,128,256]{2,1,0:T(8,128)(2,1)S(1)}, u32[]{:S(2)}, u32[]{:S(2)}) collective-permute-start(bf16[4,128,256]{2,1,0:T(8,128)(2,1)S(1)} %bitcast.28), channel_id=1, source_target_pairs={{0,384},{128,0},{256,128},{384,256},{2,386},{130,2},{258,130},{386... | collective-permute-start | bytes 786440 | tf_op jit(solution)/shard_map/ppermute | solution.py:271
  108.3 7.2 %collective-permute-start.3 = (bf16[2,128,256]{2,1,0:T(8,128)(2,1)S(1)}, bf16[2,128,256]{2,1,0:T(8,128)(2,1)S(1)}, u32[]{:S(2)}, u32[]{:S(2)}) collective-permute-start(bf16[2,128,256]{2,1,0:T(8,128)(2,1)S(1)} %slice.32), channel_id=1, source_target_pairs={{0,128},{128,256},{256,384},{384,0},{2,130},{130,258},{258,386},{3... | collective-permute-start | bytes 393224 | tf_op jit(solution)/shard_map/ppermute | solution.py:273
  110.2 6.5 %collective-permute-start.5 = (bf16[2,128,256]{2,1,0:T(8,128)(2,1)S(1)}, bf16[2,128,256]{2,1,0:T(8,128)(2,1)S(1)}, u32[]{:S(2)}, u32[]{:S(2)}) collective-permute-start(bf16[2,128,256]{2,1,0:T(8,128)(2,1)S(1)} %slice.33), channel_id=1, source_target_pairs={{0,384},{128,0},{256,128},{384,256},{2,386},{130,2},{258,130},{386... | collective-permute-start | bytes 393224 | tf_op jit(solution)/shard_map/ppermute | solution.py:274
  116.9 35.7 %collective-permute-start.6 = (bf16[4,4,2,128,256]{4,3,2,1,0:T(8,128)(2,1)S(1)}, bf16[4,4,2,128,256]{4,3,2,1,0:T(8,128)(2,1)}, u32[]{:S(2)}, u32[]{:S(2)}) collective-permute-start(bf16[4,4,2,128,256]{4,3,2,1,0:T(8,128)(2,1)S(1)} %all-to-all-done.mine), channel_id=1, source_target_pairs={{0,1},{1,0},{2,3},{3,2},{4,5},{5,4},{6,7},{7,6},{8,9},{9,8},{10,11... | collective-permute-start | bytes 6291464 | tf_op jit(solution)/shard_map/ppermute | solution.py:72
  143.3 9.3 %copy-start.1 = (f32[256,128]{1,0:T(8,128)S(1)}, f32[256,128]{1,0:T(8,128)}, u32[]{:S(2)}) copy-start(f32[256,128]{1,0:T(8,128)} %in_old.1) | copy-start | bytes 393220
  143.3 20.3 %all-to-all-start.3 = ((bf16[4,4,2,128,256]{4,3,1,2,0:T(8,128)(2,1)}), bf16[4,4,2,128,256]{4,3,1,2,0:T(8,128)(2,1)}, u32[]{:S(2)}, u32[]{:S(2)}) async-start(bf16[4,4,2,128,256]{4,3,1,2,0:T(8,128)(2,1)} %broadcast_in_dim.5), calls=%async_computation.3 | async-start | bytes 4194304 | tf_op jit(solution)/shard_map/all_to_all | solution.py:64
  147.9 4.7 %collective-permute-start.7 = (bf16[4,4,128,256]{3,2,1,0:T(8,128)(2,1)S(1)}, bf16[4,4,128,256]{3,2,1,0:T(8,128)(2,1)}, u32[]{:S(2)}, u32[]{:S(2)}) collective-permute-start(bf16[4,4,128,256]{3,2,1,0:T(8,128)(2,1)S(1)} %pad_maximum_fusion.late), channel_id=1, source_target_pairs={{0,1},{1,0},{2,3},{3,2},{4,5},{5,4},{6,7},{7,6},{8,9},{9,8},{10,11... | collective-permute-start | bytes 3145736 | tf_op jit(solution)/shard_map/ppermute | solution.py:72
  152.6 1.0 copy-start
  165.0 5.2 %collective-permute-start.8 = (bf16[4,4,128,256]{3,2,1,0:T(8,128)(2,1)S(1)}, bf16[4,4,128,256]{3,2,1,0:T(8,128)(2,1)S(1)}, u32[]{:S(2)}, u32[]{:S(2)}) collective-permute-start(bf16[4,4,128,256]{3,2,1,0:T(8,128)(2,1)S(1)} %slice_bitcast_fusion), channel_id=1, source_target_pairs={{0,1},{1,0},{2,3},{3,2},{4,5},{5,4},{6,7},{7,6},{8,9},{9,8},{10,11... | collective-permute-start | bytes 3145736 | tf_op jit(solution)/shard_map/ppermute | solution.py:72

commit v5 on v4

--- a/solution.py
+++ b/solution.py
@@ -260,7 +260,8 @@
             pltpu.SemaphoreType.DMA((SIDE,)),
         ],
     )
-    part, late = tied((part, late))
+    part, late, mine = tied((part, late, mine))
+    their = core_swap(mine)
     late = gather(jnp.where(first, late, inputs_moved), out_z)
     part = exchange(part, back_xy)
     part, late = tied((part, late))
@@ -273,8 +274,7 @@
     ahead = lax.ppermute(left[:span], ALL, ring_pairs(1))
     behind = lax.ppermute(right[span:], ALL, ring_pairs(-1))
     late = jnp.stack([late, left, jnp.concatenate([ahead, behind]), right])
-    late, mine = tied((late, mine))
-    their, their_late = core_swap(mine), core_swap(late)
+    their_late = core_swap(late)
     part, late = tied((part, late))
     mixed = local_call(
         finish_body, jax.ShapeDtypeStruct((CORES, rows, wide), bf16), role, part

time: 174 us -> 172 us (0.989)
  starting transfers between devices: 51.3 us -> 49 us
  blocking collectives: 71 us -> 73 us
    ppermute x3, starting transfers between devices: 9.56 us -> 7.17 us  [core_swap(): return lax.ppermute(block, 'core', [(0, 1), (1, 0)])]
    ppermute x1, waiting for transfers between devices: 2.22 us -> 0.01 us  [per_device(): left = lax.ppermute(late, ALL, ring_pairs(1))]
    all_gather x3, blocking collectives: 56.2 us -> 58.2 us  [gather(): lax.all_gather(block, ALL, axis_index_groups=groups, axis=0, tiled=False)]
    ppermute x1, starting transfers between devices: 1.92 us -> 3.74 us  [per_device(): ahead = lax.ppermute(left[:span], ALL, ring_pairs(1))]
    ppermute x1, starting transfers between devices: 4.57 us -> 2.83 us  [per_device(): behind = lax.ppermute(right[span:], ALL, ring_pairs(-1))]
  transfers between devices with their start and end apart: 13 -> 13, of which waited for: 8 -> 7; matrix products, arithmetic and copies ran while one was open for 2% -> 2% of each run, Pallas kernels for 3% -> 3%
where the time goes in v5:
time: 172 us; the launch traced here: 171 us
  blocking collectives  73 us (42%)
  starting transfers between devices  49 us (28%)
  waiting for transfers between devices  27.7 us (16%)
  Pallas kernels  9.4 us (5%)
  local copies, waits for them, and re-layouts  7.4 us (4%)
  other arithmetic  3.25 us (2%)
    all_gather x3, blocking collectives, gather(): lax.all_gather(block, ALL, axis_index_groups=groups, axis=0, tiled=False)  58.2 us
    all_to_all x4, starting transfers between devices, exchange(): return lax.all_to_all(parts, ALL, 0, 0, axis_index_groups=groups)  27.5 us
    all_to_all x4, waiting for transfers between devices, exchange(): return lax.all_to_all(parts, ALL, 0, 0, axis_index_groups=groups)  21.2 us
    pallas_call x4, Pallas kernels, local_call(): pl.pallas_call(body, grid=grid, out_shape=out_shape, in_specs=[pl.BlockSp...  9.4 us
    all_gather x1, blocking collectives, per_device(): grads_pair = lax.all_gather(output_grads, 'core', axis=0, tiled=False)  8.64 us
    ppermute x3, starting transfers between devices, core_swap(): return lax.ppermute(block, 'core', [(0, 1), (1, 0)])  7.17 us
    ppermute x1, starting transfers between devices, per_device(): right = lax.ppermute(late, ALL, ring_pairs(-1))  4.3 us
    ppermute x1, starting transfers between devices, per_device(): ahead = lax.ppermute(left[:span], ALL, ring_pairs(1))  3.74 us
  transfers between devices with their start and end apart: 13, of which 7 were waited for; matrix products, arithmetic and copies ran while one was open for 2% of the time, Pallas kernels for 3%

profile of v5, /device:TPU:1, one launch (start us, length us, event | category | flops | bytes accessed | tf_op | source)
XLA Modules:
  0.0 170.6 jit_solution(668703734368243510)
XLA Ops:
  0.6 8.6 %all-gather = bf16[256,256]{1,0:T(8,128)(2,1)S(1)} all-gather(bf16[128,256]{1,0:T(8,128)(2,1)} %param.7), channel_id=2, replica_groups=mesh['x'=4,'zh'=4,'y'=4,'zl'=4,'core'=2] {'core'}, dimensions={0}, use_global_device_ids=true | all-gather | bytes 196608 | tf_op jit(solution)/shard_map/all_gather | solution.py:235
  9.9 2.1 %all_gather.41 = bf16[128,256]{1,0:T(8,128)(2,1)S(1)} all-gather(bf16[128,128]{1,0:T(8,128)(2,1)} %param.6), channel_id=1, replica_groups=mesh['x'=4,'zh'=4,'y'=4,'zl'=4,'core'=2] {'core'}, dimensions={1}, use_global_device_ids=true | all-gather | bytes 98304 | tf_op jit(solution)/shard_map/all_gather | solution.py:238
  12.8 25.8 %all-gather.1 = bf16[8,128,256]{2,1,0:T(8,128)(2,1)S(1)} all-gather(bf16[2,128,256]{2,1,0:T(8,128)(2,1)S(1)} %maximum_select_fusion), channel_id=3, replica_groups={{0,32,64,96},{2,34,66,98},{4,36,68,100},{6,38,70,102},{8,40,72,104},{10..., dimensions={0}, use_global_device_ids=true | all-gather | bytes 655360 | tf_op jit(solution)/shard_map/all_gather | solution.py:60
  40.2 7.7 %all-to-all-start = ((bf16[4,4,2,128,256]{4,3,2,1,0:T(8,128)(2,1)}), bf16[4,4,2,128,256]{4,3,2,1,0:T(8,128)(2,1)S(1)}, u32[]{:S(2)}, u32[]{:S(2)}) async-start(bf16[4,4,2,128,256]{4,3,2,1,0:T(8,128)(2,1)} %broadcast_in_dim.4), calls=%async_computation | async-start | bytes 4194304 | tf_op jit(solution)/shard_map/all_to_all | solution.py:64
  49.7 2.2 %all-gather.3 = bf16[1024,256]{1,0:T(8,128)(2,1)S(1)} all-gather(bf16[512,256]{1,0:T(8,128)(2,1)S(1)} %copy-done.2), channel_id=5, replica_groups=mesh['x'=4,'zh'=4,'y'=4,'zl'=4,'core'=2] {'core'}, dimensions={0}, use_global_device_ids=true | all-gather | bytes 786432 | tf_op jit(solution)/shard_map/all_gather | solution.py:247
  51.9 11.3 %all-to-all-done.mine = bf16[4,4,2,128,256]{4,3,2,1,0:T(8,128)(2,1)S(1)} async-done(((bf16[4,4,2,128,256]{4,3,2,1,0:T(8,128)(2,1)}), bf16[4,4,2,128,256]{4,3,2,1,0:T(8,128)(2,1)S(1)}, u32[]{:S(2)}, u32[]{:S(2)}) %all-to-all-start) | async-done | bytes 2097184 | tf_op jit(solution)/shard_map/all_to_all | solution.py:64
  63.2 2.6 %shard_map.85 = bf16[4,2,512,256]{3,2,1,0:T(8,128)(2,1)} custom-call(s32[1]{0:T(128)} %bitcast.role, bf16[4,4,2,128,256]{4,3,2,1,0:T(8,128)(2,1)S(1)} %all-to-all-done.mine, bf16[2,256,128]{2,1,0:T(8,128)(2,1)S(1)} %bitcast.22, bf16[2,512,256]{2,1,0:T(8,128)(2,1)S(1)} %bitcast.21), custom_call_target="tpu_custom_call" | custom-call | flops 1073741824 | bytes 4849664 | tf_op jit(solution)/shard_map/pallas_call | solution.py:92
  65.8 4.5 %all-to-all-start.1 = ((bf16[4,2,512,256]{3,2,1,0:T(8,128)(2,1)}), bf16[4,2,512,256]{3,2,1,0:T(8,128)(2,1)}, u32[]{:S(2)}, u32[]{:S(2)}) async-start(bf16[4,2,512,256]{3,2,1,0:T(8,128)(2,1)} %shard_map.85), calls=%async_computation.1 | async-start | bytes 4194304 | tf_op jit(solution)/shard_map/all_to_all | solution.py:64
  70.3 11.4 %all-gather.4 = bf16[512,256]{1,0:T(8,128)(2,1)S(1)} all-gather(bf16[128,256]{1,0:T(8,128)(2,1)S(1)} %broadcast_select_fusion), channel_id=6, replica_groups={{0,32,64,96},{2,34,66,98},{4,36,68,100},{6,38,70,102},{8,40,72,104},{10..., dimensions={0}, use_global_device_ids=true | all-gather | bytes 327680 | tf_op jit(solution)/shard_map/all_gather | solution.py:60
  81.7 4.0 %all-to-all-done.1 = bf16[4,2,512,256]{3,2,1,0:T(8,128)(2,1)} async-done(((bf16[4,2,512,256]{3,2,1,0:T(8,128)(2,1)}), bf16[4,2,512,256]{3,2,1,0:T(8,128)(2,1)}, u32[]{:S(2)}, u32[]{:S(2)}) %all-to-all-start.1) | async-done | bytes 2097184 | tf_op jit(solution)/shard_map/all_to_all | solution.py:64
  85.7 2.0 %convert_reduce_fusion = f32[2,512,256]{2,1,0:T(8,128)S(1)} fusion(bf16[4,2,512,256]{3,2,1,0:T(8,128)(2,1)} %all-to-all-done.1), kind=kLoop, calls=%fused_computation | loop fusion | flops 1835008 | bytes 3145728 | tf_op jit(solution)/shard_map/reduce_sum | solution.py:150
  88.8 10.8 %all-to-all-start.2 = ((bf16[4,2,128,256]{3,2,1,0:T(8,128)(2,1)}), bf16[4,2,128,256]{3,2,1,0:T(8,128)(2,1)}, u32[]{:S(2)}, u32[]{:S(2)}) async-start(bf16[4,2,128,256]{3,2,1,0:T(8,128)(2,1)} %pad_maximum_fusion.1), calls=%async_computation.2 | async-start | bytes 1048576 | tf_op jit(solution)/shard_map/all_to_all | solution.py:64
  99.6 2.2 %collective-permute-start.2 = (bf16[4,128,256]{2,1,0:T(8,128)(2,1)S(1)}, bf16[4,128,256]{2,1,0:T(8,128)(2,1)S(1)}, u32[]{:S(2)}, u32[]{:S(2)}) collective-permute-start(bf16[4,128,256]{2,1,0:T(8,128)(2,1)S(1)} %bitcast.27), channel_id=1, source_target_pairs={{0,128},{128,256},{256,384},{384,0},{2,130},{130,258},{258,386},{3... | collective-permute-start | bytes 786440 | tf_op jit(solution)/shard_map/ppermute | solution.py:271
  101.7 4.3 %collective-permute-start.4 = (bf16[4,128,256]{2,1,0:T(8,128)(2,1)S(1)}, bf16[4,128,256]{2,1,0:T(8,128)(2,1)S(1)}, u32[]{:S(2)}, u32[]{:S(2)}) collective-permute-start(bf16[4,128,256]{2,1,0:T(8,128)(2,1)S(1)} %bitcast.28), channel_id=1, source_target_pairs={{0,384},{128,0},{256,128},{384,256},{2,386},{130,2},{258,130},{386... | collective-permute-start | bytes 786440 | tf_op jit(solution)/shard_map/ppermute | solution.py:272
  106.0 3.3 %collective-permute-start.6 = (bf16[4,4,2,128,256]{4,3,2,1,0:T(8,128)(2,1)S(1)}, bf16[4,4,2,128,256]{4,3,2,1,0:T(8,128)(2,1)}, u32[]{:S(2)}, u32[]{:S(2)}) collective-permute-start(bf16[4,4,2,128,256]{4,3,2,1,0:T(8,128)(2,1)S(1)} %all-to-all-done.mine), channel_id=1, source_target_pairs={{0,1},{1,0},{2,3},{3,2},{4,5},{5,4},{6,7},{7,6},{8,9},{9,8},{10,11... | collective-permute-start | bytes 6291464 | tf_op jit(solution)/shard_map/ppermute | solution.py:72
  109.4 3.7 %collective-permute-start.3 = (bf16[2,128,256]{2,1,0:T(8,128)(2,1)S(1)}, bf16[2,128,256]{2,1,0:T(8,128)(2,1)S(1)}, u32[]{:S(2)}, u32[]{:S(2)}) collective-permute-start(bf16[2,128,256]{2,1,0:T(8,128)(2,1)S(1)} %slice.32), channel_id=1, source_target_pairs={{0,128},{128,256},{256,384},{384,0},{2,130},{130,258},{258,386},{3... | collective-permute-start | bytes 393224 | tf_op jit(solution)/shard_map/ppermute | solution.py:274
  113.2 2.8 %collective-permute-start.5 = (bf16[2,128,256]{2,1,0:T(8,128)(2,1)S(1)}, bf16[2,128,256]{2,1,0:T(8,128)(2,1)S(1)}, u32[]{:S(2)}, u32[]{:S(2)}) collective-permute-start(bf16[2,128,256]{2,1,0:T(8,128)(2,1)S(1)} %slice.33), channel_id=1, source_target_pairs={{0,384},{128,0},{256,128},{384,256},{2,386},{130,2},{258,130},{386... | collective-permute-start | bytes 393224 | tf_op jit(solution)/shard_map/ppermute | solution.py:275
  116.7 2.2 %collective-permute-done.5 = bf16[2,128,256]{2,1,0:T(8,128)(2,1)S(1)} collective-permute-done((bf16[2,128,256]{2,1,0:T(8,128)(2,1)S(1)}, bf16[2,128,256]{2,1,0:T(8,128)(2,1)S(1)}, u32[]{:S(2)}, u32[]{:S(2)}) %collective-permute-start.5) | collective-permute-done | bytes 131104 | tf_op jit(solution)/shard_map/ppermute | solution.py:275
  120.2 21.0 %all-gather.5 = bf16[8,128,256]{2,1,0:T(8,128)(2,1)S(1)} all-gather(bf16[2,128,256]{2,1,0:T(8,128)(2,1)S(1)} %shard_map.86), channel_id=7, replica_groups={{0,2,4,6},{8,10,12,14},{16,18,20,22},{24,26,28,30},{32,34,36,38},{40,42..., dimensions={0}, use_global_device_ids=true | all-gather | bytes 655360 | tf_op jit(solution)/shard_map/all_gather | solution.py:60
  142.8 4.6 %all-to-all-start.3 = ((bf16[4,4,2,128,256]{4,3,1,2,0:T(8,128)(2,1)}), bf16[4,4,2,128,256]{4,3,1,2,0:T(8,128)(2,1)}, u32[]{:S(2)}, u32[]{:S(2)}) async-start(bf16[4,4,2,128,256]{4,3,1,2,0:T(8,128)(2,1)} %broadcast_in_dim.5), calls=%async_computation.3 | async-start | bytes 4194304 | tf_op jit(solution)/shard_map/all_to_all | solution.py:64
  147.4 1.9 %collective-permute-start.7 = (bf16[4,4,128,256]{3,2,1,0:T(8,128)(2,1)S(1)}, bf16[4,4,128,256]{3,2,1,0:T(8,128)(2,1)}, u32[]{:S(2)}, u32[]{:S(2)}) collective-permute-start(bf16[4,4,128,256]{3,2,1,0:T(8,128)(2,1)S(1)} %pad_maximum_fusion.late), channel_id=1, source_target_pairs={{0,1},{1,0},{2,3},{3,2},{4,5},{5,4},{6,7},{7,6},{8,9},{9,8},{10,11... | collective-permute-start | bytes 3145736 | tf_op jit(solution)/shard_map/ppermute | solution.py:72
  149.5 2.7 %collective-permute-done.7.their_late = bf16[4,4,128,256]{3,2,1,0:T(8,128)(2,1)} collective-permute-done((bf16[4,4,128,256]{3,2,1,0:T(8,128)(2,1)S(1)}, bf16[4,4,128,256]{3,2,1,0:T(8,128)(2,1)}, u32[]{:S(2)}, u32[]{:S(2)}) %collective-permute-start.7) | collective-permute-done | bytes 1048608 | tf_op jit(solution)/shard_map/ppermute | solution.py:72
  153.2 3.8 %shard_map.87 = (f32[256,128]{1,0:T(8,128)}, f32[512,256]{1,0:T(8,128)}) custom-call(s32[3]{0:T(128)S(1)} %pad_add_fusion.role, bf16[4,4,2,128,256]{4,3,2,1,0:T(8,128)(2,1)S(1)} %all-to-all-done.mine, bf16[4,4,2,128,256]{4,3,2,1,0:T(8,128)(2,1)} %collective-permute-done.6.their, bf16[4,4,128,256]{3,2,1,0:T(8,128)(2,1)S(1)} %pad_maximum_fusion.late, ...), custom_call_target="tpu_custom_call" | custom-call | flops 671088640 | bytes 7602176 | tf_op jit(solution)/shard_map/pallas_call | solution.py:92
  156.9 5.9 %all-to-all-done.3 = bf16[4,4,2,128,256]{4,3,1,2,0:T(8,128)(2,1)} async-done(((bf16[4,4,2,128,256]{4,3,1,2,0:T(8,128)(2,1)}), bf16[4,4,2,128,256]{4,3,1,2,0:T(8,128)(2,1)}, u32[]{:S(2)}, u32[]{:S(2)}) %all-to-all-start.3) | async-done | bytes 2097184 | tf_op jit(solution)/shard_map/all_to_all | solution.py:64
  (38 shorter events, 18.4 us)
Async XLA Ops:
  9.3 3.5 %collective-permute-start = (bf16[2,128,256]{2,1,0:T(8,128)(2,1)S(1)}, bf16[2,128,256]{2,1,0:T(8,128)(2,1)S(1)}, u32[]{:S(2)}, u32[]{:S(2)}) collective-permute-start(bf16[2,128,256]{2,1,0:T(8,128)(2,1)S(1)} %bitcast.32), channel_id=1, source_target_pairs={{0,0},{1,1},{2,2},{3,33},{4,4},{5,65},{6,6},{7,97},{8,8},{9,129},{... | collective-permute-start | bytes 393224 | tf_op jit(solution)/shard_map/ppermute | solution.py:236
  12.1 26.5 %collective-permute-start.1 = (bf16[128,256]{1,0:T(8,128)(2,1)S(1)}, bf16[128,256]{1,0:T(8,128)(2,1)S(1)}, u32[]{:S(2)}, u32[]{:S(2)}) collective-permute-start(bf16[128,256]{1,0:T(8,128)(2,1)S(1)} %all_gather.41), channel_id=1, source_target_pairs={{0,0},{1,1},{2,2},{3,33},{4,4},{5,65},{6,6},{7,97},{8,8},{9,129},{... | collective-permute-start | bytes 196616 | tf_op jit(solution)/shard_map/ppermute | solution.py:239
  40.2 7.7 %copy-start.3 = (bf16[256,128]{1,0:T(8,128)(2,1)S(1)}, bf16[256,128]{1,0:T(8,128)(2,1)}, u32[]{:S(2)}) copy-start(bf16[256,128]{1,0:T(8,128)(2,1)} %param.10) | copy-start | bytes 196612
  40.2 9.6 %copy-start.2 = (bf16[512,256]{1,0:T(8,128)(2,1)S(1)}, bf16[512,256]{1,0:T(8,128)(2,1)}, u32[]{:S(2)}) copy-start(bf16[512,256]{1,0:T(8,128)(2,1)} %param.11) | copy-start | bytes 786436
  40.2 23.0 %all-to-all-start = ((bf16[4,4,2,128,256]{4,3,2,1,0:T(8,128)(2,1)}), bf16[4,4,2,128,256]{4,3,2,1,0:T(8,128)(2,1)S(1)}, u32[]{:S(2)}, u32[]{:S(2)}) async-start(bf16[4,4,2,128,256]{4,3,2,1,0:T(8,128)(2,1)} %broadcast_in_dim.4), calls=%async_computation | async-start | bytes 4194304 | tf_op jit(solution)/shard_map/all_to_all | solution.py:64
  65.8 19.9 %all-to-all-start.1 = ((bf16[4,2,512,256]{3,2,1,0:T(8,128)(2,1)}), bf16[4,2,512,256]{3,2,1,0:T(8,128)(2,1)}, u32[]{:S(2)}, u32[]{:S(2)}) async-start(bf16[4,2,512,256]{3,2,1,0:T(8,128)(2,1)} %shard_map.85), calls=%async_computation.1 | async-start | bytes 4194304 | tf_op jit(solution)/shard_map/all_to_all | solution.py:64
  88.8 30.3 %all-to-all-start.2 = ((bf16[4,2,128,256]{3,2,1,0:T(8,128)(2,1)}), bf16[4,2,128,256]{3,2,1,0:T(8,128)(2,1)}, u32[]{:S(2)}, u32[]{:S(2)}) async-start(bf16[4,2,128,256]{3,2,1,0:T(8,128)(2,1)} %pad_maximum_fusion.1), calls=%async_computation.2 | async-start | bytes 1048576 | tf_op jit(solution)/shard_map/all_to_all | solution.py:64
  99.6 9.8 %collective-permute-start.2 = (bf16[4,128,256]{2,1,0:T(8,128)(2,1)S(1)}, bf16[4,128,256]{2,1,0:T(8,128)(2,1)S(1)}, u32[]{:S(2)}, u32[]{:S(2)}) collective-permute-start(bf16[4,128,256]{2,1,0:T(8,128)(2,1)S(1)} %bitcast.27), channel_id=1, source_target_pairs={{0,128},{128,256},{256,384},{384,0},{2,130},{130,258},{258,386},{3... | collective-permute-start | bytes 786440 | tf_op jit(solution)/shard_map/ppermute | solution.py:271
  101.7 11.4 %collective-permute-start.4 = (bf16[4,128,256]{2,1,0:T(8,128)(2,1)S(1)}, bf16[4,128,256]{2,1,0:T(8,128)(2,1)S(1)}, u32[]{:S(2)}, u32[]{:S(2)}) collective-permute-start(bf16[4,128,256]{2,1,0:T(8,128)(2,1)S(1)} %bitcast.28), channel_id=1, source_target_pairs={{0,384},{128,0},{256,128},{384,256},{2,386},{130,2},{258,130},{386... | collective-permute-start | bytes 786440 | tf_op jit(solution)/shard_map/ppermute | solution.py:272
  106.0 43.4 %collective-permute-start.6 = (bf16[4,4,2,128,256]{4,3,2,1,0:T(8,128)(2,1)S(1)}, bf16[4,4,2,128,256]{4,3,2,1,0:T(8,128)(2,1)}, u32[]{:S(2)}, u32[]{:S(2)}) collective-permute-start(bf16[4,4,2,128,256]{4,3,2,1,0:T(8,128)(2,1)S(1)} %all-to-all-done.mine), channel_id=1, source_target_pairs={{0,1},{1,0},{2,3},{3,2},{4,5},{5,4},{6,7},{7,6},{8,9},{9,8},{10,11... | collective-permute-start | bytes 6291464 | tf_op jit(solution)/shard_map/ppermute | solution.py:72
  109.4 7.3 %collective-permute-start.3 = (bf16[2,128,256]{2,1,0:T(8,128)(2,1)S(1)}, bf16[2,128,256]{2,1,0:T(8,128)(2,1)S(1)}, u32[]{:S(2)}, u32[]{:S(2)}) collective-permute-start(bf16[2,128,256]{2,1,0:T(8,128)(2,1)S(1)} %slice.32), channel_id=1, source_target_pairs={{0,128},{128,256},{256,384},{384,0},{2,130},{130,258},{258,386},{3... | collective-permute-start | bytes 393224 | tf_op jit(solution)/shard_map/ppermute | solution.py:274
  113.2 5.7 %collective-permute-start.5 = (bf16[2,128,256]{2,1,0:T(8,128)(2,1)S(1)}, bf16[2,128,256]{2,1,0:T(8,128)(2,1)S(1)}, u32[]{:S(2)}, u32[]{:S(2)}) collective-permute-start(bf16[2,128,256]{2,1,0:T(8,128)(2,1)S(1)} %slice.33), channel_id=1, source_target_pairs={{0,384},{128,0},{256,128},{384,256},{2,386},{130,2},{258,130},{386... | collective-permute-start | bytes 393224 | tf_op jit(solution)/shard_map/ppermute | solution.py:275
  142.8 9.3 %copy-start.1 = (f32[256,128]{1,0:T(8,128)S(1)}, f32[256,128]{1,0:T(8,128)}, u32[]{:S(2)}) copy-start(f32[256,128]{1,0:T(8,128)} %in_old.1) | copy-start | bytes 393220
  142.8 20.0 %all-to-all-start.3 = ((bf16[4,4,2,128,256]{4,3,1,2,0:T(8,128)(2,1)}), bf16[4,4,2,128,256]{4,3,1,2,0:T(8,128)(2,1)}, u32[]{:S(2)}, u32[]{:S(2)}) async-start(bf16[4,4,2,128,256]{4,3,1,2,0:T(8,128)(2,1)} %broadcast_in_dim.5), calls=%async_computation.3 | async-start | bytes 4194304 | tf_op jit(solution)/shard_map/all_to_all | solution.py:64
  147.4 4.7 %collective-permute-start.7 = (bf16[4,4,128,256]{3,2,1,0:T(8,128)(2,1)S(1)}, bf16[4,4,128,256]{3,2,1,0:T(8,128)(2,1)}, u32[]{:S(2)}, u32[]{:S(2)}) collective-permute-start(bf16[4,4,128,256]{3,2,1,0:T(8,128)(2,1)S(1)} %pad_maximum_fusion.late), channel_id=1, source_target_pairs={{0,1},{1,0},{2,3},{3,2},{4,5},{5,4},{6,7},{7,6},{8,9},{9,8},{10,11... | collective-permute-start | bytes 3145736 | tf_op jit(solution)/shard_map/ppermute | solution.py:72
  152.1 1.0 copy-start
  164.2 4.6 %collective-permute-start.8 = (bf16[4,4,128,256]{3,2,1,0:T(8,128)(2,1)S(1)}, bf16[4,4,128,256]{3,2,1,0:T(8,128)(2,1)S(1)}, u32[]{:S(2)}, u32[]{:S(2)}) collective-permute-start(bf16[4,4,128,256]{3,2,1,0:T(8,128)(2,1)S(1)} %slice_bitcast_fusion), channel_id=1, source_target_pairs={{0,1},{1,0},{2,3},{3,2},{4,5},{5,4},{6,7},{7,6},{8,9},{9,8},{10,11... | collective-permute-start | bytes 3145736 | tf_op jit(solution)/shard_map/ppermute | solution.py:72

commit v6 on v5

--- a/solution.py
+++ b/solution.py
@@ -268,12 +268,8 @@
     part = resum(first, part)
     part, late = tied((part, late))
     part = exchange(part, back_z)
-    left = lax.ppermute(late, ALL, ring_pairs(1))
-    right = lax.ppermute(late, ALL, ring_pairs(-1))
-    span = SIDE // CORES
-    ahead = lax.ppermute(left[:span], ALL, ring_pairs(1))
-    behind = lax.ppermute(right[span:], ALL, ring_pairs(-1))
-    late = jnp.stack([late, left, jnp.concatenate([ahead, behind]), right])
+    turns = [lax.ppermute(late, ALL, ring_pairs(turn)) for turn in range(1, SIDE)]
+    late = jnp.stack([late] + turns)
     their_late = core_swap(late)
     part, late = tied((part, late))
     mixed = local_call(

time: 172 us -> 171 us (level)
    ppermute x4 -> x3, starting transfers between devices: 13.1 us -> 8.4 us  [per_device(): lax.ppermute(late, ALL, ring_pairs(turn))]
    all_to_all x4, waiting for transfers between devices: 21.2 us -> 24.5 us  [exchange(): return lax.all_to_all(parts, ALL, 0, 0, axis_index_groups=groups)]
    ppermute x3, starting transfers between devices: 7.17 us -> 10.4 us  [core_swap(): return lax.ppermute(block, 'core', [(0, 1), (1, 0)])]
  transfers between devices with their start and end apart: 13 -> 12, of which waited for: 7 -> 7; matrix products, arithmetic and copies ran while one was open for 2% -> 2% of each run, Pallas kernels for 3% -> 3%
where the time goes in v6:
time: 171 us; the launch traced here: 169 us
  blocking collectives  71.9 us (42%)
  starting transfers between devices  47.4 us (28%)
  waiting for transfers between devices  29.3 us (17%)
  Pallas kernels  9.39 us (5%)
  local copies, waits for them, and re-layouts  7.39 us (4%)
  other arithmetic  3.22 us (2%)
    all_gather x3, blocking collectives, gather(): lax.all_gather(block, ALL, axis_index_groups=groups, axis=0, tiled=False)  57.1 us
    all_to_all x4, starting transfers between devices, exchange(): return lax.all_to_all(parts, ALL, 0, 0, axis_index_groups=groups)  27.3 us
    all_to_all x4, waiting for transfers between devices, exchange(): return lax.all_to_all(parts, ALL, 0, 0, axis_index_groups=groups)  24.5 us
    ppermute x3, starting transfers between devices, core_swap(): return lax.ppermute(block, 'core', [(0, 1), (1, 0)])  10.4 us
    pallas_call x4, Pallas kernels, local_call(): pl.pallas_call(body, grid=grid, out_shape=out_shape, in_specs=[pl.BlockSp...  9.39 us
    all_gather x1, blocking collectives, per_device(): grads_pair = lax.all_gather(output_grads, 'core', axis=0, tiled=False)  8.64 us
    ppermute x3, starting transfers between devices, per_device(): lax.ppermute(late, ALL, ring_pairs(turn))  8.4 us
  transfers between devices with their start and end apart: 12, of which 7 were waited for; matrix products, arithmetic and copies ran while one was open for 2% of the time, Pallas kernels for 3%

profile of v6, /device:TPU:1, one launch (start us, length us, event | category | flops | bytes accessed | tf_op | source)
XLA Modules:
  0.0 169.5 jit_solution(15031636413737216580)
XLA Ops:
  0.6 8.6 %all-gather = bf16[256,256]{1,0:T(8,128)(2,1)S(1)} all-gather(bf16[128,256]{1,0:T(8,128)(2,1)} %param.7), channel_id=2, replica_groups=mesh['x'=4,'zh'=4,'y'=4,'zl'=4,'core'=2] {'core'}, dimensions={0}, use_global_device_ids=true | all-gather | bytes 196608 | tf_op jit(solution)/shard_map/all_gather | solution.py:235
  9.9 2.1 %all_gather.41 = bf16[128,256]{1,0:T(8,128)(2,1)S(1)} all-gather(bf16[128,128]{1,0:T(8,128)(2,1)} %param.6), channel_id=1, replica_groups=mesh['x'=4,'zh'=4,'y'=4,'zl'=4,'core'=2] {'core'}, dimensions={1}, use_global_device_ids=true | all-gather | bytes 98304 | tf_op jit(solution)/shard_map/all_gather | solution.py:238
  12.8 25.8 %all-gather.1 = bf16[8,128,256]{2,1,0:T(8,128)(2,1)S(1)} all-gather(bf16[2,128,256]{2,1,0:T(8,128)(2,1)S(1)} %maximum_select_fusion), channel_id=3, replica_groups={{0,32,64,96},{2,34,66,98},{4,36,68,100},{6,38,70,102},{8,40,72,104},{10..., dimensions={0}, use_global_device_ids=true | all-gather | bytes 655360 | tf_op jit(solution)/shard_map/all_gather | solution.py:60
  40.2 7.7 %all-to-all-start = ((bf16[4,4,2,128,256]{4,3,2,1,0:T(8,128)(2,1)}), bf16[4,4,2,128,256]{4,3,2,1,0:T(8,128)(2,1)S(1)}, u32[]{:S(2)}, u32[]{:S(2)}) async-start(bf16[4,4,2,128,256]{4,3,2,1,0:T(8,128)(2,1)} %broadcast_in_dim.4), calls=%async_computation | async-start | bytes 4194304 | tf_op jit(solution)/shard_map/all_to_all | solution.py:64
  49.8 2.2 %all-gather.3 = bf16[1024,256]{1,0:T(8,128)(2,1)S(1)} all-gather(bf16[512,256]{1,0:T(8,128)(2,1)S(1)} %copy-done.2), channel_id=5, replica_groups=mesh['x'=4,'zh'=4,'y'=4,'zl'=4,'core'=2] {'core'}, dimensions={0}, use_global_device_ids=true | all-gather | bytes 786432 | tf_op jit(solution)/shard_map/all_gather | solution.py:247
  51.9 11.3 %all-to-all-done.mine = bf16[4,4,2,128,256]{4,3,2,1,0:T(8,128)(2,1)S(1)} async-done(((bf16[4,4,2,128,256]{4,3,2,1,0:T(8,128)(2,1)}), bf16[4,4,2,128,256]{4,3,2,1,0:T(8,128)(2,1)S(1)}, u32[]{:S(2)}, u32[]{:S(2)}) %all-to-all-start) | async-done | bytes 2097184 | tf_op jit(solution)/shard_map/all_to_all | solution.py:64
  63.2 2.6 %shard_map.85 = bf16[4,2,512,256]{3,2,1,0:T(8,128)(2,1)} custom-call(s32[1]{0:T(128)} %bitcast.role, bf16[4,4,2,128,256]{4,3,2,1,0:T(8,128)(2,1)S(1)} %all-to-all-done.mine, bf16[2,256,128]{2,1,0:T(8,128)(2,1)S(1)} %bitcast.21, bf16[2,512,256]{2,1,0:T(8,128)(2,1)S(1)} %bitcast.20), custom_call_target="tpu_custom_call" | custom-call | flops 1073741824 | bytes 4849664 | tf_op jit(solution)/shard_map/pallas_call | solution.py:92
  65.8 4.5 %all-to-all-start.1 = ((bf16[4,2,512,256]{3,2,1,0:T(8,128)(2,1)}), bf16[4,2,512,256]{3,2,1,0:T(8,128)(2,1)}, u32[]{:S(2)}, u32[]{:S(2)}) async-start(bf16[4,2,512,256]{3,2,1,0:T(8,128)(2,1)} %shard_map.85), calls=%async_computation.1 | async-start | bytes 4194304 | tf_op jit(solution)/shard_map/all_to_all | solution.py:64
  70.3 11.4 %all-gather.4 = bf16[512,256]{1,0:T(8,128)(2,1)S(1)} all-gather(bf16[128,256]{1,0:T(8,128)(2,1)S(1)} %broadcast_select_fusion), channel_id=6, replica_groups={{0,32,64,96},{2,34,66,98},{4,36,68,100},{6,38,70,102},{8,40,72,104},{10..., dimensions={0}, use_global_device_ids=true | all-gather | bytes 327680 | tf_op jit(solution)/shard_map/all_gather | solution.py:60
  81.7 4.2 %all-to-all-done.1 = bf16[4,2,512,256]{3,2,1,0:T(8,128)(2,1)} async-done(((bf16[4,2,512,256]{3,2,1,0:T(8,128)(2,1)}), bf16[4,2,512,256]{3,2,1,0:T(8,128)(2,1)}, u32[]{:S(2)}, u32[]{:S(2)}) %all-to-all-start.1) | async-done | bytes 2097184 | tf_op jit(solution)/shard_map/all_to_all | solution.py:64
  85.9 2.0 %convert_reduce_fusion = f32[2,512,256]{2,1,0:T(8,128)S(1)} fusion(bf16[4,2,512,256]{3,2,1,0:T(8,128)(2,1)} %all-to-all-done.1), kind=kLoop, calls=%fused_computation | loop fusion | flops 1835008 | bytes 3145728 | tf_op jit(solution)/shard_map/reduce_sum | solution.py:150
  89.0 10.6 %all-to-all-start.2 = ((bf16[4,2,128,256]{3,2,1,0:T(8,128)(2,1)}), bf16[4,2,128,256]{3,2,1,0:T(8,128)(2,1)}, u32[]{:S(2)}, u32[]{:S(2)}) async-start(bf16[4,2,128,256]{3,2,1,0:T(8,128)(2,1)} %pad_maximum_fusion.1), calls=%async_computation.2 | async-start | bytes 1048576 | tf_op jit(solution)/shard_map/all_to_all | solution.py:64
  99.5 2.2 %collective-permute-start.2 = (bf16[4,128,256]{2,1,0:T(8,128)(2,1)S(1)}, bf16[4,128,256]{2,1,0:T(8,128)(2,1)S(1)}, u32[]{:S(2)}, u32[]{:S(2)}) collective-permute-start(bf16[4,128,256]{2,1,0:T(8,128)(2,1)S(1)} %bitcast.26), channel_id=1, source_target_pairs={{0,128},{128,256},{256,384},{384,0},{2,130},{130,258},{258,386},{3... | collective-permute-start | bytes 786440 | tf_op jit(solution)/shard_map/ppermute | solution.py:271
  101.7 3.7 %collective-permute-start.3 = (bf16[4,128,256]{2,1,0:T(8,128)(2,1)S(1)}, bf16[4,128,256]{2,1,0:T(8,128)(2,1)S(1)}, u32[]{:S(2)}, u32[]{:S(2)}) collective-permute-start(bf16[4,128,256]{2,1,0:T(8,128)(2,1)S(1)} %bitcast.27), channel_id=1, source_target_pairs={{0,256},{128,384},{256,0},{384,128},{2,258},{130,386},{258,2},{386... | collective-permute-start | bytes 786440 | tf_op jit(solution)/shard_map/ppermute | solution.py:271
  105.4 2.5 %collective-permute-start.4 = (bf16[4,128,256]{2,1,0:T(8,128)(2,1)S(1)}, bf16[4,128,256]{2,1,0:T(8,128)(2,1)S(1)}, u32[]{:S(2)}, u32[]{:S(2)}) collective-permute-start(bf16[4,128,256]{2,1,0:T(8,128)(2,1)S(1)} %bitcast.28), channel_id=1, source_target_pairs={{0,384},{128,0},{256,128},{384,256},{2,386},{130,2},{258,130},{386... | collective-permute-start | bytes 786440 | tf_op jit(solution)/shard_map/ppermute | solution.py:271
  108.0 3.5 %collective-permute-start.5 = (bf16[4,4,2,128,256]{4,3,2,1,0:T(8,128)(2,1)S(1)}, bf16[4,4,2,128,256]{4,3,2,1,0:T(8,128)(2,1)}, u32[]{:S(2)}, u32[]{:S(2)}) collective-permute-start(bf16[4,4,2,128,256]{4,3,2,1,0:T(8,128)(2,1)S(1)} %all-to-all-done.mine), channel_id=1, source_target_pairs={{0,1},{1,0},{2,3},{3,2},{4,5},{5,4},{6,7},{7,6},{8,9},{9,8},{10,11... | collective-permute-start | bytes 6291464 | tf_op jit(solution)/shard_map/ppermute | solution.py:72
  113.6 3.6 %all-to-all-done.2.parts = bf16[4,2,128,256]{3,2,1,0:T(8,128)(2,1)} async-done(((bf16[4,2,128,256]{3,2,1,0:T(8,128)(2,1)}), bf16[4,2,128,256]{3,2,1,0:T(8,128)(2,1)}, u32[]{:S(2)}, u32[]{:S(2)}) %all-to-all-start.2) | async-done | bytes 524320 | tf_op jit(solution)/shard_map/all_to_all | solution.py:64
  118.3 19.9 %all-gather.5 = bf16[8,128,256]{2,1,0:T(8,128)(2,1)S(1)} all-gather(bf16[2,128,256]{2,1,0:T(8,128)(2,1)S(1)} %shard_map.86), channel_id=7, replica_groups={{0,2,4,6},{8,10,12,14},{16,18,20,22},{24,26,28,30},{32,34,36,38},{40,42..., dimensions={0}, use_global_device_ids=true | all-gather | bytes 655360 | tf_op jit(solution)/shard_map/all_gather | solution.py:60
  139.8 4.6 %all-to-all-start.3 = ((bf16[4,4,2,128,256]{4,3,1,2,0:T(8,128)(2,1)}), bf16[4,4,2,128,256]{4,3,1,2,0:T(8,128)(2,1)}, u32[]{:S(2)}, u32[]{:S(2)}) async-start(bf16[4,4,2,128,256]{4,3,1,2,0:T(8,128)(2,1)} %broadcast_in_dim.5), calls=%async_computation.3 | async-start | bytes 4194304 | tf_op jit(solution)/shard_map/all_to_all | solution.py:64
  144.4 3.0 %collective-permute-start.6 = (bf16[4,4,128,256]{3,2,1,0:T(8,128)(2,1)S(1)}, bf16[4,4,128,256]{3,2,1,0:T(8,128)(2,1)}, u32[]{:S(2)}, u32[]{:S(2)}) collective-permute-start(bf16[4,4,128,256]{3,2,1,0:T(8,128)(2,1)S(1)} %pad_maximum_fusion.late), channel_id=1, source_target_pairs={{0,1},{1,0},{2,3},{3,2},{4,5},{5,4},{6,7},{7,6},{8,9},{9,8},{10,11... | collective-permute-start | bytes 3145736 | tf_op jit(solution)/shard_map/ppermute | solution.py:72
  147.5 2.3 %collective-permute-done.6.their_late = bf16[4,4,128,256]{3,2,1,0:T(8,128)(2,1)} collective-permute-done((bf16[4,4,128,256]{3,2,1,0:T(8,128)(2,1)S(1)}, bf16[4,4,128,256]{3,2,1,0:T(8,128)(2,1)}, u32[]{:S(2)}, u32[]{:S(2)}) %collective-permute-start.6) | collective-permute-done | bytes 1048608 | tf_op jit(solution)/shard_map/ppermute | solution.py:72
  150.9 3.8 %shard_map.87 = (f32[256,128]{1,0:T(8,128)}, f32[512,256]{1,0:T(8,128)}) custom-call(s32[3]{0:T(128)S(1)} %pad_add_fusion.role, bf16[4,4,2,128,256]{4,3,2,1,0:T(8,128)(2,1)S(1)} %all-to-all-done.mine, bf16[4,4,2,128,256]{4,3,2,1,0:T(8,128)(2,1)} %collective-permute-done.5.their, bf16[4,4,128,256]{3,2,1,0:T(8,128)(2,1)S(1)} %pad_maximum_fusion.late, ...), custom_call_target="tpu_custom_call" | custom-call | flops 671088640 | bytes 7602176 | tf_op jit(solution)/shard_map/pallas_call | solution.py:92
  154.6 5.5 %all-to-all-done.3 = bf16[4,4,2,128,256]{4,3,1,2,0:T(8,128)(2,1)} async-done(((bf16[4,4,2,128,256]{4,3,1,2,0:T(8,128)(2,1)}), bf16[4,4,2,128,256]{4,3,1,2,0:T(8,128)(2,1)}, u32[]{:S(2)}, u32[]{:S(2)}) %all-to-all-start.3) | async-done | bytes 2097184 | tf_op jit(solution)/shard_map/all_to_all | solution.py:64
  161.4 3.9 %collective-permute-start.7 = (bf16[4,4,128,256]{3,2,1,0:T(8,128)(2,1)S(1)}, bf16[4,4,128,256]{3,2,1,0:T(8,128)(2,1)S(1)}, u32[]{:S(2)}, u32[]{:S(2)}) collective-permute-start(bf16[4,4,128,256]{3,2,1,0:T(8,128)(2,1)S(1)} %slice_bitcast_fusion), channel_id=1, source_target_pairs={{0,1},{1,0},{2,3},{3,2},{4,5},{5,4},{6,7},{7,6},{8,9},{9,8},{10,11... | collective-permute-start | bytes 3145736 | tf_op jit(solution)/shard_map/ppermute | solution.py:72
  (33 shorter events, 17.3 us)
Async XLA Ops:
  9.3 3.5 %collective-permute-start = (bf16[2,128,256]{2,1,0:T(8,128)(2,1)S(1)}, bf16[2,128,256]{2,1,0:T(8,128)(2,1)S(1)}, u32[]{:S(2)}, u32[]{:S(2)}) collective-permute-start(bf16[2,128,256]{2,1,0:T(8,128)(2,1)S(1)} %bitcast.30), channel_id=1, source_target_pairs={{0,0},{1,1},{2,2},{3,33},{4,4},{5,65},{6,6},{7,97},{8,8},{9,129},{... | collective-permute-start | bytes 393224 | tf_op jit(solution)/shard_map/ppermute | solution.py:236
  12.1 26.5 %collective-permute-start.1 = (bf16[128,256]{1,0:T(8,128)(2,1)S(1)}, bf16[128,256]{1,0:T(8,128)(2,1)S(1)}, u32[]{:S(2)}, u32[]{:S(2)}) collective-permute-start(bf16[128,256]{1,0:T(8,128)(2,1)S(1)} %all_gather.41), channel_id=1, source_target_pairs={{0,0},{1,1},{2,2},{3,33},{4,4},{5,65},{6,6},{7,97},{8,8},{9,129},{... | collective-permute-start | bytes 196616 | tf_op jit(solution)/shard_map/ppermute | solution.py:239
  40.2 7.7 %copy-start.3 = (bf16[256,128]{1,0:T(8,128)(2,1)S(1)}, bf16[256,128]{1,0:T(8,128)(2,1)}, u32[]{:S(2)}) copy-start(bf16[256,128]{1,0:T(8,128)(2,1)} %param.10) | copy-start | bytes 196612
  40.2 9.6 %copy-start.2 = (bf16[512,256]{1,0:T(8,128)(2,1)S(1)}, bf16[512,256]{1,0:T(8,128)(2,1)}, u32[]{:S(2)}) copy-start(bf16[512,256]{1,0:T(8,128)(2,1)} %param.11) | copy-start | bytes 786436
  40.2 23.0 %all-to-all-start = ((bf16[4,4,2,128,256]{4,3,2,1,0:T(8,128)(2,1)}), bf16[4,4,2,128,256]{4,3,2,1,0:T(8,128)(2,1)S(1)}, u32[]{:S(2)}, u32[]{:S(2)}) async-start(bf16[4,4,2,128,256]{4,3,2,1,0:T(8,128)(2,1)} %broadcast_in_dim.4), calls=%async_computation | async-start | bytes 4194304 | tf_op jit(solution)/shard_map/all_to_all | solution.py:64
  65.8 20.1 %all-to-all-start.1 = ((bf16[4,2,512,256]{3,2,1,0:T(8,128)(2,1)}), bf16[4,2,512,256]{3,2,1,0:T(8,128)(2,1)}, u32[]{:S(2)}, u32[]{:S(2)}) async-start(bf16[4,2,512,256]{3,2,1,0:T(8,128)(2,1)} %shard_map.85), calls=%async_computation.1 | async-start | bytes 4194304 | tf_op jit(solution)/shard_map/all_to_all | solution.py:64
  89.0 28.2 %all-to-all-start.2 = ((bf16[4,2,128,256]{3,2,1,0:T(8,128)(2,1)}), bf16[4,2,128,256]{3,2,1,0:T(8,128)(2,1)}, u32[]{:S(2)}, u32[]{:S(2)}) async-start(bf16[4,2,128,256]{3,2,1,0:T(8,128)(2,1)} %pad_maximum_fusion.1), calls=%async_computation.2 | async-start | bytes 1048576 | tf_op jit(solution)/shard_map/all_to_all | solution.py:64
  99.5 12.0 %collective-permute-start.2 = (bf16[4,128,256]{2,1,0:T(8,128)(2,1)S(1)}, bf16[4,128,256]{2,1,0:T(8,128)(2,1)S(1)}, u32[]{:S(2)}, u32[]{:S(2)}) collective-permute-start(bf16[4,128,256]{2,1,0:T(8,128)(2,1)S(1)} %bitcast.26), channel_id=1, source_target_pairs={{0,128},{128,256},{256,384},{384,0},{2,130},{130,258},{258,386},{3... | collective-permute-start | bytes 786440 | tf_op jit(solution)/shard_map/ppermute | solution.py:271
  101.7 9.8 %collective-permute-start.3 = (bf16[4,128,256]{2,1,0:T(8,128)(2,1)S(1)}, bf16[4,128,256]{2,1,0:T(8,128)(2,1)S(1)}, u32[]{:S(2)}, u32[]{:S(2)}) collective-permute-start(bf16[4,128,256]{2,1,0:T(8,128)(2,1)S(1)} %bitcast.27), channel_id=1, source_target_pairs={{0,256},{128,384},{256,0},{384,128},{2,258},{130,386},{258,2},{386... | collective-permute-start | bytes 786440 | tf_op jit(solution)/shard_map/ppermute | solution.py:271
  105.4 8.0 %collective-permute-start.4 = (bf16[4,128,256]{2,1,0:T(8,128)(2,1)S(1)}, bf16[4,128,256]{2,1,0:T(8,128)(2,1)S(1)}, u32[]{:S(2)}, u32[]{:S(2)}) collective-permute-start(bf16[4,128,256]{2,1,0:T(8,128)(2,1)S(1)} %bitcast.28), channel_id=1, source_target_pairs={{0,384},{128,0},{256,128},{384,256},{2,386},{130,2},{258,130},{386... | collective-permute-start | bytes 786440 | tf_op jit(solution)/shard_map/ppermute | solution.py:271
  108.0 39.5 %collective-permute-start.5 = (bf16[4,4,2,128,256]{4,3,2,1,0:T(8,128)(2,1)S(1)}, bf16[4,4,2,128,256]{4,3,2,1,0:T(8,128)(2,1)}, u32[]{:S(2)}, u32[]{:S(2)}) collective-permute-start(bf16[4,4,2,128,256]{4,3,2,1,0:T(8,128)(2,1)S(1)} %all-to-all-done.mine), channel_id=1, source_target_pairs={{0,1},{1,0},{2,3},{3,2},{4,5},{5,4},{6,7},{7,6},{8,9},{9,8},{10,11... | collective-permute-start | bytes 6291464 | tf_op jit(solution)/shard_map/ppermute | solution.py:72
  139.8 10.0 %copy-start.1 = (f32[256,128]{1,0:T(8,128)S(1)}, f32[256,128]{1,0:T(8,128)}, u32[]{:S(2)}) copy-start(f32[256,128]{1,0:T(8,128)} %in_old.1) | copy-start | bytes 393220
  139.8 20.3 %all-to-all-start.3 = ((bf16[4,4,2,128,256]{4,3,1,2,0:T(8,128)(2,1)}), bf16[4,4,2,128,256]{4,3,1,2,0:T(8,128)(2,1)}, u32[]{:S(2)}, u32[]{:S(2)}) async-start(bf16[4,4,2,128,256]{4,3,1,2,0:T(8,128)(2,1)} %broadcast_in_dim.5), calls=%async_computation.3 | async-start | bytes 4194304 | tf_op jit(solution)/shard_map/all_to_all | solution.py:64
  144.4 5.4 %collective-permute-start.6 = (bf16[4,4,128,256]{3,2,1,0:T(8,128)(2,1)S(1)}, bf16[4,4,128,256]{3,2,1,0:T(8,128)(2,1)}, u32[]{:S(2)}, u32[]{:S(2)}) collective-permute-start(bf16[4,4,128,256]{3,2,1,0:T(8,128)(2,1)S(1)} %pad_maximum_fusion.late), channel_id=1, source_target_pairs={{0,1},{1,0},{2,3},{3,2},{4,5},{5,4},{6,7},{7,6},{8,9},{9,8},{10,11... | collective-permute-start | bytes 3145736 | tf_op jit(solution)/shard_map/ppermute | solution.py:72
  149.8 1.0 copy-start
  161.4 6.2 %collective-permute-start.7 = (bf16[4,4,128,256]{3,2,1,0:T(8,128)(2,1)S(1)}, bf16[4,4,128,256]{3,2,1,0:T(8,128)(2,1)S(1)}, u32[]{:S(2)}, u32[]{:S(2)}) collective-permute-start(bf16[4,4,128,256]{3,2,1,0:T(8,128)(2,1)S(1)} %slice_bitcast_fusion), channel_id=1, source_target_pairs={{0,1},{1,0},{2,3},{3,2},{4,5},{5,4},{6,7},{7,6},{8,9},{9,8},{10,11... | collective-permute-start | bytes 3145736 | tf_op jit(solution)/shard_map/ppermute | solution.py:72

commit v7 on v6

--- a/solution.py
+++ b/solution.py
@@ -113,37 +113,26 @@
     return high, (value - high.astype(f32)).astype(bf16)
 
 
-def partial_body(role, mine, in_inverse, out_inverse, out, ready, sems):
-    deep = out_inverse.shape[1] // CORES
-
-    def send(i):
-        return pltpu.make_async_copy(ready.at[i], out.at[i], sems.at[i])
+def partial_body(role, mine, in_inverse, out_own, other, out):
+    deep = out_own.shape[0] // CORES
 
     @pl.when(role[0] == 0)
     def _():
-        inverse = jnp.concatenate([in_inverse[0], in_inverse[1]], axis=1)
 
         @pl.loop(0, SIDE)
         def _(i):
-            high, low = high_low(dot(flat(mine[i, :, 0]), inverse, by_cols))
-            ready[i, 0] = high
-            ready[i, 1] = low
-            send(i).start()
+            high, low = high_low(dot(flat(mine[i, :, 0]), in_inverse[...], by_cols))
+            out[i, 0] = high
+            out[i, 1] = low
 
     @pl.when(role[0] == 1)
     def _():
         @pl.loop(0, SIDE)
         def _(i):
             near, far = flat(mine[i, :, 0]), flat(mine[i, :, 1])
-            for half in range(CORES):
-                part = dot(near, out_inverse[half, :deep], plain)
-                part = part + dot(far, out_inverse[half, deep:], plain)
-                ready[i, half] = part.astype(bf16)
-            send(i).start()
-
-    @pl.loop(0, SIDE)
-    def _(i):
-        send(i).wait()
+            for half, inverse in ((0, other), (1, out_own)):
+                part = dot(near, inverse[:deep], plain) + dot(far, inverse[deep:], plain)
+                out[i, half] = part.astype(bf16)
 
 
 def resum(first, parts):
@@ -234,39 +223,35 @@
 
     grads_pair = lax.all_gather(output_grads, "core", axis=0, tiled=False)
     grads_moved = lax.ppermute(grads_pair, ALL, swap_pairs())
-    grads_pair, layer_inputs = tied((grads_pair, layer_inputs))
-    input_pair = lax.all_gather(layer_inputs, "core", axis=1, tiled=True)
+    grads_pair, layer_inputs, input_inverse = tied((grads_pair, layer_inputs, input_inverse))
+    input_pair = jnp.concatenate([layer_inputs, input_inverse])
+    input_pair = lax.all_gather(input_pair, "core", axis=1, tiled=True)
+    input_pair, in_inverse = input_pair[:rows], input_pair[rows:]
     inputs_moved = lax.ppermute(input_pair, ALL, swap_pairs())
     block = jnp.where(first, jnp.stack([input_pair, grads_pair[0]]), grads_moved)
     block = gather(block, out_z)
-    block, late, inputs_moved, input_inverse, output_inverse = tied(
-        (block, grads_pair[1], inputs_moved, input_inverse, output_inverse)
+    block, late, inputs_moved, other = tied(
+        (block, grads_pair[1], inputs_moved, output_inverse)
     )
     mine = gather_direct(block, out_xy)
-    in_inverse = lax.all_gather(input_inverse, "core", axis=0, tiled=False)
-    out_inverse = lax.all_gather(output_inverse, "core", axis=0, tiled=False)
+    other = core_swap(other)
+    late = gather(jnp.where(first, late, inputs_moved), out_z)
+    mine, late = tied((mine, late))
 
     part = local_call(
         partial_body,
-        pltpu.HBM((SIDE, CORES, SIDE * rows, wide), bf16),
+        jax.ShapeDtypeStruct((SIDE, CORES, SIDE * rows, wide), bf16),
         role,
         mine,
         in_inverse,
-        out_inverse,
+        output_inverse,
+        other,
         flops=2 * tokens * 4 * wide * wide,
-        out_blocks=pl.BlockSpec(memory_space=pltpu.HBM),
-        scratch=[
-            pltpu.VMEM((SIDE, CORES, SIDE * rows, wide), bf16),
-            pltpu.SemaphoreType.DMA((SIDE,)),
-        ],
-    )
+    )
+    part = exchange(part, back_xy)
+    part = resum(first, part)
     part, late, mine = tied((part, late, mine))
     their = core_swap(mine)
-    late = gather(jnp.where(first, late, inputs_moved), out_z)
-    part = exchange(part, back_xy)
-    part, late = tied((part, late))
-    part = resum(first, part)
-    part, late = tied((part, late))
     part = exchange(part, back_z)
     turns = [lax.ppermute(late, ALL, ring_pairs(turn)) for turn in range(1, SIDE)]
     late = jnp.stack([late] + turns)

time: 171 us -> 169 us (0.988)
  blocking collectives: 71.9 us -> 90.4 us
  waiting for transfers between devices: 29.3 us -> 14.9 us
  starting transfers between devices: 47.4 us -> 43.6 us
    all_to_all x0 -> x1, blocking collectives: none -> 19 us  [exchange(): return lax.all_to_all(parts, ALL, 0, 0, axis_index_groups=groups)]
    all_to_all x4 -> x3, waiting for transfers between devices: 24.5 us -> 11.7 us  [exchange(): return lax.all_to_all(parts, ALL, 0, 0, axis_index_groups=groups)]
    all_to_all x4 -> x3, starting transfers between devices: 27.3 us -> 18.9 us  [exchange(): return lax.all_to_all(parts, ALL, 0, 0, axis_index_groups=groups)]
    all_gather x3 -> x1, blocking collectives: 6.21 us -> 1.94 us  [per_device(): input_pair = lax.all_gather(input_pair, 'core', axis=1, tiled=True)]
    all_gather x3, blocking collectives: 57.1 us -> 60.8 us  [gather(): lax.all_gather(block, ALL, axis_index_groups=groups, axis=0, tiled=False)]
    ppermute x3 -> x4, starting transfers between devices: 10.4 us -> 13.9 us  [core_swap(): return lax.ppermute(block, 'core', [(0, 1), (1, 0)])]
    ppermute x3, waiting for transfers between devices: 1.94 us -> 0.01 us  [per_device(): lax.ppermute(late, ALL, ring_pairs(turn))]
  transfers between devices with their start and end apart: 12 -> 12, of which waited for: 7 -> 4; matrix products, arithmetic and copies ran while one was open for 2% -> 3% of each run, Pallas kernels for 3% -> 3%
where the time goes in v7:
time: 169 us; the launch traced here: 168 us
  blocking collectives  90.4 us (53%)
  starting transfers between devices  43.6 us (26%)
  waiting for transfers between devices  14.9 us (9%)
  Pallas kernels  8.58 us (5%)
  local copies, waits for them, and re-layouts  7.41 us (4%)
  other arithmetic  2.38 us (1%)
    all_gather x3, blocking collectives, gather(): lax.all_gather(block, ALL, axis_index_groups=groups, axis=0, tiled=False)  60.8 us
    all_to_all x1, blocking collectives, exchange(): return lax.all_to_all(parts, ALL, 0, 0, axis_index_groups=groups)  19 us
    all_to_all x3, starting transfers between devices, exchange(): return lax.all_to_all(parts, ALL, 0, 0, axis_index_groups=groups)  18.9 us
    ppermute x4, starting transfers between devices, core_swap(): return lax.ppermute(block, 'core', [(0, 1), (1, 0)])  13.9 us
    all_to_all x3, waiting for transfers between devices, exchange(): return lax.all_to_all(parts, ALL, 0, 0, axis_index_groups=groups)  11.7 us
    ppermute x3, starting transfers between devices, per_device(): lax.ppermute(late, ALL, ring_pairs(turn))  9.47 us
    all_gather x1, blocking collectives, per_device(): grads_pair = lax.all_gather(output_grads, 'core', axis=0, tiled=False)  8.64 us
    pallas_call x4, Pallas kernels, local_call(): pl.pallas_call(body, grid=grid, out_shape=out_shape, in_specs=[pl.BlockSp...  8.58 us
  transfers between devices with their start and end apart: 12, of which 4 were waited for; matrix products, arithmetic and copies ran while one was open for 3% of the time, Pallas kernels for 3%

profile of v7, /device:TPU:1, one launch (start us, length us, event | category | flops | bytes accessed | tf_op | source)
XLA Modules:
  0.0 168.1 jit_solution(16658151440832629140)
XLA Ops:
  0.6 8.6 %all-gather = bf16[256,256]{1,0:T(8,128)(2,1)S(1)} all-gather(bf16[128,256]{1,0:T(8,128)(2,1)} %param.7), channel_id=2, replica_groups=mesh['x'=4,'zh'=4,'y'=4,'zl'=4,'core'=2] {'core'}, dimensions={0}, use_global_device_ids=true | all-gather | bytes 196608 | tf_op jit(solution)/shard_map/all_gather | solution.py:224
  10.8 1.9 %all_gather.29 = bf16[384,256]{1,0:T(8,128)(2,1)S(1)} all-gather(bf16[384,128]{1,0:T(8,128)(2,1)S(1)} %pad_maximum_fusion.2), channel_id=1, replica_groups=mesh['x'=4,'zh'=4,'y'=4,'zl'=4,'core'=2] {'core'}, dimensions={1}, use_global_device_ids=true | all-gather | bytes 294912 | tf_op jit(solution)/shard_map/all_gather | solution.py:228
  13.5 25.7 %all-gather.1 = bf16[8,128,256]{2,1,0:T(8,128)(2,1)S(1)} all-gather(bf16[2,128,256]{2,1,0:T(8,128)(2,1)S(1)} %maximum_select_fusion), channel_id=3, replica_groups={{0,32,64,96},{2,34,66,98},{4,36,68,100},{6,38,70,102},{8,40,72,104},{10..., dimensions={0}, use_global_device_ids=true | all-gather | bytes 655360 | tf_op jit(solution)/shard_map/all_gather | solution.py:60
  39.2 1.6 broadcast_in_dim.4
  40.8 7.6 %all-to-all-start = ((bf16[4,4,2,128,256]{4,3,2,1,0:T(8,128)(2,1)}), bf16[4,4,2,128,256]{4,3,2,1,0:T(8,128)(2,1)S(1)}, u32[]{:S(2)}, u32[]{:S(2)}) async-start(bf16[4,4,2,128,256]{4,3,2,1,0:T(8,128)(2,1)} %broadcast_in_dim.4), calls=%async_computation | async-start | bytes 4194304 | tf_op jit(solution)/shard_map/all_to_all | solution.py:64
  48.4 1.9 %collective-permute-start.2 = (bf16[512,256]{1,0:T(8,128)(2,1)S(1)}, bf16[512,256]{1,0:T(8,128)(2,1)S(1)}, u32[]{:S(2)}, u32[]{:S(2)}) collective-permute-start(bf16[512,256]{1,0:T(8,128)(2,1)S(1)} %copy-done.1), channel_id=1, source_target_pairs={{0,1},{1,0},{2,3},{3,2},{4,5},{5,4},{6,7},{7,6},{8,9},{9,8},{10,11... | collective-permute-start | bytes 786440 | tf_op jit(solution)/shard_map/ppermute | solution.py:72
  50.3 17.2 %all-gather.2 = bf16[512,256]{1,0:T(8,128)(2,1)S(1)} all-gather(bf16[128,256]{1,0:T(8,128)(2,1)S(1)} %broadcast_select_fusion), channel_id=4, replica_groups={{0,32,64,96},{2,34,66,98},{4,36,68,100},{6,38,70,102},{8,40,72,104},{10..., dimensions={0}, use_global_device_ids=true | all-gather | bytes 327680 | tf_op jit(solution)/shard_map/all_gather | solution.py:60
  67.6 1.8 %shard_map.85 = bf16[4,2,512,256]{3,2,1,0:T(8,128)(2,1)S(1)} custom-call(s32[1]{0:T(128)} %bitcast.role, bf16[4,4,2,128,256]{4,3,2,1,0:T(8,128)(2,1)S(1)} %all-to-all-done.mine, bf16[256,256]{1,0:T(8,128)(2,1)S(1)} %slice.31.in_inverse, bf16[512,256]{1,0:T(8,128)(2,1)S(1)} %copy-done.1, bf16[512,256]{1,0:T(8,128)(2,1)S(1)} %collective-permute-done.2.other), custom_call_target="tpu_custom_call" | custom-call | flops 1073741824 | bytes 4849664 | tf_op jit(solution)/shard_map/pallas_call | solution.py:92
  69.3 19.0 %all_to_all.20 = bf16[4,2,512,256]{3,2,1,0:T(8,128)(2,1)S(1)} all-to-all(bf16[4,2,512,256]{3,2,1,0:T(8,128)(2,1)S(1)} %shard_map.85), channel_id=1, replica_groups={{0,8,16,24},{2,10,18,26},{4,12,20,28},{6,14,22,30},{32,40,48,56},{34,42..., dimensions={0} | all-to-all | bytes 4194304 | tf_op jit(solution)/shard_map/all_to_all | solution.py:64
  89.7 6.8 %all-to-all-start.2 = ((bf16[4,2,128,256]{3,2,1,0:T(8,128)(2,1)}), bf16[4,2,128,256]{3,2,1,0:T(8,128)(2,1)}, u32[]{:S(2)}, u32[]{:S(2)}) async-start(bf16[4,2,128,256]{3,2,1,0:T(8,128)(2,1)} %pad_maximum_fusion.1), calls=%async_computation.2 | async-start | bytes 1048576 | tf_op jit(solution)/shard_map/all_to_all | solution.py:64
  96.4 4.2 %collective-permute-start.4 = (bf16[4,128,256]{2,1,0:T(8,128)(2,1)S(1)}, bf16[4,128,256]{2,1,0:T(8,128)(2,1)S(1)}, u32[]{:S(2)}, u32[]{:S(2)}) collective-permute-start(bf16[4,128,256]{2,1,0:T(8,128)(2,1)S(1)} %bitcast.23), channel_id=1, source_target_pairs={{0,256},{128,384},{256,0},{384,128},{2,258},{130,386},{258,2},{386... | collective-permute-start | bytes 786440 | tf_op jit(solution)/shard_map/ppermute | solution.py:256
  100.6 2.4 %collective-permute-start.5 = (bf16[4,128,256]{2,1,0:T(8,128)(2,1)S(1)}, bf16[4,128,256]{2,1,0:T(8,128)(2,1)S(1)}, u32[]{:S(2)}, u32[]{:S(2)}) collective-permute-start(bf16[4,128,256]{2,1,0:T(8,128)(2,1)S(1)} %bitcast.24), channel_id=1, source_target_pairs={{0,384},{128,0},{256,128},{384,256},{2,386},{130,2},{258,130},{386... | collective-permute-start | bytes 786440 | tf_op jit(solution)/shard_map/ppermute | solution.py:256
  103.0 2.9 %collective-permute-start.3 = (bf16[4,128,256]{2,1,0:T(8,128)(2,1)S(1)}, bf16[4,128,256]{2,1,0:T(8,128)(2,1)S(1)}, u32[]{:S(2)}, u32[]{:S(2)}) collective-permute-start(bf16[4,128,256]{2,1,0:T(8,128)(2,1)S(1)} %bitcast.25), channel_id=1, source_target_pairs={{0,128},{128,256},{256,384},{384,0},{2,130},{130,258},{258,386},{3... | collective-permute-start | bytes 786440 | tf_op jit(solution)/shard_map/ppermute | solution.py:256
  105.9 7.3 %collective-permute-start.6 = (bf16[4,4,2,128,256]{4,3,2,1,0:T(8,128)(2,1)S(1)}, bf16[4,4,2,128,256]{4,3,2,1,0:T(8,128)(2,1)}, u32[]{:S(2)}, u32[]{:S(2)}) collective-permute-start(bf16[4,4,2,128,256]{4,3,2,1,0:T(8,128)(2,1)S(1)} %all-to-all-done.mine), channel_id=1, source_target_pairs={{0,1},{1,0},{2,3},{3,2},{4,5},{5,4},{6,7},{7,6},{8,9},{9,8},{10,11... | collective-permute-start | bytes 6291464 | tf_op jit(solution)/shard_map/ppermute | solution.py:72
  113.4 5.4 %all-to-all-done.2.parts = bf16[4,2,128,256]{3,2,1,0:T(8,128)(2,1)} async-done(((bf16[4,2,128,256]{3,2,1,0:T(8,128)(2,1)}), bf16[4,2,128,256]{3,2,1,0:T(8,128)(2,1)}, u32[]{:S(2)}, u32[]{:S(2)}) %all-to-all-start.2) | async-done | bytes 524320 | tf_op jit(solution)/shard_map/all_to_all | solution.py:64
  120.0 17.9 %all-gather.3 = bf16[8,128,256]{2,1,0:T(8,128)(2,1)S(1)} all-gather(bf16[2,128,256]{2,1,0:T(8,128)(2,1)S(1)} %shard_map.86), channel_id=5, replica_groups={{0,2,4,6},{8,10,12,14},{16,18,20,22},{24,26,28,30},{32,34,36,38},{40,42..., dimensions={0}, use_global_device_ids=true | all-gather | bytes 655360 | tf_op jit(solution)/shard_map/all_gather | solution.py:60
  139.5 4.6 %all-to-all-start.3 = ((bf16[4,4,2,128,256]{4,3,1,2,0:T(8,128)(2,1)}), bf16[4,4,2,128,256]{4,3,1,2,0:T(8,128)(2,1)}, u32[]{:S(2)}, u32[]{:S(2)}) async-start(bf16[4,4,2,128,256]{4,3,1,2,0:T(8,128)(2,1)} %broadcast_in_dim.5), calls=%async_computation.3 | async-start | bytes 4194304 | tf_op jit(solution)/shard_map/all_to_all | solution.py:64
  144.1 1.9 %collective-permute-start.7 = (bf16[4,4,128,256]{3,2,1,0:T(8,128)(2,1)S(1)}, bf16[4,4,128,256]{3,2,1,0:T(8,128)(2,1)}, u32[]{:S(2)}, u32[]{:S(2)}) collective-permute-start(bf16[4,4,128,256]{3,2,1,0:T(8,128)(2,1)S(1)} %pad_maximum_fusion.late), channel_id=1, source_target_pairs={{0,1},{1,0},{2,3},{3,2},{4,5},{5,4},{6,7},{7,6},{8,9},{9,8},{10,11... | collective-permute-start | bytes 3145736 | tf_op jit(solution)/shard_map/ppermute | solution.py:72
  146.1 2.7 %collective-permute-done.7.their_late = bf16[4,4,128,256]{3,2,1,0:T(8,128)(2,1)} collective-permute-done((bf16[4,4,128,256]{3,2,1,0:T(8,128)(2,1)S(1)}, bf16[4,4,128,256]{3,2,1,0:T(8,128)(2,1)}, u32[]{:S(2)}, u32[]{:S(2)}) %collective-permute-start.7) | collective-permute-done | bytes 1048608 | tf_op jit(solution)/shard_map/ppermute | solution.py:72
  149.9 3.8 %shard_map.87 = (f32[256,128]{1,0:T(8,128)}, f32[512,256]{1,0:T(8,128)}) custom-call(s32[3]{0:T(128)S(1)} %pad_add_fusion.role, bf16[4,4,2,128,256]{4,3,2,1,0:T(8,128)(2,1)S(1)} %all-to-all-done.mine, bf16[4,4,2,128,256]{4,3,2,1,0:T(8,128)(2,1)} %collective-permute-done.6.their, bf16[4,4,128,256]{3,2,1,0:T(8,128)(2,1)S(1)} %pad_maximum_fusion.late, ...), custom_call_target="tpu_custom_call" | custom-call | flops 671088640 | bytes 7602176 | tf_op jit(solution)/shard_map/pallas_call | solution.py:92
  153.6 6.2 %all-to-all-done.3 = bf16[4,4,2,128,256]{4,3,1,2,0:T(8,128)(2,1)} async-done(((bf16[4,4,2,128,256]{4,3,1,2,0:T(8,128)(2,1)}), bf16[4,4,2,128,256]{4,3,1,2,0:T(8,128)(2,1)}, u32[]{:S(2)}, u32[]{:S(2)}) %all-to-all-start.3) | async-done | bytes 2097184 | tf_op jit(solution)/shard_map/all_to_all | solution.py:64
  161.1 2.8 %collective-permute-start.8 = (bf16[4,4,128,256]{3,2,1,0:T(8,128)(2,1)S(1)}, bf16[4,4,128,256]{3,2,1,0:T(8,128)(2,1)S(1)}, u32[]{:S(2)}, u32[]{:S(2)}) collective-permute-start(bf16[4,4,128,256]{3,2,1,0:T(8,128)(2,1)S(1)} %slice_bitcast_fusion), channel_id=1, source_target_pairs={{0,1},{1,0},{2,3},{3,2},{4,5},{5,4},{6,7},{7,6},{8,9},{9,8},{10,11... | collective-permute-start | bytes 3145736 | tf_op jit(solution)/shard_map/ppermute | solution.py:72
  163.9 1.7 %copy.13.mixed = bf16[4,4,2,128,256]{4,3,2,1,0:T(8,128)(2,1)S(1)} copy(bf16[4,4,2,128,256]{4,3,1,2,0:T(8,128)(2,1)} %all-to-all-done.3) | data formatting | bytes 4194304 | tf_op jit(solution)/shard_map/optimization_barrier | solution.py:280
  166.2 1.9 %shard_map.88 = f32[256,256]{1,0:T(8,128)} custom-call(s32[1]{0:T(128)} %bitcast.role, bf16[4,4,2,128,256]{4,3,2,1,0:T(8,128)(2,1)S(1)} %copy.13.mixed, bf16[4,4,128,256]{3,2,1,0:T(8,128)(2,1)S(1)} %collective-permute-done.8.crossed), custom_call_target="tpu_custom_call" | custom-call | flops 268435456 | bytes 3407872 | tf_op jit(solution)/shard_map/pallas_call | solution.py:92
  (33 shorter events, 9.5 us)
Async XLA Ops:
  9.3 4.2 %collective-permute-start = (bf16[2,128,256]{2,1,0:T(8,128)(2,1)S(1)}, bf16[2,128,256]{2,1,0:T(8,128)(2,1)S(1)}, u32[]{:S(2)}, u32[]{:S(2)}) collective-permute-start(bf16[2,128,256]{2,1,0:T(8,128)(2,1)S(1)} %bitcast.27), channel_id=1, source_target_pairs={{0,0},{1,1},{2,2},{3,33},{4,4},{5,65},{6,6},{7,97},{8,8},{9,129},{... | collective-permute-start | bytes 393224 | tf_op jit(solution)/shard_map/ppermute | solution.py:225
  12.7 26.4 %collective-permute-start.1 = (bf16[128,256]{1,0:T(8,128)(2,1)S(1)}, bf16[128,256]{1,0:T(8,128)(2,1)S(1)}, u32[]{:S(2)}, u32[]{:S(2)}) collective-permute-start(bf16[128,256]{1,0:T(8,128)(2,1)S(1)} %get-tuple-element.45), channel_id=1, source_target_pairs={{0,0},{1,1},{2,2},{3,33},{4,4},{5,65},{6,6},{7,97},{8,8},{9,129},{... | collective-permute-start | bytes 196616 | tf_op jit(solution)/shard_map/ppermute | solution.py:230
  40.8 7.6 %copy-start.1 = (bf16[512,256]{1,0:T(8,128)(2,1)S(1)}, bf16[512,256]{1,0:T(8,128)(2,1)}, u32[]{:S(2)}) copy-start(bf16[512,256]{1,0:T(8,128)(2,1)} %out_own.1) | copy-start | bytes 786436
  40.8 26.8 %all-to-all-start = ((bf16[4,4,2,128,256]{4,3,2,1,0:T(8,128)(2,1)}), bf16[4,4,2,128,256]{4,3,2,1,0:T(8,128)(2,1)S(1)}, u32[]{:S(2)}, u32[]{:S(2)}) async-start(bf16[4,4,2,128,256]{4,3,2,1,0:T(8,128)(2,1)} %broadcast_in_dim.4), calls=%async_computation | async-start | bytes 4194304 | tf_op jit(solution)/shard_map/all_to_all | solution.py:64
  48.4 19.2 %collective-permute-start.2 = (bf16[512,256]{1,0:T(8,128)(2,1)S(1)}, bf16[512,256]{1,0:T(8,128)(2,1)S(1)}, u32[]{:S(2)}, u32[]{:S(2)}) collective-permute-start(bf16[512,256]{1,0:T(8,128)(2,1)S(1)} %copy-done.1), channel_id=1, source_target_pairs={{0,1},{1,0},{2,3},{3,2},{4,5},{5,4},{6,7},{7,6},{8,9},{9,8},{10,11... | collective-permute-start | bytes 786440 | tf_op jit(solution)/shard_map/ppermute | solution.py:72
  89.7 29.2 %all-to-all-start.2 = ((bf16[4,2,128,256]{3,2,1,0:T(8,128)(2,1)}), bf16[4,2,128,256]{3,2,1,0:T(8,128)(2,1)}, u32[]{:S(2)}, u32[]{:S(2)}) async-start(bf16[4,2,128,256]{3,2,1,0:T(8,128)(2,1)} %pad_maximum_fusion.1), calls=%async_computation.2 | async-start | bytes 1048576 | tf_op jit(solution)/shard_map/all_to_all | solution.py:64
  96.4 16.8 %collective-permute-start.4 = (bf16[4,128,256]{2,1,0:T(8,128)(2,1)S(1)}, bf16[4,128,256]{2,1,0:T(8,128)(2,1)S(1)}, u32[]{:S(2)}, u32[]{:S(2)}) collective-permute-start(bf16[4,128,256]{2,1,0:T(8,128)(2,1)S(1)} %bitcast.23), channel_id=1, source_target_pairs={{0,256},{128,384},{256,0},{384,128},{2,258},{130,386},{258,2},{386... | collective-permute-start | bytes 786440 | tf_op jit(solution)/shard_map/ppermute | solution.py:256
  100.6 12.6 %collective-permute-start.5 = (bf16[4,128,256]{2,1,0:T(8,128)(2,1)S(1)}, bf16[4,128,256]{2,1,0:T(8,128)(2,1)S(1)}, u32[]{:S(2)}, u32[]{:S(2)}) collective-permute-start(bf16[4,128,256]{2,1,0:T(8,128)(2,1)S(1)} %bitcast.24), channel_id=1, source_target_pairs={{0,384},{128,0},{256,128},{384,256},{2,386},{130,2},{258,130},{386... | collective-permute-start | bytes 786440 | tf_op jit(solution)/shard_map/ppermute | solution.py:256
  103.0 10.3 %collective-permute-start.3 = (bf16[4,128,256]{2,1,0:T(8,128)(2,1)S(1)}, bf16[4,128,256]{2,1,0:T(8,128)(2,1)S(1)}, u32[]{:S(2)}, u32[]{:S(2)}) collective-permute-start(bf16[4,128,256]{2,1,0:T(8,128)(2,1)S(1)} %bitcast.25), channel_id=1, source_target_pairs={{0,128},{128,256},{256,384},{384,0},{2,130},{130,258},{258,386},{3... | collective-permute-start | bytes 786440 | tf_op jit(solution)/shard_map/ppermute | solution.py:256
  105.9 42.9 %collective-permute-start.6 = (bf16[4,4,2,128,256]{4,3,2,1,0:T(8,128)(2,1)S(1)}, bf16[4,4,2,128,256]{4,3,2,1,0:T(8,128)(2,1)}, u32[]{:S(2)}, u32[]{:S(2)}) collective-permute-start(bf16[4,4,2,128,256]{4,3,2,1,0:T(8,128)(2,1)S(1)} %all-to-all-done.mine), channel_id=1, source_target_pairs={{0,1},{1,0},{2,3},{3,2},{4,5},{5,4},{6,7},{7,6},{8,9},{9,8},{10,11... | collective-permute-start | bytes 6291464 | tf_op jit(solution)/shard_map/ppermute | solution.py:72
  139.5 9.3 %copy-start.2 = (f32[256,128]{1,0:T(8,128)S(1)}, f32[256,128]{1,0:T(8,128)}, u32[]{:S(2)}) copy-start(f32[256,128]{1,0:T(8,128)} %in_old.1) | copy-start | bytes 393220
  139.5 20.3 %all-to-all-start.3 = ((bf16[4,4,2,128,256]{4,3,1,2,0:T(8,128)(2,1)}), bf16[4,4,2,128,256]{4,3,1,2,0:T(8,128)(2,1)}, u32[]{:S(2)}, u32[]{:S(2)}) async-start(bf16[4,4,2,128,256]{4,3,1,2,0:T(8,128)(2,1)} %broadcast_in_dim.5), calls=%async_computation.3 | async-start | bytes 4194304 | tf_op jit(solution)/shard_map/all_to_all | solution.py:64
  144.1 4.7 %collective-permute-start.7 = (bf16[4,4,128,256]{3,2,1,0:T(8,128)(2,1)S(1)}, bf16[4,4,128,256]{3,2,1,0:T(8,128)(2,1)}, u32[]{:S(2)}, u32[]{:S(2)}) collective-permute-start(bf16[4,4,128,256]{3,2,1,0:T(8,128)(2,1)S(1)} %pad_maximum_fusion.late), channel_id=1, source_target_pairs={{0,1},{1,0},{2,3},{3,2},{4,5},{5,4},{6,7},{7,6},{8,9},{9,8},{10,11... | collective-permute-start | bytes 3145736 | tf_op jit(solution)/shard_map/ppermute | solution.py:72
  148.8 1.0 copy-start
  161.1 5.0 %collective-permute-start.8 = (bf16[4,4,128,256]{3,2,1,0:T(8,128)(2,1)S(1)}, bf16[4,4,128,256]{3,2,1,0:T(8,128)(2,1)S(1)}, u32[]{:S(2)}, u32[]{:S(2)}) collective-permute-start(bf16[4,4,128,256]{3,2,1,0:T(8,128)(2,1)S(1)} %slice_bitcast_fusion), channel_id=1, source_target_pairs={{0,1},{1,0},{2,3},{3,2},{4,5},{5,4},{6,7},{7,6},{8,9},{9,8},{10,11... | collective-permute-start | bytes 3145736 | tf_op jit(solution)/shard_map/ppermute | solution.py:72

commit v8 on v7

--- a/solution.py
+++ b/solution.py
@@ -161,17 +161,16 @@
 
 
 def natural_body(tokens, role, mixed, crossed, out):
-    @pl.when(pl.program_id(0) == 0)
-    def _():
-        out[...] = jnp.zeros_like(out)
-
-    @pl.when(role[0] == 0)
-    def _():
-        out[...] += dot(flat(mixed[0, :, 0]), flat(crossed[0]), by_rows) / tokens
-
-    @pl.when(role[0] == 1)
-    def _():
-        out[...] += dot(flat(crossed[0]), flat(mixed[0, :, 1]), by_rows) / tokens
+    def total(left, right):
+        return sum(dot(left(i), right(i), by_rows) for i in range(SIDE)) / tokens
+
+    @pl.when(role[0] == 0)
+    def _():
+        out[...] = total(lambda i: flat(mixed[i, :, 0]), lambda i: flat(crossed[i]))
+
+    @pl.when(role[0] == 1)
+    def _():
+        out[...] = total(lambda i: flat(crossed[i]), lambda i: flat(mixed[i, :, 1]))
 
 
 def running_body(role, mine, their, late, their_late, in_old, out_old, in_new, out_new):
@@ -286,14 +285,6 @@
         mixed,
         crossed,
         flops=2 * tokens * wide * wide,
-        steps=SIDE,
-        blocks=(
-            [
-                block_at((1, SIDE, CORES, rows, wide), 0),
-                block_at((1, SIDE, rows, wide), 0),
-            ],
-            block_at((wide, wide), None),
-        ),
     )
     return (input_running, output_running, natural_gradient)
 

time: 169 us -> 168 us (level)
  no operation moved by 1% of the time
where the time goes in v8:
time: 168 us; the launch traced here: 167 us
  blocking collectives  90.4 us (54%)
  starting transfers between devices  43.6 us (26%)
  waiting for transfers between devices  14.9 us (9%)
  Pallas kernels  7.86 us (5%)
  local copies, waits for them, and re-layouts  7.41 us (4%)
  other arithmetic  2.38 us (1%)
    all_gather x3, blocking collectives, gather(): lax.all_gather(block, ALL, axis_index_groups=groups, axis=0, tiled=False)  60.8 us
    all_to_all x1, blocking collectives, exchange(): return lax.all_to_all(parts, ALL, 0, 0, axis_index_groups=groups)  19 us
    all_to_all x3, starting transfers between devices, exchange(): return lax.all_to_all(parts, ALL, 0, 0, axis_index_groups=groups)  18.9 us
    ppermute x4, starting transfers between devices, core_swap(): return lax.ppermute(block, 'core', [(0, 1), (1, 0)])  13.9 us
    all_to_all x3, waiting for transfers between devices, exchange(): return lax.all_to_all(parts, ALL, 0, 0, axis_index_groups=groups)  11.7 us
    ppermute x3, starting transfers between devices, per_device(): lax.ppermute(late, ALL, ring_pairs(turn))  9.47 us
    all_gather x1, blocking collectives, per_device(): grads_pair = lax.all_gather(output_grads, 'core', axis=0, tiled=False)  8.64 us
    pallas_call x4, Pallas kernels, local_call(): pl.pallas_call(body, grid=grid, out_shape=out_shape, in_specs=[pl.BlockSp...  7.86 us
  transfers between devices with their start and end apart: 12, of which 4 were waited for; matrix products, arithmetic and copies ran while one was open for 3% of the time, Pallas kernels for 3%

profile of v8, /device:TPU:1, one launch (start us, length us, event | category | flops | bytes accessed | tf_op | source)
XLA Modules:
  0.0 167.4 jit_solution(9309797851521033699)
XLA Ops:
  0.6 8.6 %all-gather = bf16[256,256]{1,0:T(8,128)(2,1)S(1)} all-gather(bf16[128,256]{1,0:T(8,128)(2,1)} %param.7), channel_id=2, replica_groups=mesh['x'=4,'zh'=4,'y'=4,'zl'=4,'core'=2] {'core'}, dimensions={0}, use_global_device_ids=true | all-gather | bytes 196608 | tf_op jit(solution)/shard_map/all_gather | solution.py:223
  10.8 1.9 %all_gather.29 = bf16[384,256]{1,0:T(8,128)(2,1)S(1)} all-gather(bf16[384,128]{1,0:T(8,128)(2,1)S(1)} %pad_maximum_fusion.2), channel_id=1, replica_groups=mesh['x'=4,'zh'=4,'y'=4,'zl'=4,'core'=2] {'core'}, dimensions={1}, use_global_device_ids=true | all-gather | bytes 294912 | tf_op jit(solution)/shard_map/all_gather | solution.py:227
  13.5 25.7 %all-gather.1 = bf16[8,128,256]{2,1,0:T(8,128)(2,1)S(1)} all-gather(bf16[2,128,256]{2,1,0:T(8,128)(2,1)S(1)} %maximum_select_fusion), channel_id=3, replica_groups={{0,32,64,96},{2,34,66,98},{4,36,68,100},{6,38,70,102},{8,40,72,104},{10..., dimensions={0}, use_global_device_ids=true | all-gather | bytes 655360 | tf_op jit(solution)/shard_map/all_gather | solution.py:60
  39.2 1.6 broadcast_in_dim.4
  40.8 7.6 %all-to-all-start = ((bf16[4,4,2,128,256]{4,3,2,1,0:T(8,128)(2,1)}), bf16[4,4,2,128,256]{4,3,2,1,0:T(8,128)(2,1)S(1)}, u32[]{:S(2)}, u32[]{:S(2)}) async-start(bf16[4,4,2,128,256]{4,3,2,1,0:T(8,128)(2,1)} %broadcast_in_dim.4), calls=%async_computation | async-start | bytes 4194304 | tf_op jit(solution)/shard_map/all_to_all | solution.py:64
  48.4 1.9 %collective-permute-start.2 = (bf16[512,256]{1,0:T(8,128)(2,1)S(1)}, bf16[512,256]{1,0:T(8,128)(2,1)S(1)}, u32[]{:S(2)}, u32[]{:S(2)}) collective-permute-start(bf16[512,256]{1,0:T(8,128)(2,1)S(1)} %copy-done.1), channel_id=1, source_target_pairs={{0,1},{1,0},{2,3},{3,2},{4,5},{5,4},{6,7},{7,6},{8,9},{9,8},{10,11... | collective-permute-start | bytes 786440 | tf_op jit(solution)/shard_map/ppermute | solution.py:72
  50.3 17.2 %all-gather.2 = bf16[512,256]{1,0:T(8,128)(2,1)S(1)} all-gather(bf16[128,256]{1,0:T(8,128)(2,1)S(1)} %broadcast_select_fusion), channel_id=4, replica_groups={{0,32,64,96},{2,34,66,98},{4,36,68,100},{6,38,70,102},{8,40,72,104},{10..., dimensions={0}, use_global_device_ids=true | all-gather | bytes 327680 | tf_op jit(solution)/shard_map/all_gather | solution.py:60
  67.6 1.8 %shard_map.85 = bf16[4,2,512,256]{3,2,1,0:T(8,128)(2,1)S(1)} custom-call(s32[1]{0:T(128)} %bitcast.role, bf16[4,4,2,128,256]{4,3,2,1,0:T(8,128)(2,1)S(1)} %all-to-all-done.mine, bf16[256,256]{1,0:T(8,128)(2,1)S(1)} %slice.31.in_inverse, bf16[512,256]{1,0:T(8,128)(2,1)S(1)} %copy-done.1, bf16[512,256]{1,0:T(8,128)(2,1)S(1)} %collective-permute-done.2.other), custom_call_target="tpu_custom_call" | custom-call | flops 1073741824 | bytes 4849664 | tf_op jit(solution)/shard_map/pallas_call | solution.py:92
  69.3 19.0 %all_to_all.20 = bf16[4,2,512,256]{3,2,1,0:T(8,128)(2,1)S(1)} all-to-all(bf16[4,2,512,256]{3,2,1,0:T(8,128)(2,1)S(1)} %shard_map.85), channel_id=1, replica_groups={{0,8,16,24},{2,10,18,26},{4,12,20,28},{6,14,22,30},{32,40,48,56},{34,42..., dimensions={0} | all-to-all | bytes 4194304 | tf_op jit(solution)/shard_map/all_to_all | solution.py:64
  89.7 6.8 %all-to-all-start.2 = ((bf16[4,2,128,256]{3,2,1,0:T(8,128)(2,1)}), bf16[4,2,128,256]{3,2,1,0:T(8,128)(2,1)}, u32[]{:S(2)}, u32[]{:S(2)}) async-start(bf16[4,2,128,256]{3,2,1,0:T(8,128)(2,1)} %pad_maximum_fusion.1), calls=%async_computation.2 | async-start | bytes 1048576 | tf_op jit(solution)/shard_map/all_to_all | solution.py:64
  96.4 4.2 %collective-permute-start.4 = (bf16[4,128,256]{2,1,0:T(8,128)(2,1)S(1)}, bf16[4,128,256]{2,1,0:T(8,128)(2,1)S(1)}, u32[]{:S(2)}, u32[]{:S(2)}) collective-permute-start(bf16[4,128,256]{2,1,0:T(8,128)(2,1)S(1)} %bitcast.23), channel_id=1, source_target_pairs={{0,256},{128,384},{256,0},{384,128},{2,258},{130,386},{258,2},{386... | collective-permute-start | bytes 786440 | tf_op jit(solution)/shard_map/ppermute | solution.py:255
  100.6 2.4 %collective-permute-start.5 = (bf16[4,128,256]{2,1,0:T(8,128)(2,1)S(1)}, bf16[4,128,256]{2,1,0:T(8,128)(2,1)S(1)}, u32[]{:S(2)}, u32[]{:S(2)}) collective-permute-start(bf16[4,128,256]{2,1,0:T(8,128)(2,1)S(1)} %bitcast.24), channel_id=1, source_target_pairs={{0,384},{128,0},{256,128},{384,256},{2,386},{130,2},{258,130},{386... | collective-permute-start | bytes 786440 | tf_op jit(solution)/shard_map/ppermute | solution.py:255
  103.0 2.9 %collective-permute-start.3 = (bf16[4,128,256]{2,1,0:T(8,128)(2,1)S(1)}, bf16[4,128,256]{2,1,0:T(8,128)(2,1)S(1)}, u32[]{:S(2)}, u32[]{:S(2)}) collective-permute-start(bf16[4,128,256]{2,1,0:T(8,128)(2,1)S(1)} %bitcast.25), channel_id=1, source_target_pairs={{0,128},{128,256},{256,384},{384,0},{2,130},{130,258},{258,386},{3... | collective-permute-start | bytes 786440 | tf_op jit(solution)/shard_map/ppermute | solution.py:255
  105.9 7.3 %collective-permute-start.6 = (bf16[4,4,2,128,256]{4,3,2,1,0:T(8,128)(2,1)S(1)}, bf16[4,4,2,128,256]{4,3,2,1,0:T(8,128)(2,1)}, u32[]{:S(2)}, u32[]{:S(2)}) collective-permute-start(bf16[4,4,2,128,256]{4,3,2,1,0:T(8,128)(2,1)S(1)} %all-to-all-done.mine), channel_id=1, source_target_pairs={{0,1},{1,0},{2,3},{3,2},{4,5},{5,4},{6,7},{7,6},{8,9},{9,8},{10,11... | collective-permute-start | bytes 6291464 | tf_op jit(solution)/shard_map/ppermute | solution.py:72
  113.4 5.4 %all-to-all-done.2.parts = bf16[4,2,128,256]{3,2,1,0:T(8,128)(2,1)} async-done(((bf16[4,2,128,256]{3,2,1,0:T(8,128)(2,1)}), bf16[4,2,128,256]{3,2,1,0:T(8,128)(2,1)}, u32[]{:S(2)}, u32[]{:S(2)}) %all-to-all-start.2) | async-done | bytes 524320 | tf_op jit(solution)/shard_map/all_to_all | solution.py:64
  120.0 17.9 %all-gather.3 = bf16[8,128,256]{2,1,0:T(8,128)(2,1)S(1)} all-gather(bf16[2,128,256]{2,1,0:T(8,128)(2,1)S(1)} %shard_map.86), channel_id=5, replica_groups={{0,2,4,6},{8,10,12,14},{16,18,20,22},{24,26,28,30},{32,34,36,38},{40,42..., dimensions={0}, use_global_device_ids=true | all-gather | bytes 655360 | tf_op jit(solution)/shard_map/all_gather | solution.py:60
  137.9 1.6 broadcast_in_dim.5
  139.5 4.6 %all-to-all-start.3 = ((bf16[4,4,2,128,256]{4,3,1,2,0:T(8,128)(2,1)}), bf16[4,4,2,128,256]{4,3,1,2,0:T(8,128)(2,1)}, u32[]{:S(2)}, u32[]{:S(2)}) async-start(bf16[4,4,2,128,256]{4,3,1,2,0:T(8,128)(2,1)} %broadcast_in_dim.5), calls=%async_computation.3 | async-start | bytes 4194304 | tf_op jit(solution)/shard_map/all_to_all | solution.py:64
  144.1 1.9 %collective-permute-start.7 = (bf16[4,4,128,256]{3,2,1,0:T(8,128)(2,1)S(1)}, bf16[4,4,128,256]{3,2,1,0:T(8,128)(2,1)}, u32[]{:S(2)}, u32[]{:S(2)}) collective-permute-start(bf16[4,4,128,256]{3,2,1,0:T(8,128)(2,1)S(1)} %pad_maximum_fusion.late), channel_id=1, source_target_pairs={{0,1},{1,0},{2,3},{3,2},{4,5},{5,4},{6,7},{7,6},{8,9},{9,8},{10,11... | collective-permute-start | bytes 3145736 | tf_op jit(solution)/shard_map/ppermute | solution.py:72
  146.1 2.7 %collective-permute-done.7.their_late = bf16[4,4,128,256]{3,2,1,0:T(8,128)(2,1)} collective-permute-done((bf16[4,4,128,256]{3,2,1,0:T(8,128)(2,1)S(1)}, bf16[4,4,128,256]{3,2,1,0:T(8,128)(2,1)}, u32[]{:S(2)}, u32[]{:S(2)}) %collective-permute-start.7) | collective-permute-done | bytes 1048608 | tf_op jit(solution)/shard_map/ppermute | solution.py:72
  149.9 3.8 %shard_map.87 = (f32[256,128]{1,0:T(8,128)}, f32[512,256]{1,0:T(8,128)}) custom-call(s32[3]{0:T(128)S(1)} %pad_add_fusion.role, bf16[4,4,2,128,256]{4,3,2,1,0:T(8,128)(2,1)S(1)} %all-to-all-done.mine, bf16[4,4,2,128,256]{4,3,2,1,0:T(8,128)(2,1)} %collective-permute-done.6.their, bf16[4,4,128,256]{3,2,1,0:T(8,128)(2,1)S(1)} %pad_maximum_fusion.late, ...), custom_call_target="tpu_custom_call" | custom-call | flops 671088640 | bytes 7602176 | tf_op jit(solution)/shard_map/pallas_call | solution.py:92
  153.6 6.2 %all-to-all-done.3 = bf16[4,4,2,128,256]{4,3,1,2,0:T(8,128)(2,1)} async-done(((bf16[4,4,2,128,256]{4,3,1,2,0:T(8,128)(2,1)}), bf16[4,4,2,128,256]{4,3,1,2,0:T(8,128)(2,1)}, u32[]{:S(2)}, u32[]{:S(2)}) %all-to-all-start.3) | async-done | bytes 2097184 | tf_op jit(solution)/shard_map/all_to_all | solution.py:64
  161.1 2.8 %collective-permute-start.8 = (bf16[4,4,128,256]{3,2,1,0:T(8,128)(2,1)S(1)}, bf16[4,4,128,256]{3,2,1,0:T(8,128)(2,1)S(1)}, u32[]{:S(2)}, u32[]{:S(2)}) collective-permute-start(bf16[4,4,128,256]{3,2,1,0:T(8,128)(2,1)S(1)} %slice_bitcast_fusion), channel_id=1, source_target_pairs={{0,1},{1,0},{2,3},{3,2},{4,5},{5,4},{6,7},{7,6},{8,9},{9,8},{10,11... | collective-permute-start | bytes 3145736 | tf_op jit(solution)/shard_map/ppermute | solution.py:72
  163.9 1.7 %copy.13.mixed = bf16[4,4,2,128,256]{4,3,2,1,0:T(8,128)(2,1)S(1)} copy(bf16[4,4,2,128,256]{4,3,1,2,0:T(8,128)(2,1)} %all-to-all-done.3) | data formatting | bytes 4194304 | tf_op jit(solution)/shard_map/optimization_barrier | solution.py:279
  (33 shorter events, 9.1 us)
Async XLA Ops:
  9.3 4.2 %collective-permute-start = (bf16[2,128,256]{2,1,0:T(8,128)(2,1)S(1)}, bf16[2,128,256]{2,1,0:T(8,128)(2,1)S(1)}, u32[]{:S(2)}, u32[]{:S(2)}) collective-permute-start(bf16[2,128,256]{2,1,0:T(8,128)(2,1)S(1)} %bitcast.27), channel_id=1, source_target_pairs={{0,0},{1,1},{2,2},{3,33},{4,4},{5,65},{6,6},{7,97},{8,8},{9,129},{... | collective-permute-start | bytes 393224 | tf_op jit(solution)/shard_map/ppermute | solution.py:224
  12.7 26.4 %collective-permute-start.1 = (bf16[128,256]{1,0:T(8,128)(2,1)S(1)}, bf16[128,256]{1,0:T(8,128)(2,1)S(1)}, u32[]{:S(2)}, u32[]{:S(2)}) collective-permute-start(bf16[128,256]{1,0:T(8,128)(2,1)S(1)} %get-tuple-element.45), channel_id=1, source_target_pairs={{0,0},{1,1},{2,2},{3,33},{4,4},{5,65},{6,6},{7,97},{8,8},{9,129},{... | collective-permute-start | bytes 196616 | tf_op jit(solution)/shard_map/ppermute | solution.py:229
  40.8 7.6 %copy-start.1 = (bf16[512,256]{1,0:T(8,128)(2,1)S(1)}, bf16[512,256]{1,0:T(8,128)(2,1)}, u32[]{:S(2)}) copy-start(bf16[512,256]{1,0:T(8,128)(2,1)} %out_own.1) | copy-start | bytes 786436
  40.8 26.8 %all-to-all-start = ((bf16[4,4,2,128,256]{4,3,2,1,0:T(8,128)(2,1)}), bf16[4,4,2,128,256]{4,3,2,1,0:T(8,128)(2,1)S(1)}, u32[]{:S(2)}, u32[]{:S(2)}) async-start(bf16[4,4,2,128,256]{4,3,2,1,0:T(8,128)(2,1)} %broadcast_in_dim.4), calls=%async_computation | async-start | bytes 4194304 | tf_op jit(solution)/shard_map/all_to_all | solution.py:64
  48.4 19.2 %collective-permute-start.2 = (bf16[512,256]{1,0:T(8,128)(2,1)S(1)}, bf16[512,256]{1,0:T(8,128)(2,1)S(1)}, u32[]{:S(2)}, u32[]{:S(2)}) collective-permute-start(bf16[512,256]{1,0:T(8,128)(2,1)S(1)} %copy-done.1), channel_id=1, source_target_pairs={{0,1},{1,0},{2,3},{3,2},{4,5},{5,4},{6,7},{7,6},{8,9},{9,8},{10,11... | collective-permute-start | bytes 786440 | tf_op jit(solution)/shard_map/ppermute | solution.py:72
  89.7 29.2 %all-to-all-start.2 = ((bf16[4,2,128,256]{3,2,1,0:T(8,128)(2,1)}), bf16[4,2,128,256]{3,2,1,0:T(8,128)(2,1)}, u32[]{:S(2)}, u32[]{:S(2)}) async-start(bf16[4,2,128,256]{3,2,1,0:T(8,128)(2,1)} %pad_maximum_fusion.1), calls=%async_computation.2 | async-start | bytes 1048576 | tf_op jit(solution)/shard_map/all_to_all | solution.py:64
  96.4 16.8 %collective-permute-start.4 = (bf16[4,128,256]{2,1,0:T(8,128)(2,1)S(1)}, bf16[4,128,256]{2,1,0:T(8,128)(2,1)S(1)}, u32[]{:S(2)}, u32[]{:S(2)}) collective-permute-start(bf16[4,128,256]{2,1,0:T(8,128)(2,1)S(1)} %bitcast.23), channel_id=1, source_target_pairs={{0,256},{128,384},{256,0},{384,128},{2,258},{130,386},{258,2},{386... | collective-permute-start | bytes 786440 | tf_op jit(solution)/shard_map/ppermute | solution.py:255
  100.6 12.6 %collective-permute-start.5 = (bf16[4,128,256]{2,1,0:T(8,128)(2,1)S(1)}, bf16[4,128,256]{2,1,0:T(8,128)(2,1)S(1)}, u32[]{:S(2)}, u32[]{:S(2)}) collective-permute-start(bf16[4,128,256]{2,1,0:T(8,128)(2,1)S(1)} %bitcast.24), channel_id=1, source_target_pairs={{0,384},{128,0},{256,128},{384,256},{2,386},{130,2},{258,130},{386... | collective-permute-start | bytes 786440 | tf_op jit(solution)/shard_map/ppermute | solution.py:255
  103.0 10.3 %collective-permute-start.3 = (bf16[4,128,256]{2,1,0:T(8,128)(2,1)S(1)}, bf16[4,128,256]{2,1,0:T(8,128)(2,1)S(1)}, u32[]{:S(2)}, u32[]{:S(2)}) collective-permute-start(bf16[4,128,256]{2,1,0:T(8,128)(2,1)S(1)} %bitcast.25), channel_id=1, source_target_pairs={{0,128},{128,256},{256,384},{384,0},{2,130},{130,258},{258,386},{3... | collective-permute-start | bytes 786440 | tf_op jit(solution)/shard_map/ppermute | solution.py:255
  105.9 42.9 %collective-permute-start.6 = (bf16[4,4,2,128,256]{4,3,2,1,0:T(8,128)(2,1)S(1)}, bf16[4,4,2,128,256]{4,3,2,1,0:T(8,128)(2,1)}, u32[]{:S(2)}, u32[]{:S(2)}) collective-permute-start(bf16[4,4,2,128,256]{4,3,2,1,0:T(8,128)(2,1)S(1)} %all-to-all-done.mine), channel_id=1, source_target_pairs={{0,1},{1,0},{2,3},{3,2},{4,5},{5,4},{6,7},{7,6},{8,9},{9,8},{10,11... | collective-permute-start | bytes 6291464 | tf_op jit(solution)/shard_map/ppermute | solution.py:72
  139.5 9.3 %copy-start.2 = (f32[256,128]{1,0:T(8,128)S(1)}, f32[256,128]{1,0:T(8,128)}, u32[]{:S(2)}) copy-start(f32[256,128]{1,0:T(8,128)} %in_old.1) | copy-start | bytes 393220
  139.5 20.3 %all-to-all-start.3 = ((bf16[4,4,2,128,256]{4,3,1,2,0:T(8,128)(2,1)}), bf16[4,4,2,128,256]{4,3,1,2,0:T(8,128)(2,1)}, u32[]{:S(2)}, u32[]{:S(2)}) async-start(bf16[4,4,2,128,256]{4,3,1,2,0:T(8,128)(2,1)} %broadcast_in_dim.5), calls=%async_computation.3 | async-start | bytes 4194304 | tf_op jit(solution)/shard_map/all_to_all | solution.py:64
  144.1 4.7 %collective-permute-start.7 = (bf16[4,4,128,256]{3,2,1,0:T(8,128)(2,1)S(1)}, bf16[4,4,128,256]{3,2,1,0:T(8,128)(2,1)}, u32[]{:S(2)}, u32[]{:S(2)}) collective-permute-start(bf16[4,4,128,256]{3,2,1,0:T(8,128)(2,1)S(1)} %pad_maximum_fusion.late), channel_id=1, source_target_pairs={{0,1},{1,0},{2,3},{3,2},{4,5},{5,4},{6,7},{7,6},{8,9},{9,8},{10,11... | collective-permute-start | bytes 3145736 | tf_op jit(solution)/shard_map/ppermute | solution.py:72
  148.8 1.0 copy-start
  161.1 5.0 %collective-permute-start.8 = (bf16[4,4,128,256]{3,2,1,0:T(8,128)(2,1)S(1)}, bf16[4,4,128,256]{3,2,1,0:T(8,128)(2,1)S(1)}, u32[]{:S(2)}, u32[]{:S(2)}) collective-permute-start(bf16[4,4,128,256]{3,2,1,0:T(8,128)(2,1)S(1)} %slice_bitcast_fusion), channel_id=1, source_target_pairs={{0,1},{1,0},{2,3},{3,2},{4,5},{5,4},{6,7},{7,6},{8,9},{9,8},{10,11... | collective-permute-start | bytes 3145736 | tf_op jit(solution)/shard_map/ppermute | solution.py:72

commit v9 on v8

--- a/solution.py
+++ b/solution.py
@@ -113,8 +113,8 @@
     return high, (value - high.astype(f32)).astype(bf16)
 
 
-def partial_body(role, mine, in_inverse, out_own, other, out):
-    deep = out_own.shape[0] // CORES
+def partial_body(role, mine, in_inverse, out_inverse, out):
+    deep = out_inverse.shape[1] // CORES
 
     @pl.when(role[0] == 0)
     def _():
@@ -130,8 +130,9 @@
         @pl.loop(0, SIDE)
         def _(i):
             near, far = flat(mine[i, :, 0]), flat(mine[i, :, 1])
-            for half, inverse in ((0, other), (1, out_own)):
-                part = dot(near, inverse[:deep], plain) + dot(far, inverse[deep:], plain)
+            for half in range(CORES):
+                part = dot(near, out_inverse[half, :deep], plain)
+                part = part + dot(far, out_inverse[half, deep:], plain)
                 out[i, half] = part.astype(bf16)
 
 
@@ -221,19 +222,20 @@
     back_xy = role_groups("y", "x")
 
     grads_pair = lax.all_gather(output_grads, "core", axis=0, tiled=False)
-    grads_moved = lax.ppermute(grads_pair, ALL, swap_pairs())
-    grads_pair, layer_inputs, input_inverse = tied((grads_pair, layer_inputs, input_inverse))
     input_pair = jnp.concatenate([layer_inputs, input_inverse])
     input_pair = lax.all_gather(input_pair, "core", axis=1, tiled=True)
+    grads_pair, input_pair = tied((grads_pair, input_pair))
     input_pair, in_inverse = input_pair[:rows], input_pair[rows:]
-    inputs_moved = lax.ppermute(input_pair, ALL, swap_pairs())
+    moved = jnp.concatenate([grads_pair, input_pair[None]])
+    output_inverse, moved = tied((output_inverse, moved))
+    moved = lax.ppermute(moved, ALL, swap_pairs())
+    out_inverse = lax.all_gather(output_inverse, "core", axis=0, tiled=False)
+    moved, grads_pair, out_inverse = tied((moved, grads_pair, out_inverse))
+    grads_moved, inputs_moved = moved[:CORES], moved[CORES]
     block = jnp.where(first, jnp.stack([input_pair, grads_pair[0]]), grads_moved)
     block = gather(block, out_z)
-    block, late, inputs_moved, other = tied(
-        (block, grads_pair[1], inputs_moved, output_inverse)
-    )
+    block, late, inputs_moved = tied((block, grads_pair[1], inputs_moved))
     mine = gather_direct(block, out_xy)
-    other = core_swap(other)
     late = gather(jnp.where(first, late, inputs_moved), out_z)
     mine, late = tied((mine, late))
 
@@ -243,8 +245,7 @@
         role,
         mine,
         in_inverse,
-        output_inverse,
-        other,
+        out_inverse,
         flops=2 * tokens * 4 * wide * wide,
     )
     part = exchange(part, back_xy)

time: 168 us -> 168 us (level); the launches traced: 167 us -> 165 us
  waiting for transfers between devices: 14.9 us -> 19.8 us
  starting transfers between devices: 43.6 us -> 38.8 us
  blocking collectives: 90.4 us -> 88.3 us
    all_gather x1, blocking collectives: 8.64 us -> 2.11 us  [per_device(): grads_pair = lax.all_gather(output_grads, 'core', axis=0, tiled=False)]
    all_gather x1, blocking collectives: 1.94 us -> 8.46 us  [per_device(): input_pair = lax.all_gather(input_pair, 'core', axis=1, tiled=True)]
    ppermute x4 -> x3, starting transfers between devices: 13.9 us -> 7.56 us  [core_swap(): return lax.ppermute(block, 'core', [(0, 1), (1, 0)])]
    all_gather x3, blocking collectives: 60.8 us -> 56.3 us  [gather(): lax.all_gather(block, ALL, axis_index_groups=groups, axis=0, tiled=False)]
    all_to_all x3, starting transfers between devices: 18.9 us -> 22.1 us  [exchange(): return lax.all_to_all(parts, ALL, 0, 0, axis_index_groups=groups)]
    all_to_all x3, waiting for transfers between devices: 11.7 us -> 14.3 us  [exchange(): return lax.all_to_all(parts, ALL, 0, 0, axis_index_groups=groups)]
    all_gather x0 -> x1, blocking collectives: none -> 2.39 us  [per_device(): out_inverse = lax.all_gather(output_inverse, 'core', axis=0, tiled=False)]
    ppermute x3, waiting for transfers between devices: 0.01 us -> 2.36 us  [per_device(): lax.ppermute(late, ALL, ring_pairs(turn))]
  transfers between devices with their start and end apart: 12 -> 10, of which waited for: 4 -> 6; matrix products, arithmetic and copies ran while one was open for 3% -> 2% of each run, Pallas kernels for 3% -> 3%
where the time goes in v9:
time: 168 us; the launch traced here: 165 us
  blocking collectives  88.3 us (53%)
  starting transfers between devices  38.8 us (23%)
  waiting for transfers between devices  19.8 us (12%)
  Pallas kernels  7.84 us (5%)
  local copies, waits for them, and re-layouts  7.37 us (4%)
  other arithmetic  2.4 us (1%)
    all_gather x3, blocking collectives, gather(): lax.all_gather(block, ALL, axis_index_groups=groups, axis=0, tiled=False)  56.3 us
    all_to_all x3, starting transfers between devices, exchange(): return lax.all_to_all(parts, ALL, 0, 0, axis_index_groups=groups)  22.1 us
    all_to_all x1, blocking collectives, exchange(): return lax.all_to_all(parts, ALL, 0, 0, axis_index_groups=groups)  19.1 us
    all_to_all x3, waiting for transfers between devices, exchange(): return lax.all_to_all(parts, ALL, 0, 0, axis_index_groups=groups)  14.3 us
    all_gather x1, blocking collectives, per_device(): input_pair = lax.all_gather(input_pair, 'core', axis=1, tiled=True)  8.46 us
    ppermute x3, starting transfers between devices, per_device(): lax.ppermute(late, ALL, ring_pairs(turn))  8.4 us
    pallas_call x4, Pallas kernels, local_call(): pl.pallas_call(body, grid=grid, out_shape=out_shape, in_specs=[pl.BlockSp...  7.84 us
    ppermute x3, starting transfers between devices, core_swap(): return lax.ppermute(block, 'core', [(0, 1), (1, 0)])  7.56 us
  transfers between devices with their start and end apart: 10, of which 6 were waited for; matrix products, arithmetic and copies ran while one was open for 2% of the time, Pallas kernels for 3%

profile of v9, /device:TPU:1, one launch (start us, length us, event | category | flops | bytes accessed | tf_op | source)
XLA Modules:
  0.0 165.4 jit_solution(13229944157344735253)
XLA Ops:
  1.5 8.5 %all_gather.35 = bf16[384,256]{1,0:T(8,128)(2,1)S(1)} all-gather(bf16[384,128]{1,0:T(8,128)(2,1)S(1)} %pad_maximum_fusion.3), channel_id=1, replica_groups=mesh['x'=4,'zh'=4,'y'=4,'zl'=4,'core'=2] {'core'}, dimensions={1}, use_global_device_ids=true | all-gather | bytes 294912 | tf_op jit(solution)/shard_map/all_gather | solution.py:226
  9.9 2.1 %all-gather = bf16[256,256]{1,0:T(8,128)(2,1)S(1)} all-gather(bf16[128,256]{1,0:T(8,128)(2,1)} %param.7), channel_id=2, replica_groups=mesh['x'=4,'zh'=4,'y'=4,'zl'=4,'core'=2] {'core'}, dimensions={0}, use_global_device_ids=true | all-gather | bytes 196608 | tf_op jit(solution)/shard_map/all_gather | solution.py:224
  12.8 2.4 %all-gather.1 = bf16[1024,256]{1,0:T(8,128)(2,1)S(1)} all-gather(bf16[512,256]{1,0:T(8,128)(2,1)} %param.11), channel_id=3, replica_groups=mesh['x'=4,'zh'=4,'y'=4,'zl'=4,'core'=2] {'core'}, dimensions={0}, use_global_device_ids=true | all-gather | bytes 786432 | tf_op jit(solution)/shard_map/all_gather | solution.py:232
  15.2 26.3 %all-gather.2 = bf16[8,128,256]{2,1,0:T(8,128)(2,1)S(1)} all-gather(bf16[2,128,256]{2,1,0:T(8,128)(2,1)S(1)} %maximum_select_fusion), channel_id=4, replica_groups={{0,32,64,96},{2,34,66,98},{4,36,68,100},{6,38,70,102},{8,40,72,104},{10..., dimensions={0}, use_global_device_ids=true | all-gather | bytes 655360 | tf_op jit(solution)/shard_map/all_gather | solution.py:60
  43.1 5.9 %all-to-all-start = ((bf16[4,4,2,128,256]{4,3,2,1,0:T(8,128)(2,1)}), bf16[4,4,2,128,256]{4,3,2,1,0:T(8,128)(2,1)S(1)}, u32[]{:S(2)}, u32[]{:S(2)}) async-start(bf16[4,4,2,128,256]{4,3,2,1,0:T(8,128)(2,1)} %broadcast_in_dim.4), calls=%async_computation | async-start | bytes 4194304 | tf_op jit(solution)/shard_map/all_to_all | solution.py:64
  49.1 11.3 %all-gather.3 = bf16[512,256]{1,0:T(8,128)(2,1)S(1)} all-gather(bf16[128,256]{1,0:T(8,128)(2,1)S(1)} %broadcast_select_fusion), channel_id=5, replica_groups={{0,32,64,96},{2,34,66,98},{4,36,68,100},{6,38,70,102},{8,40,72,104},{10..., dimensions={0}, use_global_device_ids=true | all-gather | bytes 327680 | tf_op jit(solution)/shard_map/all_gather | solution.py:60
  60.3 4.4 %all-to-all-done.mine = bf16[4,4,2,128,256]{4,3,2,1,0:T(8,128)(2,1)S(1)} async-done(((bf16[4,4,2,128,256]{4,3,2,1,0:T(8,128)(2,1)}), bf16[4,4,2,128,256]{4,3,2,1,0:T(8,128)(2,1)S(1)}, u32[]{:S(2)}, u32[]{:S(2)}) %all-to-all-start) | async-done | bytes 2097184 | tf_op jit(solution)/shard_map/all_to_all | solution.py:64
  64.7 1.8 %shard_map.85 = bf16[4,2,512,256]{3,2,1,0:T(8,128)(2,1)S(1)} custom-call(s32[1]{0:T(128)} %bitcast.role, bf16[4,4,2,128,256]{4,3,2,1,0:T(8,128)(2,1)S(1)} %all-to-all-done.mine, bf16[256,256]{1,0:T(8,128)(2,1)S(1)} %slice.34.in_inverse, bf16[2,512,256]{2,1,0:T(8,128)(2,1)S(1)} %bitcast.22), custom_call_target="tpu_custom_call" | custom-call | flops 1073741824 | bytes 4849664 | tf_op jit(solution)/shard_map/pallas_call | solution.py:92
  66.4 19.1 %all_to_all.20 = bf16[4,2,512,256]{3,2,1,0:T(8,128)(2,1)S(1)} all-to-all(bf16[4,2,512,256]{3,2,1,0:T(8,128)(2,1)S(1)} %shard_map.85), channel_id=1, replica_groups={{0,8,16,24},{2,10,18,26},{4,12,20,28},{6,14,22,30},{32,40,48,56},{34,42..., dimensions={0} | all-to-all | bytes 4194304 | tf_op jit(solution)/shard_map/all_to_all | solution.py:64
  86.9 11.7 %all-to-all-start.2 = ((bf16[4,2,128,256]{3,2,1,0:T(8,128)(2,1)}), bf16[4,2,128,256]{3,2,1,0:T(8,128)(2,1)}, u32[]{:S(2)}, u32[]{:S(2)}) async-start(bf16[4,2,128,256]{3,2,1,0:T(8,128)(2,1)} %pad_maximum_fusion.1), calls=%async_computation.2 | async-start | bytes 1048576 | tf_op jit(solution)/shard_map/all_to_all | solution.py:64
  98.6 2.2 %collective-permute-start.1 = (bf16[4,128,256]{2,1,0:T(8,128)(2,1)S(1)}, bf16[4,128,256]{2,1,0:T(8,128)(2,1)S(1)}, u32[]{:S(2)}, u32[]{:S(2)}) collective-permute-start(bf16[4,128,256]{2,1,0:T(8,128)(2,1)S(1)} %bitcast.29), channel_id=1, source_target_pairs={{0,128},{128,256},{256,384},{384,0},{2,130},{130,258},{258,386},{3... | collective-permute-start | bytes 786440 | tf_op jit(solution)/shard_map/ppermute | solution.py:256
  100.8 3.7 %collective-permute-start.2 = (bf16[4,128,256]{2,1,0:T(8,128)(2,1)S(1)}, bf16[4,128,256]{2,1,0:T(8,128)(2,1)S(1)}, u32[]{:S(2)}, u32[]{:S(2)}) collective-permute-start(bf16[4,128,256]{2,1,0:T(8,128)(2,1)S(1)} %bitcast.30), channel_id=1, source_target_pairs={{0,256},{128,384},{256,0},{384,128},{2,258},{130,386},{258,2},{386... | collective-permute-start | bytes 786440 | tf_op jit(solution)/shard_map/ppermute | solution.py:256
  104.5 2.5 %collective-permute-start.3 = (bf16[4,128,256]{2,1,0:T(8,128)(2,1)S(1)}, bf16[4,128,256]{2,1,0:T(8,128)(2,1)S(1)}, u32[]{:S(2)}, u32[]{:S(2)}) collective-permute-start(bf16[4,128,256]{2,1,0:T(8,128)(2,1)S(1)} %bitcast.31), channel_id=1, source_target_pairs={{0,384},{128,0},{256,128},{384,256},{2,386},{130,2},{258,130},{386... | collective-permute-start | bytes 786440 | tf_op jit(solution)/shard_map/ppermute | solution.py:256
  107.0 3.2 %collective-permute-start.4 = (bf16[4,4,2,128,256]{4,3,2,1,0:T(8,128)(2,1)S(1)}, bf16[4,4,2,128,256]{4,3,2,1,0:T(8,128)(2,1)}, u32[]{:S(2)}, u32[]{:S(2)}) collective-permute-start(bf16[4,4,2,128,256]{4,3,2,1,0:T(8,128)(2,1)S(1)} %all-to-all-done.mine), channel_id=1, source_target_pairs={{0,1},{1,0},{2,3},{3,2},{4,5},{5,4},{6,7},{7,6},{8,9},{9,8},{10,11... | collective-permute-start | bytes 6291464 | tf_op jit(solution)/shard_map/ppermute | solution.py:72
  110.3 2.4 %collective-permute-done.3 = bf16[4,128,256]{2,1,0:T(8,128)(2,1)S(1)} collective-permute-done((bf16[4,128,256]{2,1,0:T(8,128)(2,1)S(1)}, bf16[4,128,256]{2,1,0:T(8,128)(2,1)S(1)}, u32[]{:S(2)}, u32[]{:S(2)}) %collective-permute-start.3) | collective-permute-done | bytes 262176 | tf_op jit(solution)/shard_map/ppermute | solution.py:256
  112.8 3.7 %all-to-all-done.2.parts = bf16[4,2,128,256]{3,2,1,0:T(8,128)(2,1)} async-done(((bf16[4,2,128,256]{3,2,1,0:T(8,128)(2,1)}), bf16[4,2,128,256]{3,2,1,0:T(8,128)(2,1)}, u32[]{:S(2)}, u32[]{:S(2)}) %all-to-all-start.2) | async-done | bytes 524320 | tf_op jit(solution)/shard_map/all_to_all | solution.py:64
  117.6 18.7 %all-gather.4 = bf16[8,128,256]{2,1,0:T(8,128)(2,1)S(1)} all-gather(bf16[2,128,256]{2,1,0:T(8,128)(2,1)S(1)} %shard_map.86), channel_id=6, replica_groups={{0,2,4,6},{8,10,12,14},{16,18,20,22},{24,26,28,30},{32,34,36,38},{40,42..., dimensions={0}, use_global_device_ids=true | all-gather | bytes 655360 | tf_op jit(solution)/shard_map/all_gather | solution.py:60
  137.9 4.6 %all-to-all-start.3 = ((bf16[4,4,2,128,256]{4,3,1,2,0:T(8,128)(2,1)}), bf16[4,4,2,128,256]{4,3,1,2,0:T(8,128)(2,1)}, u32[]{:S(2)}, u32[]{:S(2)}) async-start(bf16[4,4,2,128,256]{4,3,1,2,0:T(8,128)(2,1)} %broadcast_in_dim.5), calls=%async_computation.3 | async-start | bytes 4194304 | tf_op jit(solution)/shard_map/all_to_all | solution.py:64
  142.5 1.9 %collective-permute-start.5 = (bf16[4,4,128,256]{3,2,1,0:T(8,128)(2,1)S(1)}, bf16[4,4,128,256]{3,2,1,0:T(8,128)(2,1)}, u32[]{:S(2)}, u32[]{:S(2)}) collective-permute-start(bf16[4,4,128,256]{3,2,1,0:T(8,128)(2,1)S(1)} %pad_maximum_fusion.late), channel_id=1, source_target_pairs={{0,1},{1,0},{2,3},{3,2},{4,5},{5,4},{6,7},{7,6},{8,9},{9,8},{10,11... | collective-permute-start | bytes 3145736 | tf_op jit(solution)/shard_map/ppermute | solution.py:72
  144.5 2.7 %collective-permute-done.5.their_late = bf16[4,4,128,256]{3,2,1,0:T(8,128)(2,1)} collective-permute-done((bf16[4,4,128,256]{3,2,1,0:T(8,128)(2,1)S(1)}, bf16[4,4,128,256]{3,2,1,0:T(8,128)(2,1)}, u32[]{:S(2)}, u32[]{:S(2)}) %collective-permute-start.5) | collective-permute-done | bytes 1048608 | tf_op jit(solution)/shard_map/ppermute | solution.py:72
  148.2 3.8 %shard_map.87 = (f32[256,128]{1,0:T(8,128)}, f32[512,256]{1,0:T(8,128)}) custom-call(s32[3]{0:T(128)S(1)} %pad_add_fusion.role, bf16[4,4,2,128,256]{4,3,2,1,0:T(8,128)(2,1)S(1)} %all-to-all-done.mine, bf16[4,4,2,128,256]{4,3,2,1,0:T(8,128)(2,1)} %collective-permute-done.4.their, bf16[4,4,128,256]{3,2,1,0:T(8,128)(2,1)S(1)} %pad_maximum_fusion.late, ...), custom_call_target="tpu_custom_call" | custom-call | flops 671088640 | bytes 7602176 | tf_op jit(solution)/shard_map/pallas_call | solution.py:92
  152.0 6.2 %all-to-all-done.3 = bf16[4,4,2,128,256]{4,3,1,2,0:T(8,128)(2,1)} async-done(((bf16[4,4,2,128,256]{4,3,1,2,0:T(8,128)(2,1)}), bf16[4,4,2,128,256]{4,3,1,2,0:T(8,128)(2,1)}, u32[]{:S(2)}, u32[]{:S(2)}) %all-to-all-start.3) | async-done | bytes 2097184 | tf_op jit(solution)/shard_map/all_to_all | solution.py:64
  159.5 2.4 %collective-permute-start.6 = (bf16[4,4,128,256]{3,2,1,0:T(8,128)(2,1)S(1)}, bf16[4,4,128,256]{3,2,1,0:T(8,128)(2,1)S(1)}, u32[]{:S(2)}, u32[]{:S(2)}) collective-permute-start(bf16[4,4,128,256]{3,2,1,0:T(8,128)(2,1)S(1)} %slice_bitcast_fusion), channel_id=1, source_target_pairs={{0,1},{1,0},{2,3},{3,2},{4,5},{5,4},{6,7},{7,6},{8,9},{9,8},{10,11... | collective-permute-start | bytes 3145736 | tf_op jit(solution)/shard_map/ppermute | solution.py:72
  161.9 1.7 %copy.13.mixed = bf16[4,4,2,128,256]{4,3,2,1,0:T(8,128)(2,1)S(1)} copy(bf16[4,4,2,128,256]{4,3,1,2,0:T(8,128)(2,1)} %all-to-all-done.3) | data formatting | bytes 4194304 | tf_op jit(solution)/shard_map/optimization_barrier | solution.py:280
  (30 shorter events, 11.6 us)
Async XLA Ops:
  12.1 3.1 %collective-permute-start = (bf16[3,128,256]{2,1,0:T(8,128)(2,1)S(1)}, bf16[3,128,256]{2,1,0:T(8,128)(2,1)S(1)}, u32[]{:S(2)}, u32[]{:S(2)}) collective-permute-start(bf16[3,128,256]{2,1,0:T(8,128)(2,1)S(1)} %pad_maximum_fusion.2), channel_id=1, source_target_pairs={{0,0},{1,1},{2,2},{3,33},{4,4},{5,65},{6,6},{7,97},{8,8},{9,129},{... | collective-permute-start | bytes 589832 | tf_op jit(solution)/shard_map/ppermute | solution.py:231
  43.1 21.6 %all-to-all-start = ((bf16[4,4,2,128,256]{4,3,2,1,0:T(8,128)(2,1)}), bf16[4,4,2,128,256]{4,3,2,1,0:T(8,128)(2,1)S(1)}, u32[]{:S(2)}, u32[]{:S(2)}) async-start(bf16[4,4,2,128,256]{4,3,2,1,0:T(8,128)(2,1)} %broadcast_in_dim.4), calls=%async_computation | async-start | bytes 4194304 | tf_op jit(solution)/shard_map/all_to_all | solution.py:64
  86.9 29.5 %all-to-all-start.2 = ((bf16[4,2,128,256]{3,2,1,0:T(8,128)(2,1)}), bf16[4,2,128,256]{3,2,1,0:T(8,128)(2,1)}, u32[]{:S(2)}, u32[]{:S(2)}) async-start(bf16[4,2,128,256]{3,2,1,0:T(8,128)(2,1)} %pad_maximum_fusion.1), calls=%async_computation.2 | async-start | bytes 1048576 | tf_op jit(solution)/shard_map/all_to_all | solution.py:64
  98.6 11.6 %collective-permute-start.1 = (bf16[4,128,256]{2,1,0:T(8,128)(2,1)S(1)}, bf16[4,128,256]{2,1,0:T(8,128)(2,1)S(1)}, u32[]{:S(2)}, u32[]{:S(2)}) collective-permute-start(bf16[4,128,256]{2,1,0:T(8,128)(2,1)S(1)} %bitcast.29), channel_id=1, source_target_pairs={{0,128},{128,256},{256,384},{384,0},{2,130},{130,258},{258,386},{3... | collective-permute-start | bytes 786440 | tf_op jit(solution)/shard_map/ppermute | solution.py:256
  100.8 9.5 %collective-permute-start.2 = (bf16[4,128,256]{2,1,0:T(8,128)(2,1)S(1)}, bf16[4,128,256]{2,1,0:T(8,128)(2,1)S(1)}, u32[]{:S(2)}, u32[]{:S(2)}) collective-permute-start(bf16[4,128,256]{2,1,0:T(8,128)(2,1)S(1)} %bitcast.30), channel_id=1, source_target_pairs={{0,256},{128,384},{256,0},{384,128},{2,258},{130,386},{258,2},{386... | collective-permute-start | bytes 786440 | tf_op jit(solution)/shard_map/ppermute | solution.py:256
  104.5 8.1 %collective-permute-start.3 = (bf16[4,128,256]{2,1,0:T(8,128)(2,1)S(1)}, bf16[4,128,256]{2,1,0:T(8,128)(2,1)S(1)}, u32[]{:S(2)}, u32[]{:S(2)}) collective-permute-start(bf16[4,128,256]{2,1,0:T(8,128)(2,1)S(1)} %bitcast.31), channel_id=1, source_target_pairs={{0,384},{128,0},{256,128},{384,256},{2,386},{130,2},{258,130},{386... | collective-permute-start | bytes 786440 | tf_op jit(solution)/shard_map/ppermute | solution.py:256
  107.0 40.1 %collective-permute-start.4 = (bf16[4,4,2,128,256]{4,3,2,1,0:T(8,128)(2,1)S(1)}, bf16[4,4,2,128,256]{4,3,2,1,0:T(8,128)(2,1)}, u32[]{:S(2)}, u32[]{:S(2)}) collective-permute-start(bf16[4,4,2,128,256]{4,3,2,1,0:T(8,128)(2,1)S(1)} %all-to-all-done.mine), channel_id=1, source_target_pairs={{0,1},{1,0},{2,3},{3,2},{4,5},{5,4},{6,7},{7,6},{8,9},{9,8},{10,11... | collective-permute-start | bytes 6291464 | tf_op jit(solution)/shard_map/ppermute | solution.py:72
  137.9 9.3 %copy-start.1 = (f32[256,128]{1,0:T(8,128)S(1)}, f32[256,128]{1,0:T(8,128)}, u32[]{:S(2)}) copy-start(f32[256,128]{1,0:T(8,128)} %in_old.1) | copy-start | bytes 393220
  137.9 20.3 %all-to-all-start.3 = ((bf16[4,4,2,128,256]{4,3,1,2,0:T(8,128)(2,1)}), bf16[4,4,2,128,256]{4,3,1,2,0:T(8,128)(2,1)}, u32[]{:S(2)}, u32[]{:S(2)}) async-start(bf16[4,4,2,128,256]{4,3,1,2,0:T(8,128)(2,1)} %broadcast_in_dim.5), calls=%async_computation.3 | async-start | bytes 4194304 | tf_op jit(solution)/shard_map/all_to_all | solution.py:64
  142.5 4.7 %collective-permute-start.5 = (bf16[4,4,128,256]{3,2,1,0:T(8,128)(2,1)S(1)}, bf16[4,4,128,256]{3,2,1,0:T(8,128)(2,1)}, u32[]{:S(2)}, u32[]{:S(2)}) collective-permute-start(bf16[4,4,128,256]{3,2,1,0:T(8,128)(2,1)S(1)} %pad_maximum_fusion.late), channel_id=1, source_target_pairs={{0,1},{1,0},{2,3},{3,2},{4,5},{5,4},{6,7},{7,6},{8,9},{9,8},{10,11... | collective-permute-start | bytes 3145736 | tf_op jit(solution)/shard_map/ppermute | solution.py:72
  147.2 1.0 copy-start
  159.5 4.7 %collective-permute-start.6 = (bf16[4,4,128,256]{3,2,1,0:T(8,128)(2,1)S(1)}, bf16[4,4,128,256]{3,2,1,0:T(8,128)(2,1)S(1)}, u32[]{:S(2)}, u32[]{:S(2)}) collective-permute-start(bf16[4,4,128,256]{3,2,1,0:T(8,128)(2,1)S(1)} %slice_bitcast_fusion), channel_id=1, source_target_pairs={{0,1},{1,0},{2,3},{3,2},{4,5},{5,4},{6,7},{7,6},{8,9},{9,8},{10,11... | collective-permute-start | bytes 3145736 | tf_op jit(solution)/shard_map/ppermute | solution.py:72

commit v10 on v9

--- a/solution.py
+++ b/solution.py
@@ -147,18 +147,11 @@
     return jnp.stack([part.reshape(SIDE, -1, part.shape[1]) for part in parts], axis=1)
 
 
-def finish_body(role, parts, out):
-    totals = [sum(parts[k, half].astype(f32) for k in range(SIDE)) for half in range(CORES)]
-
-    @pl.when(role[0] == 0)
-    def _():
-        out[0] = (totals[0] + totals[1]).astype(bf16)
-        out[1] = jnp.zeros_like(out[1])
-
-    @pl.when(role[0] == 1)
-    def _():
-        out[0] = totals[0].astype(bf16)
-        out[1] = totals[1].astype(bf16)
+def finish(first, parts):
+    total = jnp.sum(parts.astype(f32), axis=0)
+    near = jnp.where(first, total[0] + total[1], total[0])
+    far = jnp.where(first, jnp.zeros_like(total[1]), total[1])
+    return jnp.stack([near, far]).astype(bf16)
 
 
 def natural_body(tokens, role, mixed, crossed, out):
@@ -257,9 +250,7 @@
     late = jnp.stack([late] + turns)
     their_late = core_swap(late)
     part, late = tied((part, late))
-    mixed = local_call(
-        finish_body, jax.ShapeDtypeStruct((CORES, rows, wide), bf16), role, part
-    )
+    mixed = finish(first, part)
     mixed = gather(mixed, back_z)
     mixed = gather_direct(mixed, back_xy)
     input_running, output_running = local_call(

time: 168 us -> 170 us (1.012)
  the two profiles are of different devices: /device:TPU:1 before, /device:TPU:65 now
where the time goes in v10:
time: 170 us; the launch traced here: 169 us
  blocking collectives  70.9 us (42%)
  starting transfers between devices  52.2 us (31%)
  waiting for transfers between devices  27.2 us (16%)
  local copies, waits for them, and re-layouts  7.34 us (4%)
  Pallas kernels  6.71 us (4%)
  other arithmetic  3.58 us (2%)
    all_gather x3, blocking collectives, gather(): lax.all_gather(block, ALL, axis_index_groups=groups, axis=0, tiled=False)  45.3 us
    all_to_all x3, starting transfers between devices, exchange(): return lax.all_to_all(parts, ALL, 0, 0, axis_index_groups=groups)  22.1 us
    all_to_all x3, waiting for transfers between devices, exchange(): return lax.all_to_all(parts, ALL, 0, 0, axis_index_groups=groups)  20.4 us
    all_to_all x1, blocking collectives, exchange(): return lax.all_to_all(parts, ALL, 0, 0, axis_index_groups=groups)  18.8 us
    ppermute x1, starting transfers between devices, per_device(): moved = lax.ppermute(moved, ALL, swap_pairs())  12.7 us
    ppermute x3, starting transfers between devices, core_swap(): return lax.ppermute(block, 'core', [(0, 1), (1, 0)])  8.99 us
    ppermute x3, starting transfers between devices, per_device(): lax.ppermute(late, ALL, ring_pairs(turn))  8.4 us
    pallas_call x3, Pallas kernels, local_call(): pl.pallas_call(body, grid=grid, out_shape=out_shape, in_specs=[pl.BlockSp...  6.71 us
  transfers between devices with their start and end apart: 10, of which 7 were waited for; matrix products, arithmetic and copies ran while one was open for 3% of the time, Pallas kernels for 2%

profile of v10, /device:TPU:65, one launch (start us, length us, event | category | flops | bytes accessed | tf_op | source)
XLA Modules:
  0.0 168.7 jit_solution(15167310515125390567)
XLA Ops:
  1.5 2.3 %all_gather.33 = bf16[384,256]{1,0:T(8,128)(2,1)S(1)} all-gather(bf16[384,128]{1,0:T(8,128)(2,1)S(1)} %pad_maximum_fusion.4), channel_id=1, replica_groups=mesh['x'=4,'zh'=4,'y'=4,'zl'=4,'core'=2] {'core'}, dimensions={1}, use_global_device_ids=true | all-gather | bytes 294912 | tf_op jit(solution)/shard_map/all_gather | solution.py:219
  3.7 2.1 %all-gather = bf16[256,256]{1,0:T(8,128)(2,1)S(1)} all-gather(bf16[128,256]{1,0:T(8,128)(2,1)} %param.7), channel_id=2, replica_groups=mesh['x'=4,'zh'=4,'y'=4,'zl'=4,'core'=2] {'core'}, dimensions={0}, use_global_device_ids=true | all-gather | bytes 196608 | tf_op jit(solution)/shard_map/all_gather | solution.py:217
  5.9 12.7 %collective-permute-start = (bf16[3,128,256]{2,1,0:T(8,128)(2,1)S(1)}, bf16[3,128,256]{2,1,0:T(8,128)(2,1)S(1)}, u32[]{:S(2)}, u32[]{:S(2)}) collective-permute-start(bf16[3,128,256]{2,1,0:T(8,128)(2,1)S(1)} %pad_maximum_fusion.2), channel_id=1, source_target_pairs={{0,0},{1,1},{2,2},{3,33},{4,4},{5,65},{6,6},{7,97},{8,8},{9,129},{... | collective-permute-start | bytes 589832 | tf_op jit(solution)/shard_map/ppermute | solution.py:224
  18.6 2.4 %all-gather.1 = bf16[1024,256]{1,0:T(8,128)(2,1)S(1)} all-gather(bf16[512,256]{1,0:T(8,128)(2,1)} %param.11), channel_id=3, replica_groups=mesh['x'=4,'zh'=4,'y'=4,'zl'=4,'core'=2] {'core'}, dimensions={0}, use_global_device_ids=true | all-gather | bytes 786432 | tf_op jit(solution)/shard_map/all_gather | solution.py:225
  21.0 2.8 %collective-permute-done = bf16[3,128,256]{2,1,0:T(8,128)(2,1)S(1)} collective-permute-done((bf16[3,128,256]{2,1,0:T(8,128)(2,1)S(1)}, bf16[3,128,256]{2,1,0:T(8,128)(2,1)S(1)}, u32[]{:S(2)}, u32[]{:S(2)}) %collective-permute-start) | collective-permute-done | bytes 196640 | tf_op jit(solution)/shard_map/ppermute | solution.py:224
  23.8 15.0 %all-gather.2 = bf16[8,128,256]{2,1,0:T(8,128)(2,1)S(1)} all-gather(bf16[2,128,256]{2,1,0:T(8,128)(2,1)S(1)} %maximum_select_fusion), channel_id=4, replica_groups={{0,32,64,96},{2,34,66,98},{4,36,68,100},{6,38,70,102},{8,40,72,104},{10..., dimensions={0}, use_global_device_ids=true | all-gather | bytes 655360 | tf_op jit(solution)/shard_map/all_gather | solution.py:60
  40.4 5.8 %all-to-all-start = ((bf16[4,4,2,128,256]{4,3,2,1,0:T(8,128)(2,1)}), bf16[4,4,2,128,256]{4,3,2,1,0:T(8,128)(2,1)S(1)}, u32[]{:S(2)}, u32[]{:S(2)}) async-start(bf16[4,4,2,128,256]{4,3,2,1,0:T(8,128)(2,1)} %broadcast_in_dim.6), calls=%async_computation | async-start | bytes 4194304 | tf_op jit(solution)/shard_map/all_to_all | solution.py:64
  46.2 10.7 %all-gather.3 = bf16[512,256]{1,0:T(8,128)(2,1)S(1)} all-gather(bf16[128,256]{1,0:T(8,128)(2,1)S(1)} %broadcast_select_fusion), channel_id=5, replica_groups={{0,32,64,96},{2,34,66,98},{4,36,68,100},{6,38,70,102},{8,40,72,104},{10..., dimensions={0}, use_global_device_ids=true | all-gather | bytes 327680 | tf_op jit(solution)/shard_map/all_gather | solution.py:60
  56.9 4.9 %all-to-all-done.mine = bf16[4,4,2,128,256]{4,3,2,1,0:T(8,128)(2,1)S(1)} async-done(((bf16[4,4,2,128,256]{4,3,2,1,0:T(8,128)(2,1)}), bf16[4,4,2,128,256]{4,3,2,1,0:T(8,128)(2,1)S(1)}, u32[]{:S(2)}, u32[]{:S(2)}) %all-to-all-start) | async-done | bytes 2097184 | tf_op jit(solution)/shard_map/all_to_all | solution.py:64
  61.8 1.8 %shard_map.85 = bf16[4,2,512,256]{3,2,1,0:T(8,128)(2,1)S(1)} custom-call(s32[1]{0:T(128)} %bitcast.role, bf16[4,4,2,128,256]{4,3,2,1,0:T(8,128)(2,1)S(1)} %all-to-all-done.mine, bf16[256,256]{1,0:T(8,128)(2,1)S(1)} %slice.42.in_inverse, bf16[2,512,256]{2,1,0:T(8,128)(2,1)S(1)} %bitcast.25), custom_call_target="tpu_custom_call" | custom-call | flops 1073741824 | bytes 4849664 | tf_op jit(solution)/shard_map/pallas_call | solution.py:92
  63.6 18.8 %all_to_all.20 = bf16[4,2,512,256]{3,2,1,0:T(8,128)(2,1)S(1)} all-to-all(bf16[4,2,512,256]{3,2,1,0:T(8,128)(2,1)S(1)} %shard_map.85), channel_id=1, replica_groups={{0,8,16,24},{2,10,18,26},{4,12,20,28},{6,14,22,30},{32,40,48,56},{34,42..., dimensions={0} | all-to-all | bytes 4194304 | tf_op jit(solution)/shard_map/all_to_all | solution.py:64
  83.8 11.7 %all-to-all-start.2 = ((bf16[4,2,128,256]{3,2,1,0:T(8,128)(2,1)}), bf16[4,2,128,256]{3,2,1,0:T(8,128)(2,1)}, u32[]{:S(2)}, u32[]{:S(2)}) async-start(bf16[4,2,128,256]{3,2,1,0:T(8,128)(2,1)} %pad_maximum_fusion.1), calls=%async_computation.2 | async-start | bytes 1048576 | tf_op jit(solution)/shard_map/all_to_all | solution.py:64
  95.5 1.9 %collective-permute-start.1 = (bf16[4,128,256]{2,1,0:T(8,128)(2,1)S(1)}, bf16[4,128,256]{2,1,0:T(8,128)(2,1)S(1)}, u32[]{:S(2)}, u32[]{:S(2)}) collective-permute-start(bf16[4,128,256]{2,1,0:T(8,128)(2,1)S(1)} %bitcast.31), channel_id=1, source_target_pairs={{0,128},{128,256},{256,384},{384,0},{2,130},{130,258},{258,386},{3... | collective-permute-start | bytes 786440 | tf_op jit(solution)/shard_map/ppermute | solution.py:249
  97.4 3.9 %collective-permute-start.2 = (bf16[4,128,256]{2,1,0:T(8,128)(2,1)S(1)}, bf16[4,128,256]{2,1,0:T(8,128)(2,1)S(1)}, u32[]{:S(2)}, u32[]{:S(2)}) collective-permute-start(bf16[4,128,256]{2,1,0:T(8,128)(2,1)S(1)} %bitcast.32), channel_id=1, source_target_pairs={{0,256},{128,384},{256,0},{384,128},{2,258},{130,386},{258,2},{386... | collective-permute-start | bytes 786440 | tf_op jit(solution)/shard_map/ppermute | solution.py:249
  101.4 2.5 %collective-permute-start.3 = (bf16[4,128,256]{2,1,0:T(8,128)(2,1)S(1)}, bf16[4,128,256]{2,1,0:T(8,128)(2,1)S(1)}, u32[]{:S(2)}, u32[]{:S(2)}) collective-permute-start(bf16[4,128,256]{2,1,0:T(8,128)(2,1)S(1)} %bitcast.33), channel_id=1, source_target_pairs={{0,384},{128,0},{256,128},{384,256},{2,386},{130,2},{258,130},{386... | collective-permute-start | bytes 786440 | tf_op jit(solution)/shard_map/ppermute | solution.py:249
  103.9 5.1 %collective-permute-start.4 = (bf16[4,4,2,128,256]{4,3,2,1,0:T(8,128)(2,1)S(1)}, bf16[4,4,2,128,256]{4,3,2,1,0:T(8,128)(2,1)}, u32[]{:S(2)}, u32[]{:S(2)}) collective-permute-start(bf16[4,4,2,128,256]{4,3,2,1,0:T(8,128)(2,1)S(1)} %all-to-all-done.mine), channel_id=1, source_target_pairs={{0,1},{1,0},{2,3},{3,2},{4,5},{5,4},{6,7},{7,6},{8,9},{9,8},{10,11... | collective-permute-start | bytes 6291464 | tf_op jit(solution)/shard_map/ppermute | solution.py:72
  109.6 9.6 %all-to-all-done.2 = bf16[4,2,128,256]{3,2,1,0:T(8,128)(2,1)} async-done(((bf16[4,2,128,256]{3,2,1,0:T(8,128)(2,1)}), bf16[4,2,128,256]{3,2,1,0:T(8,128)(2,1)}, u32[]{:S(2)}, u32[]{:S(2)}) %all-to-all-start.2) | async-done | bytes 524320 | tf_op jit(solution)/shard_map/all_to_all | solution.py:64
  120.4 19.6 %all_gather.40 = bf16[4,2,128,256]{3,2,1,0:T(8,128)(2,1)S(1)} all-gather(bf16[1,2,128,256]{3,2,1,0:T(8,128)(2,1)S(1)} %pad_maximum_fusion.3), channel_id=1, replica_groups={{0,2,4,6},{8,10,12,14},{16,18,20,22},{24,26,28,30},{32,34,36,38},{40,42..., dimensions={0}, use_global_device_ids=true | all-gather | bytes 655360 | tf_op jit(solution)/shard_map/all_gather | solution.py:60
  141.7 4.6 %all-to-all-start.3 = ((bf16[4,4,2,128,256]{4,3,1,2,0:T(8,128)(2,1)}), bf16[4,4,2,128,256]{4,3,1,2,0:T(8,128)(2,1)}, u32[]{:S(2)}, u32[]{:S(2)}) async-start(bf16[4,4,2,128,256]{4,3,1,2,0:T(8,128)(2,1)} %broadcast_in_dim.8), calls=%async_computation.3 | async-start | bytes 4194304 | tf_op jit(solution)/shard_map/all_to_all | solution.py:64
  146.2 1.9 %collective-permute-start.5 = (bf16[4,4,128,256]{3,2,1,0:T(8,128)(2,1)S(1)}, bf16[4,4,128,256]{3,2,1,0:T(8,128)(2,1)}, u32[]{:S(2)}, u32[]{:S(2)}) collective-permute-start(bf16[4,4,128,256]{3,2,1,0:T(8,128)(2,1)S(1)} %pad_maximum_fusion.late), channel_id=1, source_target_pairs={{0,1},{1,0},{2,3},{3,2},{4,5},{5,4},{6,7},{7,6},{8,9},{9,8},{10,11... | collective-permute-start | bytes 3145736 | tf_op jit(solution)/shard_map/ppermute | solution.py:72
  148.3 2.7 %collective-permute-done.5.their_late = bf16[4,4,128,256]{3,2,1,0:T(8,128)(2,1)} collective-permute-done((bf16[4,4,128,256]{3,2,1,0:T(8,128)(2,1)S(1)}, bf16[4,4,128,256]{3,2,1,0:T(8,128)(2,1)}, u32[]{:S(2)}, u32[]{:S(2)}) %collective-permute-start.5) | collective-permute-done | bytes 1048608 | tf_op jit(solution)/shard_map/ppermute | solution.py:72
  152.0 3.8 %shard_map.86 = (f32[256,128]{1,0:T(8,128)}, f32[512,256]{1,0:T(8,128)}) custom-call(s32[3]{0:T(128)S(1)} %pad_add_fusion.role, bf16[4,4,2,128,256]{4,3,2,1,0:T(8,128)(2,1)S(1)} %all-to-all-done.mine, bf16[4,4,2,128,256]{4,3,2,1,0:T(8,128)(2,1)} %collective-permute-done.4.their, bf16[4,4,128,256]{3,2,1,0:T(8,128)(2,1)S(1)} %pad_maximum_fusion.late, ...), custom_call_target="tpu_custom_call" | custom-call | flops 671088640 | bytes 7602176 | tf_op jit(solution)/shard_map/pallas_call | solution.py:92
  155.8 5.9 %all-to-all-done.3 = bf16[4,4,2,128,256]{4,3,1,2,0:T(8,128)(2,1)} async-done(((bf16[4,4,2,128,256]{4,3,1,2,0:T(8,128)(2,1)}), bf16[4,4,2,128,256]{4,3,1,2,0:T(8,128)(2,1)}, u32[]{:S(2)}, u32[]{:S(2)}) %all-to-all-start.3) | async-done | bytes 2097184 | tf_op jit(solution)/shard_map/all_to_all | solution.py:64
  163.0 1.9 %collective-permute-start.6 = (bf16[4,4,128,256]{3,2,1,0:T(8,128)(2,1)S(1)}, bf16[4,4,128,256]{3,2,1,0:T(8,128)(2,1)S(1)}, u32[]{:S(2)}, u32[]{:S(2)}) collective-permute-start(bf16[4,4,128,256]{3,2,1,0:T(8,128)(2,1)S(1)} %slice_bitcast_fusion), channel_id=1, source_target_pairs={{0,1},{1,0},{2,3},{3,2},{4,5},{5,4},{6,7},{7,6},{8,9},{9,8},{10,11... | collective-permute-start | bytes 3145736 | tf_op jit(solution)/shard_map/ppermute | solution.py:72
  (33 shorter events, 13.4 us)
Async XLA Ops:
  5.9 17.9 %collective-permute-start = (bf16[3,128,256]{2,1,0:T(8,128)(2,1)S(1)}, bf16[3,128,256]{2,1,0:T(8,128)(2,1)S(1)}, u32[]{:S(2)}, u32[]{:S(2)}) collective-permute-start(bf16[3,128,256]{2,1,0:T(8,128)(2,1)S(1)} %pad_maximum_fusion.2), channel_id=1, source_target_pairs={{0,0},{1,1},{2,2},{3,33},{4,4},{5,65},{6,6},{7,97},{8,8},{9,129},{... | collective-permute-start | bytes 589832 | tf_op jit(solution)/shard_map/ppermute | solution.py:224
  40.4 21.4 %all-to-all-start = ((bf16[4,4,2,128,256]{4,3,2,1,0:T(8,128)(2,1)}), bf16[4,4,2,128,256]{4,3,2,1,0:T(8,128)(2,1)S(1)}, u32[]{:S(2)}, u32[]{:S(2)}) async-start(bf16[4,4,2,128,256]{4,3,2,1,0:T(8,128)(2,1)} %broadcast_in_dim.6), calls=%async_computation | async-start | bytes 4194304 | tf_op jit(solution)/shard_map/all_to_all | solution.py:64
  83.8 35.4 %all-to-all-start.2 = ((bf16[4,2,128,256]{3,2,1,0:T(8,128)(2,1)}), bf16[4,2,128,256]{3,2,1,0:T(8,128)(2,1)}, u32[]{:S(2)}, u32[]{:S(2)}) async-start(bf16[4,2,128,256]{3,2,1,0:T(8,128)(2,1)} %pad_maximum_fusion.1), calls=%async_computation.2 | async-start | bytes 1048576 | tf_op jit(solution)/shard_map/all_to_all | solution.py:64
  95.5 13.6 %collective-permute-start.1 = (bf16[4,128,256]{2,1,0:T(8,128)(2,1)S(1)}, bf16[4,128,256]{2,1,0:T(8,128)(2,1)S(1)}, u32[]{:S(2)}, u32[]{:S(2)}) collective-permute-start(bf16[4,128,256]{2,1,0:T(8,128)(2,1)S(1)} %bitcast.31), channel_id=1, source_target_pairs={{0,128},{128,256},{256,384},{384,0},{2,130},{130,258},{258,386},{3... | collective-permute-start | bytes 786440 | tf_op jit(solution)/shard_map/ppermute | solution.py:249
  97.4 11.7 %collective-permute-start.2 = (bf16[4,128,256]{2,1,0:T(8,128)(2,1)S(1)}, bf16[4,128,256]{2,1,0:T(8,128)(2,1)S(1)}, u32[]{:S(2)}, u32[]{:S(2)}) collective-permute-start(bf16[4,128,256]{2,1,0:T(8,128)(2,1)S(1)} %bitcast.32), channel_id=1, source_target_pairs={{0,256},{128,384},{256,0},{384,128},{2,258},{130,386},{258,2},{386... | collective-permute-start | bytes 786440 | tf_op jit(solution)/shard_map/ppermute | solution.py:249
  101.4 8.1 %collective-permute-start.3 = (bf16[4,128,256]{2,1,0:T(8,128)(2,1)S(1)}, bf16[4,128,256]{2,1,0:T(8,128)(2,1)S(1)}, u32[]{:S(2)}, u32[]{:S(2)}) collective-permute-start(bf16[4,128,256]{2,1,0:T(8,128)(2,1)S(1)} %bitcast.33), channel_id=1, source_target_pairs={{0,384},{128,0},{256,128},{384,256},{2,386},{130,2},{258,130},{386... | collective-permute-start | bytes 786440 | tf_op jit(solution)/shard_map/ppermute | solution.py:249
  103.9 47.0 %collective-permute-start.4 = (bf16[4,4,2,128,256]{4,3,2,1,0:T(8,128)(2,1)S(1)}, bf16[4,4,2,128,256]{4,3,2,1,0:T(8,128)(2,1)}, u32[]{:S(2)}, u32[]{:S(2)}) collective-permute-start(bf16[4,4,2,128,256]{4,3,2,1,0:T(8,128)(2,1)S(1)} %all-to-all-done.mine), channel_id=1, source_target_pairs={{0,1},{1,0},{2,3},{3,2},{4,5},{5,4},{6,7},{7,6},{8,9},{9,8},{10,11... | collective-permute-start | bytes 6291464 | tf_op jit(solution)/shard_map/ppermute | solution.py:72
  141.7 9.3 %copy-start.1 = (f32[256,128]{1,0:T(8,128)S(1)}, f32[256,128]{1,0:T(8,128)}, u32[]{:S(2)}) copy-start(f32[256,128]{1,0:T(8,128)} %in_old.1) | copy-start | bytes 393220
  141.7 20.0 %all-to-all-start.3 = ((bf16[4,4,2,128,256]{4,3,1,2,0:T(8,128)(2,1)}), bf16[4,4,2,128,256]{4,3,1,2,0:T(8,128)(2,1)}, u32[]{:S(2)}, u32[]{:S(2)}) async-start(bf16[4,4,2,128,256]{4,3,1,2,0:T(8,128)(2,1)} %broadcast_in_dim.8), calls=%async_computation.3 | async-start | bytes 4194304 | tf_op jit(solution)/shard_map/all_to_all | solution.py:64
  146.2 4.7 %collective-permute-start.5 = (bf16[4,4,128,256]{3,2,1,0:T(8,128)(2,1)S(1)}, bf16[4,4,128,256]{3,2,1,0:T(8,128)(2,1)}, u32[]{:S(2)}, u32[]{:S(2)}) collective-permute-start(bf16[4,4,128,256]{3,2,1,0:T(8,128)(2,1)S(1)} %pad_maximum_fusion.late), channel_id=1, source_target_pairs={{0,1},{1,0},{2,3},{3,2},{4,5},{5,4},{6,7},{7,6},{8,9},{9,8},{10,11... | collective-permute-start | bytes 3145736 | tf_op jit(solution)/shard_map/ppermute | solution.py:72
  150.9 1.0 copy-start
  163.0 4.6 %collective-permute-start.6 = (bf16[4,4,128,256]{3,2,1,0:T(8,128)(2,1)S(1)}, bf16[4,4,128,256]{3,2,1,0:T(8,128)(2,1)S(1)}, u32[]{:S(2)}, u32[]{:S(2)}) collective-permute-start(bf16[4,4,128,256]{3,2,1,0:T(8,128)(2,1)S(1)} %slice_bitcast_fusion), channel_id=1, source_target_pairs={{0,1},{1,0},{2,3},{3,2},{4,5},{5,4},{6,7},{7,6},{8,9},{9,8},{10,11... | collective-permute-start | bytes 3145736 | tf_op jit(solution)/shard_map/ppermute | solution.py:72
